TPU v7x, 512 devices: a whole 4x8x8 slice. The times are simulated.
512 devices in a mesh: row: 16 (over z_lo, x), col: 32 (over y, z_hi, core).
Axes of the slice: x: 4, y: 8, z: 8 (z_hi: 2, z_lo: 4; z = z_hi * 4 + z_lo), core: 2. Of those that a mesh axis runs over, the one named last changes fastest.
Arguments:
- inputs: bfloat16 [512, 6144], P('row'), may hold values from -6 to 6
- cotangent: bfloat16 [512, 24576], P('row', 'col'), may hold values from -1.1953125 to 1.1953125
- gate_weight: bfloat16 [6144, 24576], P('row', 'col'), may hold values from -0.078125 to 0.078125
- up_weight: bfloat16 [6144, 24576], P('row', 'col'), may hold values from -0.078125 to 0.078125
Outputs:
- input_grad: bfloat16 [512, 6144], P('col', 'row')
- gate_grad: bfloat16 [6144, 24576], P('row', 'col')
- up_grad: bfloat16 [6144, 24576], P('row', 'col')
All inputs are finite; a program needn't handle non-finite values.
Results may differ from a plain program's by a relative error of at most 0.005.
Values may be sent and summed in bfloat16 or wider, within the bound.
No kernel may reach another device: no remote copies, remote signals or barrier semaphores. Data moves between devices by JAX's collectives and lax.ppermute only.
A program may use at most 64 MiB of HBM per device.

v0:
```python
import jax
import jax.numpy as jnp
from jax import lax
from jax.sharding import PartitionSpec as P


def over_tokens(left, right):
    return lax.dot_general(
        left, right, (((0,), (0,)), ((), ())), preferred_element_type=jnp.float32
    )


def over_hidden(left, right):
    return lax.dot_general(
        left, right, (((1,), (1,)), ((), ())), preferred_element_type=jnp.float32
    )


def local_grads(gate_full, up_full, cotangent):
    sigmoid_gate = jax.nn.sigmoid(gate_full)
    cot_wide = cotangent.astype(jnp.float32)
    d_gate = (cot_wide * up_full * sigmoid_gate * (1.0 + gate_full * (1.0 - sigmoid_gate))).astype(
        jnp.bfloat16
    )
    d_up = (cot_wide * gate_full * sigmoid_gate).astype(jnp.bfloat16)
    return (d_gate, d_up)


def shards(inputs, cotangent, gate_weight, up_weight):
    panels = lax.all_to_all(inputs, "row", split_axis=1, concat_axis=0, tiled=True)
    hidden_cols = gate_weight.shape[1]
    joined = jnp.concatenate([gate_weight, up_weight], axis=1)
    token_rows = panels
    summed = lax.psum_scatter(
        jnp.dot(token_rows, joined, preferred_element_type=jnp.float32),
        "row",
        scatter_dimension=0,
        tiled=True,
    )
    d_gate, d_up = local_grads(summed[:, :hidden_cols], summed[:, hidden_cols:], cotangent)
    piece_gate = lax.all_gather(d_gate, "row", axis=0, tiled=True)
    piece_up = lax.all_gather(d_up, "row", axis=0, tiled=True)
    token_rows = panels
    gate_acc = over_tokens(token_rows, piece_gate)
    up_acc = over_tokens(token_rows, piece_up)
    input_term = over_hidden(piece_gate, gate_weight) + over_hidden(piece_up, up_weight)
    input_grad = lax.psum_scatter(input_term, "col", scatter_dimension=0, tiled=True).astype(
        jnp.bfloat16
    )
    return (input_grad, gate_acc.astype(jnp.bfloat16), up_acc.astype(jnp.bfloat16))


def solution(mesh):
    in_specs = (P("row", None), P("row", "col"), P("row", "col"), P("row", "col"))
    out_specs = (P("col", "row"), P("row", "col"), P("row", "col"))
    return jax.shard_map(shards, mesh=mesh, in_specs=in_specs, out_specs=out_specs, check_vma=False)
```

profile of v0, /device:TPU:2, one launch (start us, length us, event | category | flops | bytes accessed | tf_op | source)
XLA Modules:
  0.0 353.3 jit_solution(9734142860770051894)
XLA Ops:
  7.2 0.0 reduce-scatter.7.cloned.1.call-start
  7.2 1.0 copy.32
  8.2 21.6 %all_to_all.19 = bf16[32,16,384]{2,0,1:T(8,128)(2,1)S(1)} all-to-all(bf16[32,16,384]{2,0,1:T(8,128)(2,1)S(1)} %bitcast.26), channel_id=1, replica_groups=mesh['row'=16,'col'=32] {'row'}, dimensions={1} | all-to-all | bytes 786432 | tf_op jit(solution)/shard_map/all_to_all | solution.py:30
  29.9 2.3 convolution_bitcast_fusion
  32.2 2.3 copy.28
  34.5 0.0 copy-start.2
  34.5 0.0 copy-start
  34.5 0.0 reduce-scatter.7.cloned.1.call-update
  34.5 0.0 copy-start.1
  34.5 0.0 reduce-scatter.5.cloned.1.call-start
  34.6 91.7 %reduce-scatter.7.cloned.1.call-done = f32[32,1536]{1,0:T(8,128)} async-done(((f32[512,1536]{1,0:T(8,128)}), f32[32,1536]{1,0:T(8,128)}) %reduce-scatter.7.cloned.1.call-update) | async-done | bytes 196624 | tf_op jit(solution)/shard_map/reduce_scatter | solution.py:34
  126.2 0.0 copy-done.2
  126.2 1.0 fusion.9
  127.2 46.3 %all_gather.7 = bf16[512,768]{1,0:T(8,128)(2,1)S(1)} all-gather(bf16[32,768]{1,0:T(8,128)(2,1)S(1)} %get-tuple-element.18), channel_id=1, replica_groups=mesh['row'=16,'col'=32] {'row'}, dimensions={0}, use_global_device_ids=true | all-gather | bytes 835584 | tf_op jit(solution)/shard_map/all_gather | solution.py:42
  173.6 42.9 %all_gather.6 = bf16[512,768]{1,0:T(8,128)(2,1)S(1)} all-gather(bf16[32,768]{1,0:T(8,128)(2,1)S(1)} %get-tuple-element.19), channel_id=1, replica_groups=mesh['row'=16,'col'=32] {'row'}, dimensions={0}, use_global_device_ids=true | all-gather | bytes 835584 | tf_op jit(solution)/shard_map/all_gather | solution.py:41
  216.4 0.0 copy-done
  216.4 0.6 fusion.11
  217.0 0.0 copy-done.1
  217.0 1.5 convolution_add_fusion
  218.5 0.0 reduce-scatter.5.cloned.1.call-update
  218.5 0.6 fusion.1
  219.2 1.1 copy.27
  220.2 0.6 fusion
  220.8 1.1 copy.26
  221.9 123.2 %reduce-scatter.5.cloned.1.call-done = f32[16,384]{1,0:T(8,128)} async-done(((f32[512,384]{1,0:T(8,128)}), f32[16,384]{1,0:T(8,128)}) %reduce-scatter.5.cloned.1.call-update) | async-done | bytes 24592 | tf_op jit(solution)/shard_map/reduce_scatter | solution.py:47
  345.1 1.3 convert_element_type.27
Async XLA Ops:
  7.2 119.1 %reduce-scatter.7.cloned.1.call-start = ((), (), s32[]{:S(2)}) async-start(), calls=%async_computation.4 | async-start | bytes 3342336 | tf_op jit(solution)/shard_map/reduce_scatter | solution.py:34
  34.5 91.7 %copy-start.2 = (bf16[32,768]{1,0:T(8,128)(2,1)S(1)}, bf16[32,768]{1,0:T(8,128)(2,1)}, u32[]{:S(2)}) copy-start(bf16[32,768]{1,0:T(8,128)(2,1)} %param.5) | copy-start | bytes 147460
  34.5 181.9 %copy-start = (bf16[384,768]{1,0:T(8,128)(2,1)S(1)}, bf16[384,768]{1,0:T(8,128)(2,1)}, u32[]{:S(2)}) copy-start(bf16[384,768]{1,0:T(8,128)(2,1)} %param.6) | copy-start | bytes 1769476
  34.5 182.5 %copy-start.1 = (bf16[384,768]{1,0:T(8,128)(2,1)S(1)}, bf16[384,768]{1,0:T(8,128)(2,1)}, u32[]{:S(2)}) copy-start(bf16[384,768]{1,0:T(8,128)(2,1)} %param.7) | copy-start | bytes 1769476
  34.5 310.5 %reduce-scatter.5.cloned.1.call-start = ((), (), s32[]{:S(2)}) async-start(), calls=%async_computation.3 | async-start | bytes 811008 | tf_op jit(solution)/shard_map/reduce_scatter | solution.py:47
Sparse Core Ops, SparseCore 0:
  34.6 91.5 reduce-scatter.6
  218.7 126.3 reduce-scatter.4
where the time goes:
time: 354 us; the launch traced here: 353 us
  waiting for transfers between devices  215 us (61%)
  blocking collectives  111 us (31%)
  between operations  14.1 us (4%)
  local copies, waits for them, and re-layouts  5.55 us (2%)
  matrix products  5.54 us (2%)
    reduce_scatter x1, waiting for transfers between devices, shards(): lax.psum_scatter(input_term, 'col', scatter_dimension=0, tiled=True)  123 us
    reduce_scatter x1, waiting for transfers between devices, shards(): lax.psum_scatter(jnp.dot(token_rows, joined, preferred_element_type=jnp.f...  91.7 us
    all_gather x1, blocking collectives, shards(): piece_up = lax.all_gather(d_up, 'row', axis=0, tiled=True)  46.3 us
    all_gather x1, blocking collectives, shards(): piece_gate = lax.all_gather(d_gate, 'row', axis=0, tiled=True)  42.9 us
    all_to_all x1, blocking collectives, shards(): lax.all_to_all(inputs, 'row', split_axis=1, concat_axis=0, tiled=True)  21.6 us
  transfers between devices with their start and end apart: 2, of which 2 were waited for; matrix products, arithmetic and copies ran while one was open for 1% of the time, Pallas kernels for 0%

commit v1 on v0

v1 whole, which is shorter than its diff:
```python
import jax
import jax.numpy as jnp
from jax import lax
from jax.sharding import PartitionSpec as P


def over_tokens(left, right):
    return lax.dot_general(
        left, right, (((0,), (0,)), ((), ())), preferred_element_type=jnp.float32
    )


def over_hidden(left, right):
    return lax.dot_general(
        left, right, (((1,), (1,)), ((), ())), preferred_element_type=jnp.float32
    )


def local_grads(gate_full, up_full, cotangent):
    sigmoid_gate = jax.nn.sigmoid(gate_full)
    cot_wide = cotangent.astype(jnp.float32)
    d_gate = (cot_wide * up_full * sigmoid_gate * (1.0 + gate_full * (1.0 - sigmoid_gate))).astype(
        jnp.bfloat16
    )
    d_up = (cot_wide * gate_full * sigmoid_gate).astype(jnp.bfloat16)
    return (d_gate, d_up)


def shards(rows, cols, inputs, cotangent, gate_weight, up_weight):
    depth, hidden = gate_weight.shape
    own = inputs.shape[0]
    tokens = own * rows
    panels = lax.all_to_all(inputs, "row", split_axis=1, concat_axis=0, tiled=True)
    joined = jnp.concatenate([gate_weight, up_weight], axis=1)
    partial = jnp.dot(panels, joined, preferred_element_type=jnp.float32).astype(jnp.bfloat16)
    parts = lax.all_to_all(partial.reshape(rows, own, 2 * hidden), "row", 0, 0)
    summed = jnp.sum(parts.astype(jnp.float32), axis=0)
    d_gate, d_up = local_grads(summed[:, :hidden], summed[:, hidden:], cotangent)
    d_own = jnp.concatenate([d_gate, d_up], axis=1)
    d_all = lax.all_to_all(jnp.broadcast_to(d_own[None], (rows, own, 2 * hidden)), "row", 0, 0)
    d_all = d_all.reshape(tokens, 2 * hidden)
    input_term = over_hidden(d_all, joined).astype(jnp.bfloat16)
    pieces = lax.all_to_all(input_term.reshape(cols, tokens // cols, depth), "col", 0, 0)
    grads = over_tokens(panels, d_all).astype(jnp.bfloat16)
    input_grad = jnp.sum(pieces.astype(jnp.float32), axis=0).astype(jnp.bfloat16)
    return (input_grad, grads[:, :hidden], grads[:, hidden:])


def solution(mesh):
    in_specs = (P("row", None), P("row", "col"), P("row", "col"), P("row", "col"))
    out_specs = (P("col", "row"), P("row", "col"), P("row", "col"))
    rows, cols = mesh.shape["row"], mesh.shape["col"]

    def local(*arrays):
        return shards(rows, cols, *arrays)

    return jax.shard_map(local, mesh=mesh, in_specs=in_specs, out_specs=out_specs, check_vma=False)
```

time: 354 us -> 144 us (0.41)
  the two profiles are of different devices: /device:TPU:2 before, /device:TPU:1 now
where the time goes in v1:
time: 144 us
  blocking collectives  81.7 us (57%)
  starting transfers between devices  26.4 us (18%)
  waiting for transfers between devices  25.1 us (17%)
  local copies, waits for them, and re-layouts  4.95 us (3%)
  matrix products  3.73 us (3%)
    all_to_all x1, blocking collectives, shards(): lax.all_to_all(jnp.broadcast_to(d_own[None], (rows, own, 2 * hidden)), 'r...  41 us
    all_to_all x1, blocking collectives, shards(): parts = lax.all_to_all(partial.reshape(rows, own, 2 * hidden), 'row', 0, 0)  40.7 us
    all_to_all x1, starting transfers between devices, shards(): lax.all_to_all(input_term.reshape(cols, tokens // cols, depth), 'col', 0, 0)  16 us
    all_to_all x1, waiting for transfers between devices, shards(): lax.all_to_all(input_term.reshape(cols, tokens // cols, depth), 'col', 0, 0)  13.5 us
    all_to_all x1, waiting for transfers between devices, shards(): lax.all_to_all(inputs, 'row', split_axis=1, concat_axis=0, tiled=True)  11.6 us
    all_to_all x1, starting transfers between devices, shards(): lax.all_to_all(inputs, 'row', split_axis=1, concat_axis=0, tiled=True)  10.4 us
  transfers between devices with their start and end apart: 2, of which 2 were waited for; matrix products, arithmetic and copies ran while one was open for 2% of the time, Pallas kernels for 0%

profile of v1, /device:TPU:1, one launch (start us, length us, event | category | flops | bytes accessed | tf_op | source)
XLA Modules:
  0.0 143.5 jit_solution(9849541400189993264)
XLA Ops:
  0.6 0.0 copy-start
  0.6 0.0 copy-start.1
  0.7 1.9 %copy.14 = bf16[4,16,8,384]{3,2,0,1:T(8,128)(2,1)} copy(bf16[4,16,8,384]{3,2,1,0:T(8,128)(2,1)} %bitcast.30) | data formatting | bytes 786432 | tf_op jit(solution)/shard_map/all_to_all | solution.py:33
  2.5 10.4 %all-to-all-start = ((bf16[32,16,384]{2,0,1:T(8,128)(2,1)}), bf16[32,16,384]{2,0,1:T(8,128)(2,1)S(1)}, u32[]{:S(2)}, u32[]{:S(2)}) async-start(bf16[32,16,384]{2,0,1:T(8,128)(2,1)} %bitcast.26), calls=%async_computation | async-start | bytes 786432 | tf_op jit(solution)/shard_map/all_to_all | solution.py:33
  12.9 0.0 copy-done
  13.0 0.0 copy-done.1
  13.0 11.6 %all-to-all-done = bf16[32,16,384]{2,0,1:T(8,128)(2,1)S(1)} async-done(((bf16[32,16,384]{2,0,1:T(8,128)(2,1)}), bf16[32,16,384]{2,0,1:T(8,128)(2,1)S(1)}, u32[]{:S(2)}, u32[]{:S(2)}) %all-to-all-start) | async-done | bytes 393248 | tf_op jit(solution)/shard_map/all_to_all | solution.py:33
  24.6 1.0 convolution_convert_fusion
  25.6 40.7 %all_to_all.34 = bf16[16,32,1536]{2,1,0:T(8,128)(2,1)S(1)} all-to-all(bf16[16,32,1536]{2,1,0:T(8,128)(2,1)S(1)} %bitcast.27), channel_id=1, replica_groups=mesh['row'=16,'col'=32] {'row'}, dimensions={0} | all-to-all | bytes 3145728 | tf_op jit(solution)/shard_map/all_to_all | solution.py:36
  66.3 0.0 copy-start.2
  66.3 0.2 convert_reduce_fusion
  66.5 0.6 copy-done.2
  67.1 0.1 fusion.5
  67.1 0.1 broadcast_in_dim.2
  67.3 41.0 %all_to_all.35 = bf16[16,32,1536]{2,1,0:T(8,128)(2,1)S(1)} all-to-all(bf16[16,32,1536]{2,1,0:T(8,128)(2,1)S(1)} %broadcast_in_dim.2), channel_id=1, replica_groups=mesh['row'=16,'col'=32] {'row'}, dimensions={0} | all-to-all | bytes 3145728 | tf_op jit(solution)/shard_map/all_to_all | solution.py:40
  108.3 1.7 %convolution_convert_fusion.1 = bf16[512,384]{1,0:T(8,128)(2,1)} fusion(bf16[512,1536]{1,0:T(8,128)(2,1)S(1)} %bitcast.28, bf16[384,1536]{1,0:T(8,128)(2,1)S(1)} %constant_dynamic-update-slice_fusion), kind=kOutput, calls=%fused_computation.5 | convolution fusion | flops 604176384 | bytes 3145728 | tf_op jit(solution)/shard_map/dot_general | solution.py:14
  110.0 16.0 %all-to-all-start.3 = ((bf16[32,16,384]{2,1,0:T(8,128)(2,1)}), bf16[32,16,384]{2,1,0:T(8,128)(2,1)S(1)}, u32[]{:S(2)}, u32[]{:S(2)}) async-start(bf16[32,16,384]{2,1,0:T(8,128)(2,1)} %bitcast.5), calls=%async_computation.3 | async-start | bytes 786432 | tf_op jit(solution)/shard_map/all_to_all | solution.py:43
  126.1 1.0 fusion.1
  127.1 0.1 fusion.8
  127.2 1.1 copy.11
  128.3 1.1 copy.10
  129.4 13.5 %all-to-all-done.3 = bf16[32,16,384]{2,1,0:T(8,128)(2,1)S(1)} async-done(((bf16[32,16,384]{2,1,0:T(8,128)(2,1)}), bf16[32,16,384]{2,1,0:T(8,128)(2,1)S(1)}, u32[]{:S(2)}, u32[]{:S(2)}) %all-to-all-start.3) | async-done | bytes 393248 | tf_op jit(solution)/shard_map/all_to_all | solution.py:43
  142.9 0.7 reduce_sum.22
  (3 shorter events, 0.1 us)
Async XLA Ops:
  0.6 12.3 %copy-start = (bf16[384,768]{1,0:T(8,128)(2,1)S(1)}, bf16[384,768]{1,0:T(8,128)(2,1)}, u32[]{:S(2)}) copy-start(bf16[384,768]{1,0:T(8,128)(2,1)} %param.6) | copy-start | bytes 1769476
  0.6 12.3 %copy-start.1 = (bf16[384,768]{1,0:T(8,128)(2,1)S(1)}, bf16[384,768]{1,0:T(8,128)(2,1)}, u32[]{:S(2)}) copy-start(bf16[384,768]{1,0:T(8,128)(2,1)} %param.7) | copy-start | bytes 1769476
  2.5 22.1 %all-to-all-start = ((bf16[32,16,384]{2,0,1:T(8,128)(2,1)}), bf16[32,16,384]{2,0,1:T(8,128)(2,1)S(1)}, u32[]{:S(2)}, u32[]{:S(2)}) async-start(bf16[32,16,384]{2,0,1:T(8,128)(2,1)} %bitcast.26), calls=%async_computation | async-start | bytes 786432 | tf_op jit(solution)/shard_map/all_to_all | solution.py:33
  66.3 0.8 copy-start.2
  110.0 32.8 %all-to-all-start.3 = ((bf16[32,16,384]{2,1,0:T(8,128)(2,1)}), bf16[32,16,384]{2,1,0:T(8,128)(2,1)S(1)}, u32[]{:S(2)}, u32[]{:S(2)}) async-start(bf16[32,16,384]{2,1,0:T(8,128)(2,1)} %bitcast.5), calls=%async_computation.3 | async-start | bytes 786432 | tf_op jit(solution)/shard_map/all_to_all | solution.py:43

commit v2 on v1

v2 whole, which is shorter than its diff:
```python
import functools

import jax
import jax.numpy as jnp
from jax import lax
from jax.experimental import pallas as pl
from jax.experimental.pallas import tpu as pltpu
from jax.sharding import PartitionSpec as P

GROUP = 8
VMEM_BYTES = 40 * 1024 * 1024

VMEM = pl.BlockSpec(memory_space=pltpu.VMEM)
SMEM = pl.BlockSpec(memory_space=pltpu.SMEM)
BF16, F32 = jnp.bfloat16, jnp.float32


def rows_at(start, size):
    return pl.ds(pl.multiple_of(start * size, size), size)


def lay_kernel(where_ref, tokens_ref, out_ref):
    rows, own, depth = out_ref.shape
    at = rows_at(where_ref[0], own)
    for row in range(rows):
        out_ref[row] = tokens_ref[at, row * depth : (row + 1) * depth]


def forward_kernel(where_ref, mine_ref, other_ref, gate_ref, up_ref, out_ref):
    rows, own, depth = mine_ref.shape
    hidden = gate_ref.shape[1]
    for side_core, tokens_ref in enumerate((mine_ref, other_ref)):
        half = jnp.bitwise_xor(where_ref[0], side_core)
        tokens = tokens_ref[...].reshape(rows * own, depth)
        for i, weight_ref in enumerate((gate_ref, up_ref)):
            total = jnp.dot(tokens, weight_ref[...], preferred_element_type=F32).astype(BF16)
            for row in range(rows):
                side, m = divmod(row, GROUP)
                out_ref[m, rows_at(2 * side + half, own), i * hidden : (i + 1) * hidden] = total[
                    row * own : (row + 1) * own
                ]


def sum_kernel(where_ref, parts_ref, keep_ref, send_ref):
    count = parts_ref.shape[0]
    rows = keep_ref.shape[0]
    for ref, side in ((send_ref, 1 - where_ref[0]), (keep_ref, where_ref[0])):
        at = rows_at(side, rows)
        total = parts_ref[0, at, :].astype(F32)
        for part in range(1, count):
            total += parts_ref[part, at, :].astype(F32)
        ref[...] = total.astype(ref.dtype)


def act_kernel(keep_ref, came_ref, cot_ref, out_ref):
    hidden = cot_ref.shape[1]
    total = keep_ref[...] + came_ref[...].astype(F32)
    gate, up = total[:, :hidden], total[:, hidden:]
    cot = cot_ref[...].astype(F32)
    sig = 1.0 / (1.0 + jnp.exp(-gate))
    out_ref[:, :hidden] = (cot * up * sig * (1.0 + gate * (1.0 - sig))).astype(BF16)
    out_ref[:, hidden:] = (cot * gate * sig).astype(BF16)


def copies_kernel(where_ref, mine_ref, other_ref, out_ref):
    rows = mine_ref.shape[0]
    mine, other = mine_ref[...], other_ref[...]
    for m in range(out_ref.shape[0]):
        out_ref[m, rows_at(where_ref[0], rows), :] = mine
        out_ref[m, rows_at(1 - where_ref[0], rows), :] = other


def half_tokens(d_ref, half, own):
    return jnp.concatenate(
        [
            d_ref[m, rows_at(2 * side + half, own), :]
            for side in range(2)
            for m in range(GROUP)
        ],
        axis=0,
    )


def over_hidden(left, right):
    return lax.dot_general(left, right, (((1,), (1,)), ((), ())), preferred_element_type=F32)


def over_tokens(left, right):
    return lax.dot_general(left, right, (((0,), (0,)), ((), ())), preferred_element_type=F32)


def term_of(half, own, d_ref, gate_ref, up_ref):
    hidden = gate_ref.shape[1]
    d = half_tokens(d_ref, half, own)
    return over_hidden(d[:, :hidden], gate_ref[...]) + over_hidden(d[:, hidden:], up_ref[...])


def other_term_kernel(where_ref, d_ref, gate_ref, up_ref, out_ref):
    own = d_ref.shape[1] // 4
    out_ref[...] = term_of(1 - where_ref[0], own, d_ref, gate_ref, up_ref)


def own_term_kernel(where_ref, d_ref, gate_ref, up_ref, came_ref, out_ref):
    own = d_ref.shape[1] // 4
    total = term_of(where_ref[0], own, d_ref, gate_ref, up_ref) + came_ref[...]
    out_ref[...] = total.astype(BF16).reshape(out_ref.shape)


def weight_grad_kernel(where_ref, mine_ref, other_ref, d_ref, gate_ref, up_ref):
    rows, own, depth = mine_ref.shape
    hidden = gate_ref.shape[1]
    mine = mine_ref[...].reshape(rows * own, depth)
    other = other_ref[...].reshape(rows * own, depth)
    d_mine = half_tokens(d_ref, where_ref[0], own)
    d_other = half_tokens(d_ref, 1 - where_ref[0], own)
    for i, ref in enumerate((gate_ref, up_ref)):
        span = slice(i * hidden, (i + 1) * hidden)
        total = over_tokens(mine, d_mine[:, span]) + over_tokens(other, d_other[:, span])
        ref[...] = total.astype(BF16)


def call(kernel, outs, n_where, n_in, flops=0, nbytes=0):
    return pl.pallas_call(
        kernel,
        out_shape=outs,
        in_specs=[SMEM] * n_where + [VMEM] * n_in,
        out_specs=jax.tree.map(lambda _: VMEM, outs),
        compiler_params=pltpu.CompilerParams(vmem_limit_bytes=VMEM_BYTES),
        cost_estimate=pl.CostEstimate(flops=flops, bytes_accessed=nbytes, transcendentals=0),
    )


def shards(rows, cols, inputs, cotangent, gate_weight, up_weight):
    depth, hidden = gate_weight.shape
    tokens = inputs.shape[0]
    own = tokens // 2
    wide = 2 * hidden
    flops = 2 * rows * tokens * depth * wide
    pairs = [list(range(0, GROUP)), list(range(GROUP, 2 * GROUP))]
    y_groups = [[4 * y + k for y in range(cols // 4)] for k in range(4)]
    row, col = lax.axis_index("row"), lax.axis_index("col")

    def scalar(value):
        return value.astype(jnp.int32).reshape(1)

    side, core = scalar(row // GROUP), scalar(col % 2)
    z_hi = scalar((col // 2) % 2)

    def shape(dims, dtype=BF16):
        return jax.ShapeDtypeStruct(dims, dtype)

    def exchange(array, axis, groups=None):
        return lax.all_to_all(array, axis, 0, 0, axis_index_groups=groups)

    def swap(array, axis, count, bit):
        return lax.ppermute(array, axis, [(i, i ^ bit) for i in range(count)])

    sent = call(lay_kernel, shape((rows, own, depth)), 1, 1)(core, inputs)
    mine = exchange(sent, "row")
    other = swap(mine, "col", cols, 1)

    partial = call(forward_kernel, shape((GROUP, 2 * tokens, wide)), 1, 4, flops)(
        core, mine, other, gate_weight, up_weight
    )
    parts = exchange(partial, "row", pairs)
    keep, send = call(sum_kernel, [shape((tokens, wide), F32), shape((tokens, wide))], 1, 1)(
        side, parts
    )
    came = swap(send, "row", rows, GROUP)
    d_own = call(act_kernel, shape((tokens, wide)), 0, 3)(keep, came, cotangent)
    d_far = swap(d_own, "row", rows, GROUP)
    copies = call(copies_kernel, shape((GROUP, 2 * tokens, wide)), 1, 2)(side, d_own, d_far)
    d_all = exchange(copies, "row", pairs)

    far_term = call(other_term_kernel, shape((rows * own, depth), F32), 1, 3, flops // 2)(
        core, d_all, gate_weight, up_weight
    )
    came_term = swap(far_term, "col", cols, 1)
    term = call(own_term_kernel, shape((rows // 2, 2 * own, depth)), 1, 4, flops // 2)(
        core, d_all, gate_weight, up_weight, came_term
    )
    over_y = exchange(term, "col", y_groups)
    keep, send = call(sum_kernel, [shape((own, depth), F32), shape((own, depth), F32)], 1, 1)(
        z_hi, over_y
    )
    input_grad = (keep + swap(send, "col", cols, 2)).astype(BF16)

    grad = shape((depth, hidden))
    gate_grad, up_grad = call(weight_grad_kernel, [grad, grad], 1, 3, flops)(
        core, mine, other, d_all
    )
    return (input_grad, gate_grad, up_grad)


def solution(mesh):
    in_specs = (P("row", None), P("row", "col"), P("row", "col"), P("row", "col"))
    out_specs = (P("col", "row"), P("row", "col"), P("row", "col"))
    local = functools.partial(shards, mesh.shape["row"], mesh.shape["col"])
    return jax.shard_map(local, mesh=mesh, in_specs=in_specs, out_specs=out_specs, check_vma=False)
```

time: 144 us -> 128 us (0.89)
  blocking collectives: 81.7 us -> 44.1 us
  waiting for transfers between devices: 25.1 us -> 41.6 us
  Pallas kernels: 0 us -> 6.07 us
  starting transfers between devices: 26.4 us -> 31.3 us
  matrix products: 3.73 us -> 0 us
  local copies, waits for them, and re-layouts: 4.95 us -> 3.14 us
    all_to_all x2, blocking collectives: 81.7 us -> 44.1 us  [exchange(): return lax.all_to_all(array, axis, 0, 0, axis_index_groups=groups)]
    ppermute x0 -> x5, starting transfers between devices: none -> 20.9 us  [swap(): return lax.ppermute(array, axis, [(i, i ^ bit) for i in range(count)])]
    all_to_all x2, starting transfers between devices: 26.4 us -> 10.4 us  [exchange(): return lax.all_to_all(array, axis, 0, 0, axis_index_groups=groups)]
    ppermute x0 -> x5, waiting for transfers between devices: none -> 11.7 us  [swap(): return lax.ppermute(array, axis, [(i, i ^ bit) for i in range(count)])]
    pallas_call x0 -> x9, Pallas kernels: none -> 6.07 us  [the longest x1 2.17 us: shards(): call(forward_kernel, shape((GROUP, 2 * tokens, wide)), 1, 4, flops)]
    all_to_all x2, waiting for transfers between devices: 25.1 us -> 29.9 us  [exchange(): return lax.all_to_all(array, axis, 0, 0, axis_index_groups=groups)]
    dot_general x3 -> x0, matrix products: 3.73 us -> none  [the longest x1 1.75 us: over_hidden(): lax.dot_general(left, right, (((1,), (1,)), ((), ())), preferred_element_...]
    all_to_all x1 -> x0, local copies, waits for them, and re-layouts: 1.87 us -> none  [shards(): lax.all_to_all(inputs, 'row', split_axis=1, concat_axis=0, tiled=True)]
  transfers between devices with their start and end apart: 2 -> 7, of which waited for: 2 -> 6; matrix products, arithmetic and copies ran while one was open for 2% -> 0% of each run, Pallas kernels for 0% -> 1%
where the time goes in v2:
time: 128 us
  blocking collectives  44.1 us (34%)
  waiting for transfers between devices  41.6 us (32%)
  starting transfers between devices  31.3 us (24%)
  Pallas kernels  6.07 us (5%)
  local copies, waits for them, and re-layouts  3.14 us (2%)
    all_to_all x2, blocking collectives, exchange(): return lax.all_to_all(array, axis, 0, 0, axis_index_groups=groups)  44.1 us
    all_to_all x2, waiting for transfers between devices, exchange(): return lax.all_to_all(array, axis, 0, 0, axis_index_groups=groups)  29.9 us
    ppermute x5, starting transfers between devices, swap(): return lax.ppermute(array, axis, [(i, i ^ bit) for i in range(count)])  20.9 us
    ppermute x5, waiting for transfers between devices, swap(): return lax.ppermute(array, axis, [(i, i ^ bit) for i in range(count)])  11.7 us
    all_to_all x2, starting transfers between devices, exchange(): return lax.all_to_all(array, axis, 0, 0, axis_index_groups=groups)  10.4 us
    unnamed x12, local copies, waits for them, and re-layouts  3.14 us
  transfers between devices with their start and end apart: 7, of which 6 were waited for; matrix products, arithmetic and copies ran while one was open for 0% of the time, Pallas kernels for 1%

profile of v2, /device:TPU:1, one launch (start us, length us, event | category | flops | bytes accessed | tf_op | source)
XLA Modules:
  0.0 127.6 jit_solution(14220997921426091786)
XLA Ops:
  0.6 0.0 copy-start.4
  0.7 1.0 copy-done.4
  1.7 18.6 %all_to_all.20.mine_ref = bf16[16,16,384]{2,1,0:T(8,128)(2,1)S(1)} all-to-all(bf16[16,16,384]{2,1,0:T(8,128)(2,1)S(1)} %shard_map.67), channel_id=1, replica_groups=mesh['row'=16,'col'=32] {'row'}, dimensions={0} | all-to-all | bytes 393216 | tf_op jit(solution)/shard_map/all_to_all | solution.py:153
  20.3 4.1 %collective-permute-start = (bf16[16,16,384]{2,1,0:T(8,128)(2,1)S(1)}, bf16[16,16,384]{2,1,0:T(8,128)(2,1)S(1)}, u32[]{:S(2)}, u32[]{:S(2)}) collective-permute-start(bf16[16,16,384]{2,1,0:T(8,128)(2,1)S(1)} %all_to_all.20.mine_ref), channel_id=1, source_target_pairs={{0,1},{1,0},{2,3},{3,2},{4,5},{5,4},{6,7},{7,6},{8,9},{9,8},{10,11... | collective-permute-start | bytes 589832 | tf_op jit(solution)/shard_map/ppermute | solution.py:156
  24.3 1.0 collective-permute-done.other_ref
  25.4 0.0 copy-start
  25.4 1.1 copy-done
  26.4 0.0 copy-start.2
  26.4 1.1 copy-done.2
  27.5 2.2 %shard_map.68 = bf16[8,64,1536]{2,1,0:T(8,128)(2,1)} custom-call(s32[1]{0:T(128)} %bitcast.1.where_ref, bf16[16,16,384]{2,1,0:T(8,128)(2,1)S(1)} %all_to_all.20.mine_ref, bf16[16,16,384]{2,1,0:T(8,128)(2,1)S(1)} %collective-permute-done.other_ref, bf16[384,768]{1,0:T(8,128)(2,1)S(1)} %copy-done, bf16[384,768]{1,0:T(8,128)(2,1)S(1)} %copy-done.2), custom_call_target="tpu_custom_call" | custom-call | flops 603979776 | tf_op jit(solution)/shard_map/pallas_call | solution.py:162
  29.7 3.6 %all-to-all-start.1 = ((bf16[8,64,1536]{2,1,0:T(8,128)(2,1)}), bf16[8,64,1536]{2,1,0:T(8,128)(2,1)S(1)}, u32[]{:S(2)}, u32[]{:S(2)}) async-start(bf16[8,64,1536]{2,1,0:T(8,128)(2,1)} %shard_map.68), calls=%async_computation.1 | async-start | bytes 3145728 | tf_op jit(solution)/shard_map/all_to_all | solution.py:153
  33.3 0.0 copy-start.5
  33.3 20.5 %all-to-all-done.1.parts_ref = bf16[8,64,1536]{2,1,0:T(8,128)(2,1)S(1)} async-done(((bf16[8,64,1536]{2,1,0:T(8,128)(2,1)}), bf16[8,64,1536]{2,1,0:T(8,128)(2,1)S(1)}, u32[]{:S(2)}, u32[]{:S(2)}) %all-to-all-start.1) | async-done | bytes 1572896 | tf_op jit(solution)/shard_map/all_to_all | solution.py:153
  53.8 0.2 shard_map.69
  54.0 2.3 %collective-permute-start.1 = (bf16[32,1536]{1,0:T(8,128)(2,1)S(1)}, bf16[32,1536]{1,0:T(8,128)(2,1)S(1)}, u32[]{:S(2)}, u32[]{:S(2)}) collective-permute-start(bf16[32,1536]{1,0:T(8,128)(2,1)S(1)} %get-tuple-element.10), channel_id=1, source_target_pairs={{0,256},{32,288},{64,320},{96,352},{128,384},{160,416},{192,448},{... | collective-permute-start | bytes 294920 | tf_op jit(solution)/shard_map/ppermute | solution.py:156
  56.3 5.0 %collective-permute-done.1.came_ref = bf16[32,1536]{1,0:T(8,128)(2,1)S(1)} collective-permute-done((bf16[32,1536]{1,0:T(8,128)(2,1)S(1)}, bf16[32,1536]{1,0:T(8,128)(2,1)S(1)}, u32[]{:S(2)}, u32[]{:S(2)}) %collective-permute-start.1) | collective-permute-done | bytes 98336 | tf_op jit(solution)/shard_map/ppermute | solution.py:156
  61.3 0.0 copy-done.5
  61.3 0.1 shard_map.70.mine_ref
  61.4 1.9 %collective-permute-start.2 = (bf16[32,1536]{1,0:T(8,128)(2,1)S(1)}, bf16[32,1536]{1,0:T(8,128)(2,1)S(1)}, u32[]{:S(2)}, u32[]{:S(2)}) collective-permute-start(bf16[32,1536]{1,0:T(8,128)(2,1)S(1)} %shard_map.70.mine_ref), channel_id=1, source_target_pairs={{0,256},{32,288},{64,320},{96,352},{128,384},{160,416},{192,448},{... | collective-permute-start | bytes 294920 | tf_op jit(solution)/shard_map/ppermute | solution.py:156
  63.3 4.3 %collective-permute-done.2.other_ref = bf16[32,1536]{1,0:T(8,128)(2,1)S(1)} collective-permute-done((bf16[32,1536]{1,0:T(8,128)(2,1)S(1)}, bf16[32,1536]{1,0:T(8,128)(2,1)S(1)}, u32[]{:S(2)}, u32[]{:S(2)}) %collective-permute-start.2) | collective-permute-done | bytes 98336 | tf_op jit(solution)/shard_map/ppermute | solution.py:156
  67.6 0.1 shard_map.71
  67.7 0.0 copy-start.1
  67.8 0.0 copy-start.3
  67.8 25.5 %all_to_all.21.d_ref = bf16[8,64,1536]{2,1,0:T(8,128)(2,1)S(1)} all-to-all(bf16[8,64,1536]{2,1,0:T(8,128)(2,1)S(1)} %shard_map.71), channel_id=1, replica_groups={{0,32,64,96,128,160,192,224},{256,288,320,352,384,416,448,480},{1,33,65..., dimensions={0} | all-to-all | bytes 3145728 | tf_op jit(solution)/shard_map/all_to_all | solution.py:153
  93.3 0.0 copy-done.1
  93.3 0.0 copy-done.3
  93.3 0.6 shard_map.72
  93.9 4.6 %collective-permute-start.3 = (f32[256,384]{1,0:T(8,128)S(1)}, f32[256,384]{1,0:T(8,128)S(1)}, u32[]{:S(2)}, u32[]{:S(2)}) collective-permute-start(f32[256,384]{1,0:T(8,128)S(1)} %shard_map.72), channel_id=1, source_target_pairs={{0,1},{1,0},{2,3},{3,2},{4,5},{5,4},{6,7},{7,6},{8,9},{9,8},{10,11... | collective-permute-start | bytes 1179656 | tf_op jit(solution)/shard_map/ppermute | solution.py:156
  98.5 1.3 %collective-permute-done.3.came_ref = f32[256,384]{1,0:T(8,128)S(1)} collective-permute-done((f32[256,384]{1,0:T(8,128)S(1)}, f32[256,384]{1,0:T(8,128)S(1)}, u32[]{:S(2)}, u32[]{:S(2)}) %collective-permute-start.3) | collective-permute-done | bytes 393248 | tf_op jit(solution)/shard_map/ppermute | solution.py:156
  99.8 1.3 shard_map.73
  101.1 6.8 %all-to-all-start.3 = ((bf16[8,32,384]{2,1,0:T(8,128)(2,1)}), bf16[8,32,384]{2,1,0:T(8,128)(2,1)S(1)}, u32[]{:S(2)}, u32[]{:S(2)}) async-start(bf16[8,32,384]{2,1,0:T(8,128)(2,1)} %shard_map.73), calls=%async_computation.3 | async-start | bytes 393216 | tf_op jit(solution)/shard_map/all_to_all | solution.py:153
  108.0 9.4 %all-to-all-done.3.parts_ref = bf16[8,32,384]{2,1,0:T(8,128)(2,1)S(1)} async-done(((bf16[8,32,384]{2,1,0:T(8,128)(2,1)}), bf16[8,32,384]{2,1,0:T(8,128)(2,1)S(1)}, u32[]{:S(2)}, u32[]{:S(2)}) %all-to-all-start.3) | async-done | bytes 196640 | tf_op jit(solution)/shard_map/all_to_all | solution.py:153
  117.4 7.9 %collective-permute-start.4 = (f32[16,384]{1,0:T(8,128)S(1)}, f32[16,384]{1,0:T(8,128)S(1)}, u32[]{:S(2)}, u32[]{:S(2)}) collective-permute-start(f32[16,384]{1,0:T(8,128)S(1)} %get-tuple-element.12), channel_id=1, source_target_pairs={{0,2},{1,3},{2,0},{3,1},{4,6},{5,7},{6,4},{7,5},{8,10},{9,11},{10,... | collective-permute-start | bytes 73736 | tf_op jit(solution)/shard_map/ppermute | solution.py:156
  125.4 1.6 %shard_map.75 = (bf16[384,768]{1,0:T(8,128)(2,1)}, bf16[384,768]{1,0:T(8,128)(2,1)}) custom-call(s32[1]{0:T(128)} %bitcast.1.where_ref, bf16[16,16,384]{2,1,0:T(8,128)(2,1)S(1)} %all_to_all.20.mine_ref, bf16[16,16,384]{2,1,0:T(8,128)(2,1)S(1)} %collective-permute-done.other_ref, bf16[8,64,1536]{2,1,0:T(8,128)(2,1)S(1)} %all_to_all.21.d_ref), custom_call_target="tpu_custom_call" | custom-call | flops 603979776 | tf_op jit(solution)/shard_map/pallas_call | solution.py:189
  127.0 0.0 collective-permute-done.4
  127.0 0.6 add_convert_fusion
  (2 shorter events, 0.0 us)
Async XLA Ops:
  0.6 1.0 copy-start.4
  20.3 5.1 %collective-permute-start = (bf16[16,16,384]{2,1,0:T(8,128)(2,1)S(1)}, bf16[16,16,384]{2,1,0:T(8,128)(2,1)S(1)}, u32[]{:S(2)}, u32[]{:S(2)}) collective-permute-start(bf16[16,16,384]{2,1,0:T(8,128)(2,1)S(1)} %all_to_all.20.mine_ref), channel_id=1, source_target_pairs={{0,1},{1,0},{2,3},{3,2},{4,5},{5,4},{6,7},{7,6},{8,9},{9,8},{10,11... | collective-permute-start | bytes 589832 | tf_op jit(solution)/shard_map/ppermute | solution.py:156
  25.4 1.1 copy-start
  26.4 1.1 copy-start.2
  29.7 24.1 %all-to-all-start.1 = ((bf16[8,64,1536]{2,1,0:T(8,128)(2,1)}), bf16[8,64,1536]{2,1,0:T(8,128)(2,1)S(1)}, u32[]{:S(2)}, u32[]{:S(2)}) async-start(bf16[8,64,1536]{2,1,0:T(8,128)(2,1)} %shard_map.68), calls=%async_computation.1 | async-start | bytes 3145728 | tf_op jit(solution)/shard_map/all_to_all | solution.py:153
  33.3 28.0 %copy-start.5 = (bf16[32,768]{1,0:T(8,128)(2,1)S(1)}, bf16[32,768]{1,0:T(8,128)(2,1)}, u32[]{:S(2)}) copy-start(bf16[32,768]{1,0:T(8,128)(2,1)} %cot_ref.1) | copy-start | bytes 147460
  54.0 7.3 %collective-permute-start.1 = (bf16[32,1536]{1,0:T(8,128)(2,1)S(1)}, bf16[32,1536]{1,0:T(8,128)(2,1)S(1)}, u32[]{:S(2)}, u32[]{:S(2)}) collective-permute-start(bf16[32,1536]{1,0:T(8,128)(2,1)S(1)} %get-tuple-element.10), channel_id=1, source_target_pairs={{0,256},{32,288},{64,320},{96,352},{128,384},{160,416},{192,448},{... | collective-permute-start | bytes 294920 | tf_op jit(solution)/shard_map/ppermute | solution.py:156
  61.4 6.3 %collective-permute-start.2 = (bf16[32,1536]{1,0:T(8,128)(2,1)S(1)}, bf16[32,1536]{1,0:T(8,128)(2,1)S(1)}, u32[]{:S(2)}, u32[]{:S(2)}) collective-permute-start(bf16[32,1536]{1,0:T(8,128)(2,1)S(1)} %shard_map.70.mine_ref), channel_id=1, source_target_pairs={{0,256},{32,288},{64,320},{96,352},{128,384},{160,416},{192,448},{... | collective-permute-start | bytes 294920 | tf_op jit(solution)/shard_map/ppermute | solution.py:156
  67.7 25.6 %copy-start.1 = (bf16[384,768]{1,0:T(8,128)(2,1)S(1)}, bf16[384,768]{1,0:T(8,128)(2,1)}, u32[]{:S(2)}) copy-start(bf16[384,768]{1,0:T(8,128)(2,1)} %gate_ref.5) | copy-start | bytes 1769476
  67.8 25.6 %copy-start.3 = (bf16[384,768]{1,0:T(8,128)(2,1)S(1)}, bf16[384,768]{1,0:T(8,128)(2,1)}, u32[]{:S(2)}) copy-start(bf16[384,768]{1,0:T(8,128)(2,1)} %up_ref.5) | copy-start | bytes 1769476
  93.9 5.9 %collective-permute-start.3 = (f32[256,384]{1,0:T(8,128)S(1)}, f32[256,384]{1,0:T(8,128)S(1)}, u32[]{:S(2)}, u32[]{:S(2)}) collective-permute-start(f32[256,384]{1,0:T(8,128)S(1)} %shard_map.72), channel_id=1, source_target_pairs={{0,1},{1,0},{2,3},{3,2},{4,5},{5,4},{6,7},{7,6},{8,9},{9,8},{10,11... | collective-permute-start | bytes 1179656 | tf_op jit(solution)/shard_map/ppermute | solution.py:156
  101.1 16.3 %all-to-all-start.3 = ((bf16[8,32,384]{2,1,0:T(8,128)(2,1)}), bf16[8,32,384]{2,1,0:T(8,128)(2,1)S(1)}, u32[]{:S(2)}, u32[]{:S(2)}) async-start(bf16[8,32,384]{2,1,0:T(8,128)(2,1)} %shard_map.73), calls=%async_computation.3 | async-start | bytes 393216 | tf_op jit(solution)/shard_map/all_to_all | solution.py:153
  117.4 9.6 %collective-permute-start.4 = (f32[16,384]{1,0:T(8,128)S(1)}, f32[16,384]{1,0:T(8,128)S(1)}, u32[]{:S(2)}, u32[]{:S(2)}) collective-permute-start(f32[16,384]{1,0:T(8,128)S(1)} %get-tuple-element.12), channel_id=1, source_target_pairs={{0,2},{1,3},{2,0},{3,1},{4,6},{5,7},{6,4},{7,5},{8,10},{9,11},{10,... | collective-permute-start | bytes 73736 | tf_op jit(solution)/shard_map/ppermute | solution.py:156

commit v3 on v2

v3 whole, which is shorter than its diff:
```python
import functools

import jax
import jax.numpy as jnp
from jax import lax
from jax.experimental import pallas as pl
from jax.experimental.pallas import tpu as pltpu
from jax.sharding import PartitionSpec as P

GROUP = 8
VMEM_BYTES = 40 * 1024 * 1024

VMEM = pl.BlockSpec(memory_space=pltpu.VMEM)
SMEM = pl.BlockSpec(memory_space=pltpu.SMEM)
BF16, F32 = jnp.bfloat16, jnp.float32


def rows_at(start, size):
    return pl.ds(pl.multiple_of(start * size, size), size)


def lay_kernel(half_ref, tokens_ref, out_ref):
    rows, part, depth = out_ref.shape
    at = rows_at(half_ref[0], part)
    for row in range(rows):
        out_ref[row] = tokens_ref[at, row * depth : (row + 1) * depth]


def forward_kernel(tokens_ref, gate_ref, up_ref, out_ref):
    rows, part, depth = tokens_ref.shape
    hidden = gate_ref.shape[1]
    tokens = tokens_ref[...].reshape(rows * part, depth)
    for i, weight_ref in enumerate((gate_ref, up_ref)):
        total = jnp.dot(tokens, weight_ref[...], preferred_element_type=F32).astype(BF16)
        for row in range(rows):
            side, m = divmod(row, GROUP)
            out_ref[m, side * part : (side + 1) * part, i * hidden : (i + 1) * hidden] = total[
                row * part : (row + 1) * part
            ]


def sum_kernel(parts_ref, keep_ref, send_ref):
    total = parts_ref[0].astype(F32)
    for part in range(1, parts_ref.shape[0]):
        total += parts_ref[part].astype(F32)
    keep_ref[...] = total
    send_ref[...] = total.astype(BF16)


def act_kernel(where_ref, keep_ref, came_ref, cot_ref, far_cot_ref, out_ref):
    part = keep_ref.shape[0] // 2
    hidden = cot_ref.shape[1]
    half = rows_at(where_ref[1], part)
    for side, ref in ((where_ref[0], cot_ref), (1 - where_ref[0], far_cot_ref)):
        at = rows_at(side, part)
        cot = ref[half, :].astype(F32)
        total = keep_ref[at, :] + came_ref[at, :].astype(F32)
        gate, up = total[:, :hidden], total[:, hidden:]
        sig = 1.0 / (1.0 + jnp.exp(-gate))
        d_gate = (cot * up * sig * (1.0 + gate * (1.0 - sig))).astype(BF16)
        d_up = (cot * gate * sig).astype(BF16)
        for m in range(out_ref.shape[0]):
            out_ref[m, at, :hidden] = d_gate
            out_ref[m, at, hidden:] = d_up


def by_row(d_ref):
    part = d_ref.shape[1] // 2
    return jnp.concatenate(
        [
            d_ref[m, side * part : (side + 1) * part, :]
            for side in range(2)
            for m in range(GROUP)
        ],
        axis=0,
    )


def over_hidden(left, right):
    return lax.dot_general(left, right, (((1,), (1,)), ((), ())), preferred_element_type=F32)


def over_tokens(left, right):
    return lax.dot_general(left, right, (((0,), (0,)), ((), ())), preferred_element_type=F32)


def term_of(d_ref, gate_ref, up_ref):
    hidden = gate_ref.shape[1]
    d = by_row(d_ref)
    return over_hidden(d[:, :hidden], gate_ref[...]) + over_hidden(d[:, hidden:], up_ref[...])


def far_term_kernel(d_ref, gate_ref, up_ref, out_ref):
    out_ref[...] = term_of(d_ref, gate_ref, up_ref)


def near_term_kernel(d_ref, gate_ref, up_ref, came_ref, out_ref):
    total = term_of(d_ref, gate_ref, up_ref) + came_ref[...]
    out_ref[...] = total.astype(BF16).reshape(out_ref.shape)


def weight_grad_kernel(far_ref, near_ref, d_far_ref, d_near_ref, gate_ref, up_ref):
    rows, part, depth = far_ref.shape
    hidden = gate_ref.shape[1]
    far = far_ref[...].reshape(rows * part, depth)
    near = near_ref[...].reshape(rows * part, depth)
    d_far, d_near = by_row(d_far_ref), by_row(d_near_ref)
    for i, ref in enumerate((gate_ref, up_ref)):
        span = slice(i * hidden, (i + 1) * hidden)
        total = over_tokens(far, d_far[:, span]) + over_tokens(near, d_near[:, span])
        ref[...] = total.astype(BF16)


def call(kernel, outs, n_where, n_in, flops=0, nbytes=0):
    return pl.pallas_call(
        kernel,
        out_shape=outs,
        in_specs=[SMEM] * n_where + [VMEM] * n_in,
        out_specs=jax.tree.map(lambda _: VMEM, outs),
        compiler_params=pltpu.CompilerParams(vmem_limit_bytes=VMEM_BYTES),
        cost_estimate=pl.CostEstimate(flops=flops, bytes_accessed=nbytes, transcendentals=0),
    )


def shards(rows, cols, inputs, cotangent, gate_weight, up_weight):
    depth, hidden = gate_weight.shape
    part = inputs.shape[0] // 2
    wide = 2 * hidden
    flops = 2 * rows * part * depth * wide
    pairs = [list(range(0, GROUP)), list(range(GROUP, 2 * GROUP))]
    core_groups = [[2 * i + core for i in range(cols // 2)] for core in range(2)]
    row, col = lax.axis_index("row"), lax.axis_index("col")

    def scalar(value):
        return value.astype(jnp.int32).reshape(1)

    side = scalar(row // GROUP)
    halves = {"far": scalar(1 - col % 2), "near": scalar(col % 2)}

    def shape(dims, dtype=BF16):
        return jax.ShapeDtypeStruct(dims, dtype)

    def exchange(array, axis, groups=None):
        return lax.all_to_all(array, axis, 0, 0, axis_index_groups=groups)

    def swap(array, axis, count, bit):
        return lax.ppermute(array, axis, [(i, i ^ bit) for i in range(count)])

    sent = call(lay_kernel, shape((rows, part, depth)), 1, 1)(halves["far"], inputs)
    tokens = {"far": exchange(sent, "row")}
    tokens["near"] = swap(tokens["far"], "col", cols, 1)

    far_cot = swap(cotangent, "row", rows, GROUP)
    d = {}
    for half in ("far", "near"):
        partial = call(forward_kernel, shape((GROUP, 2 * part, wide)), 0, 3, flops)(
            tokens[half], gate_weight, up_weight
        )
        parts = exchange(partial, "row", pairs)
        keep, send = call(
            sum_kernel, [shape((2 * part, wide), F32), shape((2 * part, wide))], 0, 1
        )(parts)
        came = swap(send, "row", rows, GROUP)
        copies = call(act_kernel, shape((GROUP, 2 * part, wide)), 1, 4)(
            jnp.concatenate([side, halves[half]]), keep, came, cotangent, far_cot
        )
        d[half] = exchange(copies, "row", pairs)

    far_term = call(far_term_kernel, shape((rows * part, depth), F32), 0, 3, flops)(
        d["far"], gate_weight, up_weight
    )
    came = swap(far_term, "col", cols, 1)
    term = call(near_term_kernel, shape((rows, part, depth)), 0, 4, flops)(
        d["near"], gate_weight, up_weight, came
    )
    over_col = exchange(term, "col", core_groups)
    input_grad = jnp.sum(over_col.astype(F32), axis=0).astype(BF16)

    grad = shape((depth, hidden))
    gate_grad, up_grad = call(weight_grad_kernel, [grad, grad], 0, 4, 2 * flops)(
        tokens["far"], tokens["near"], d["far"], d["near"]
    )
    return (input_grad, gate_grad, up_grad)


def solution(mesh):
    in_specs = (P("row", None), P("row", "col"), P("row", "col"), P("row", "col"))
    out_specs = (P("col", "row"), P("row", "col"), P("row", "col"))
    local = functools.partial(shards, mesh.shape["row"], mesh.shape["col"])
    return jax.shard_map(local, mesh=mesh, in_specs=in_specs, out_specs=out_specs, check_vma=False)
```

time: 128 us -> 119 us (0.930)
  the two profiles are of different devices: /device:TPU:1 before, /device:TPU:2 now
where the time goes in v3:
time: 119 us; the launch traced here: 118 us
  starting transfers between devices  49.2 us (41%)
  waiting for transfers between devices  36.2 us (30%)
  blocking collectives  18.3 us (15%)
  Pallas kernels  10.5 us (9%)
  local copies, waits for them, and re-layouts  2.12 us (2%)
    all_to_all x5, starting transfers between devices, exchange(): return lax.all_to_all(array, axis, 0, 0, axis_index_groups=groups)  35.9 us
    all_to_all x5, waiting for transfers between devices, exchange(): return lax.all_to_all(array, axis, 0, 0, axis_index_groups=groups)  23.3 us
    all_to_all x1, blocking collectives, exchange(): return lax.all_to_all(array, axis, 0, 0, axis_index_groups=groups)  18.3 us
    ppermute x5, starting transfers between devices, swap(): return lax.ppermute(array, axis, [(i, i ^ bit) for i in range(count)])  13.2 us
    ppermute x5, waiting for transfers between devices, swap(): return lax.ppermute(array, axis, [(i, i ^ bit) for i in range(count)])  12.9 us
    pallas_call x2, Pallas kernels, shards(): call(act_kernel, shape((GROUP, 2 * part, wide)), 1, 4)  3.12 us
    pallas_call x2, Pallas kernels, shards(): call(forward_kernel, shape((GROUP, 2 * part, wide)), 0, 3, flops)  2.95 us
  transfers between devices with their start and end apart: 10, of which 8 were waited for; matrix products, arithmetic and copies ran while one was open for 0% of the time, Pallas kernels for 7%

profile of v3, /device:TPU:2, one launch (start us, length us, event | category | flops | bytes accessed | tf_op | source)
XLA Modules:
  0.0 117.8 jit_solution(1030230333642200636)
XLA Ops:
  0.6 0.0 copy-start
  0.7 0.0 copy-start.3
  0.7 1.0 copy-done.3
  1.7 18.3 %all_to_all.30.tokens_ref.far_ref = bf16[16,16,384]{2,1,0:T(8,128)(2,1)S(1)} all-to-all(bf16[16,16,384]{2,1,0:T(8,128)(2,1)S(1)} %shard_map.67), channel_id=1, replica_groups=mesh['row'=16,'col'=32] {'row'}, dimensions={0} | all-to-all | bytes 393216 | tf_op jit(solution)/shard_map/all_to_all | solution.py:144
  20.1 0.0 copy-done
  20.1 0.0 copy-start.1
  20.1 1.1 copy-done.1
  21.1 1.5 %shard_map.71 = bf16[8,32,1536]{2,1,0:T(8,128)(2,1)} custom-call(bf16[16,16,384]{2,1,0:T(8,128)(2,1)S(1)} %all_to_all.30.tokens_ref.far_ref, bf16[384,768]{1,0:T(8,128)(2,1)S(1)} %copy-done, bf16[384,768]{1,0:T(8,128)(2,1)S(1)} %copy-done.1), custom_call_target="tpu_custom_call" | custom-call | flops 301989888 | tf_op jit(solution)/shard_map/pallas_call | solution.py:156
  22.6 0.0 copy-start.2
  22.6 5.0 %all-to-all-start.3 = ((bf16[8,32,1536]{2,1,0:T(8,128)(2,1)}), bf16[8,32,1536]{2,1,0:T(8,128)(2,1)S(1)}, u32[]{:S(2)}, u32[]{:S(2)}) async-start(bf16[8,32,1536]{2,1,0:T(8,128)(2,1)} %shard_map.71), calls=%async_computation.3 | async-start | bytes 1572864 | tf_op jit(solution)/shard_map/all_to_all | solution.py:144
  27.7 1.9 %collective-permute-start = (bf16[16,16,384]{2,1,0:T(8,128)(2,1)S(1)}, bf16[16,16,384]{2,1,0:T(8,128)(2,1)S(1)}, u32[]{:S(2)}, u32[]{:S(2)}) collective-permute-start(bf16[16,16,384]{2,1,0:T(8,128)(2,1)S(1)} %all_to_all.30.tokens_ref.far_ref), channel_id=1, source_target_pairs={{0,1},{1,0},{2,3},{3,2},{4,5},{5,4},{6,7},{7,6},{8,9},{9,8},{10,11... | collective-permute-start | bytes 589832 | tf_op jit(solution)/shard_map/ppermute | solution.py:147
  29.6 1.4 %collective-permute-done.tokens_ref.near_ref = bf16[16,16,384]{2,1,0:T(8,128)(2,1)S(1)} collective-permute-done((bf16[16,16,384]{2,1,0:T(8,128)(2,1)S(1)}, bf16[16,16,384]{2,1,0:T(8,128)(2,1)S(1)}, u32[]{:S(2)}, u32[]{:S(2)}) %collective-permute-start) | collective-permute-done | bytes 196640 | tf_op jit(solution)/shard_map/ppermute | solution.py:147
  31.0 0.0 copy-done.2
  31.0 1.5 %shard_map.68 = bf16[8,32,1536]{2,1,0:T(8,128)(2,1)} custom-call(bf16[16,16,384]{2,1,0:T(8,128)(2,1)S(1)} %collective-permute-done.tokens_ref.near_ref, bf16[384,768]{1,0:T(8,128)(2,1)S(1)} %copy-done, bf16[384,768]{1,0:T(8,128)(2,1)S(1)} %copy-done.2), custom_call_target="tpu_custom_call" | custom-call | flops 301989888 | tf_op jit(solution)/shard_map/pallas_call | solution.py:156
  32.4 0.0 copy-start.4
  32.4 4.9 %all-to-all-done.3.parts_ref = bf16[8,32,1536]{2,1,0:T(8,128)(2,1)S(1)} async-done(((bf16[8,32,1536]{2,1,0:T(8,128)(2,1)}), bf16[8,32,1536]{2,1,0:T(8,128)(2,1)S(1)}, u32[]{:S(2)}, u32[]{:S(2)}) %all-to-all-start.3) | async-done | bytes 786464 | tf_op jit(solution)/shard_map/all_to_all | solution.py:144
  37.3 4.9 %all-to-all-start.1 = ((bf16[8,32,1536]{2,1,0:T(8,128)(2,1)}), bf16[8,32,1536]{2,1,0:T(8,128)(2,1)S(1)}, u32[]{:S(2)}, u32[]{:S(2)}) async-start(bf16[8,32,1536]{2,1,0:T(8,128)(2,1)} %shard_map.68), calls=%async_computation.1 | async-start | bytes 1572864 | tf_op jit(solution)/shard_map/all_to_all | solution.py:144
  42.2 0.0 copy-done.4
  42.2 3.5 %collective-permute-start.2 = (bf16[32,768]{1,0:T(8,128)(2,1)S(1)}, bf16[32,768]{1,0:T(8,128)(2,1)S(1)}, u32[]{:S(2)}, u32[]{:S(2)}) collective-permute-start(bf16[32,768]{1,0:T(8,128)(2,1)S(1)} %copy-done.4), channel_id=1, source_target_pairs={{0,256},{32,288},{64,320},{96,352},{128,384},{160,416},{192,448},{... | collective-permute-start | bytes 147464 | tf_op jit(solution)/shard_map/ppermute | solution.py:147
  45.7 0.1 shard_map.72
  45.8 3.3 %collective-permute-start.3 = (bf16[32,1536]{1,0:T(8,128)(2,1)S(1)}, bf16[32,1536]{1,0:T(8,128)(2,1)S(1)}, u32[]{:S(2)}, u32[]{:S(2)}) collective-permute-start(bf16[32,1536]{1,0:T(8,128)(2,1)S(1)} %get-tuple-element.12), channel_id=1, source_target_pairs={{0,256},{32,288},{64,320},{96,352},{128,384},{160,416},{192,448},{... | collective-permute-start | bytes 294920 | tf_op jit(solution)/shard_map/ppermute | solution.py:147
  49.1 0.1 pad_add_fusion.1.where_ref
  49.2 3.0 %collective-permute-done.2.far_cot_ref = bf16[32,768]{1,0:T(8,128)(2,1)S(1)} collective-permute-done((bf16[32,768]{1,0:T(8,128)(2,1)S(1)}, bf16[32,768]{1,0:T(8,128)(2,1)S(1)}, u32[]{:S(2)}, u32[]{:S(2)}) %collective-permute-start.2) | collective-permute-done | bytes 49184 | tf_op jit(solution)/shard_map/ppermute | solution.py:147
  52.2 1.8 %collective-permute-done.3.came_ref = bf16[32,1536]{1,0:T(8,128)(2,1)S(1)} collective-permute-done((bf16[32,1536]{1,0:T(8,128)(2,1)S(1)}, bf16[32,1536]{1,0:T(8,128)(2,1)S(1)}, u32[]{:S(2)}, u32[]{:S(2)}) %collective-permute-start.3) | collective-permute-done | bytes 98336 | tf_op jit(solution)/shard_map/ppermute | solution.py:147
  54.0 1.6 %shard_map.73 = bf16[8,32,1536]{2,1,0:T(8,128)(2,1)} custom-call(s32[2]{0:T(128)S(1)} %pad_add_fusion.1.where_ref, f32[32,1536]{1,0:T(8,128)S(1)} %get-tuple-element.11.keep_ref, bf16[32,1536]{1,0:T(8,128)(2,1)S(1)} %collective-permute-done.3.came_ref, bf16[32,768]{1,0:T(8,128)(2,1)S(1)} %copy-done.4, bf16[32,768]{1,0:T(8,128)(2,1)S(1)} %collective-permute-done.2.far_cot_ref), custom_call_target="tpu_custom_call" | custom-call | tf_op jit(solution)/shard_map/pallas_call | solution.py:164
  55.6 0.0 all-to-all-done.1.parts_ref
  55.6 7.6 %all-to-all-start.4 = ((bf16[8,32,1536]{2,1,0:T(8,128)(2,1)}), bf16[8,32,1536]{2,1,0:T(8,128)(2,1)S(1)}, u32[]{:S(2)}, u32[]{:S(2)}) async-start(bf16[8,32,1536]{2,1,0:T(8,128)(2,1)} %shard_map.73), calls=%async_computation.4 | async-start | bytes 1572864 | tf_op jit(solution)/shard_map/all_to_all | solution.py:144
  63.2 0.1 shard_map.69
  63.4 2.7 %collective-permute-start.1 = (bf16[32,1536]{1,0:T(8,128)(2,1)S(1)}, bf16[32,1536]{1,0:T(8,128)(2,1)S(1)}, u32[]{:S(2)}, u32[]{:S(2)}) collective-permute-start(bf16[32,1536]{1,0:T(8,128)(2,1)S(1)} %get-tuple-element.10), channel_id=1, source_target_pairs={{0,256},{32,288},{64,320},{96,352},{128,384},{160,416},{192,448},{... | collective-permute-start | bytes 294920 | tf_op jit(solution)/shard_map/ppermute | solution.py:147
  66.0 0.1 pad_add_fusion.where_ref
  66.1 6.6 %collective-permute-done.1.came_ref = bf16[32,1536]{1,0:T(8,128)(2,1)S(1)} collective-permute-done((bf16[32,1536]{1,0:T(8,128)(2,1)S(1)}, bf16[32,1536]{1,0:T(8,128)(2,1)S(1)}, u32[]{:S(2)}, u32[]{:S(2)}) %collective-permute-start.1) | collective-permute-done | bytes 98336 | tf_op jit(solution)/shard_map/ppermute | solution.py:147
  72.8 1.5 %shard_map.70 = bf16[8,32,1536]{2,1,0:T(8,128)(2,1)} custom-call(s32[2]{0:T(128)S(1)} %pad_add_fusion.where_ref, f32[32,1536]{1,0:T(8,128)S(1)} %get-tuple-element.9.keep_ref, bf16[32,1536]{1,0:T(8,128)(2,1)S(1)} %collective-permute-done.1.came_ref, bf16[32,768]{1,0:T(8,128)(2,1)S(1)} %copy-done.4, bf16[32,768]{1,0:T(8,128)(2,1)S(1)} %collective-permute-done.2.far_cot_ref), custom_call_target="tpu_custom_call" | custom-call | tf_op jit(solution)/shard_map/pallas_call | solution.py:164
  74.3 0.4 all-to-all-done.4.d_ref.d_far_ref
  74.7 5.4 %all-to-all-start.2 = ((bf16[8,32,1536]{2,1,0:T(8,128)(2,1)}), bf16[8,32,1536]{2,1,0:T(8,128)(2,1)S(1)}, u32[]{:S(2)}, u32[]{:S(2)}) async-start(bf16[8,32,1536]{2,1,0:T(8,128)(2,1)} %shard_map.70), calls=%async_computation.2 | async-start | bytes 1572864 | tf_op jit(solution)/shard_map/all_to_all | solution.py:144
  80.1 1.3 %shard_map.74 = f32[256,384]{1,0:T(8,128)} custom-call(bf16[8,32,1536]{2,1,0:T(8,128)(2,1)S(1)} %all-to-all-done.4.d_ref.d_far_ref, bf16[384,768]{1,0:T(8,128)(2,1)S(1)} %copy-done, bf16[384,768]{1,0:T(8,128)(2,1)S(1)} %copy-done.2), custom_call_target="tpu_custom_call" | custom-call | flops 301989888 | tf_op jit(solution)/shard_map/pallas_call | solution.py:169
  81.4 1.9 %collective-permute-start.4 = (f32[256,384]{1,0:T(8,128)}, f32[256,384]{1,0:T(8,128)S(1)}, u32[]{:S(2)}, u32[]{:S(2)}) collective-permute-start(f32[256,384]{1,0:T(8,128)} %shard_map.74), channel_id=1, source_target_pairs={{0,1},{1,0},{2,3},{3,2},{4,5},{5,4},{6,7},{7,6},{8,9},{9,8},{10,11... | collective-permute-start | bytes 1179656 | tf_op jit(solution)/shard_map/ppermute | solution.py:147
  83.3 5.5 %all-to-all-done.2.d_ref.d_near_ref = bf16[8,32,1536]{2,1,0:T(8,128)(2,1)S(1)} async-done(((bf16[8,32,1536]{2,1,0:T(8,128)(2,1)}), bf16[8,32,1536]{2,1,0:T(8,128)(2,1)S(1)}, u32[]{:S(2)}, u32[]{:S(2)}) %all-to-all-start.2) | async-done | bytes 786464 | tf_op jit(solution)/shard_map/all_to_all | solution.py:144
  88.8 0.0 collective-permute-done.4.came_ref
  88.8 1.3 %shard_map.75 = bf16[16,16,384]{2,1,0:T(8,128)(2,1)} custom-call(bf16[8,32,1536]{2,1,0:T(8,128)(2,1)S(1)} %all-to-all-done.2.d_ref.d_near_ref, bf16[384,768]{1,0:T(8,128)(2,1)S(1)} %copy-done, bf16[384,768]{1,0:T(8,128)(2,1)S(1)} %copy-done.2, f32[256,384]{1,0:T(8,128)S(1)} %collective-permute-done.4.came_ref), custom_call_target="tpu_custom_call" | custom-call | flops 301989888 | tf_op jit(solution)/shard_map/pallas_call | solution.py:173
  90.0 12.9 %all-to-all-start.5 = ((bf16[16,16,384]{2,1,0:T(8,128)(2,1)}), bf16[16,16,384]{2,1,0:T(8,128)(2,1)S(1)}, u32[]{:S(2)}, u32[]{:S(2)}) async-start(bf16[16,16,384]{2,1,0:T(8,128)(2,1)} %shard_map.75), calls=%async_computation.5 | async-start | bytes 393216 | tf_op jit(solution)/shard_map/all_to_all | solution.py:144
  103.0 1.6 %shard_map.76 = (bf16[384,768]{1,0:T(8,128)(2,1)}, bf16[384,768]{1,0:T(8,128)(2,1)}) custom-call(bf16[16,16,384]{2,1,0:T(8,128)(2,1)S(1)} %all_to_all.30.tokens_ref.far_ref, bf16[16,16,384]{2,1,0:T(8,128)(2,1)S(1)} %collective-permute-done.tokens_ref.near_ref, bf16[8,32,1536]{2,1,0:T(8,128)(2,1)S(1)} %all-to-all-done.4.d_ref.d_far_ref, ...), custom_call_target="tpu_custom_call" | custom-call | flops 603979776 | tf_op jit(solution)/shard_map/pallas_call | solution.py:180
  104.6 12.6 %all-to-all-done.5 = bf16[16,16,384]{2,1,0:T(8,128)(2,1)S(1)} async-done(((bf16[16,16,384]{2,1,0:T(8,128)(2,1)}), bf16[16,16,384]{2,1,0:T(8,128)(2,1)S(1)}, u32[]{:S(2)}, u32[]{:S(2)}) %all-to-all-start.5) | async-done | bytes 196640 | tf_op jit(solution)/shard_map/all_to_all | solution.py:144
  117.2 0.6 reduce_sum.12
  (1 shorter events, 0.0 us)
Async XLA Ops:
  0.6 19.4 %copy-start = (bf16[384,768]{1,0:T(8,128)(2,1)S(1)}, bf16[384,768]{1,0:T(8,128)(2,1)}, u32[]{:S(2)}) copy-start(bf16[384,768]{1,0:T(8,128)(2,1)} %gate_ref.7) | copy-start | bytes 1769476
  0.7 1.1 copy-start.3
  20.1 1.1 copy-start.1
  22.6 8.4 %copy-start.2 = (bf16[384,768]{1,0:T(8,128)(2,1)S(1)}, bf16[384,768]{1,0:T(8,128)(2,1)}, u32[]{:S(2)}) copy-start(bf16[384,768]{1,0:T(8,128)(2,1)} %up_ref.7) | copy-start | bytes 1769476
  22.6 14.7 %all-to-all-start.3 = ((bf16[8,32,1536]{2,1,0:T(8,128)(2,1)}), bf16[8,32,1536]{2,1,0:T(8,128)(2,1)S(1)}, u32[]{:S(2)}, u32[]{:S(2)}) async-start(bf16[8,32,1536]{2,1,0:T(8,128)(2,1)} %shard_map.71), calls=%async_computation.3 | async-start | bytes 1572864 | tf_op jit(solution)/shard_map/all_to_all | solution.py:144
  27.7 3.3 %collective-permute-start = (bf16[16,16,384]{2,1,0:T(8,128)(2,1)S(1)}, bf16[16,16,384]{2,1,0:T(8,128)(2,1)S(1)}, u32[]{:S(2)}, u32[]{:S(2)}) collective-permute-start(bf16[16,16,384]{2,1,0:T(8,128)(2,1)S(1)} %all_to_all.30.tokens_ref.far_ref), channel_id=1, source_target_pairs={{0,1},{1,0},{2,3},{3,2},{4,5},{5,4},{6,7},{7,6},{8,9},{9,8},{10,11... | collective-permute-start | bytes 589832 | tf_op jit(solution)/shard_map/ppermute | solution.py:147
  32.4 9.8 %copy-start.4 = (bf16[32,768]{1,0:T(8,128)(2,1)S(1)}, bf16[32,768]{1,0:T(8,128)(2,1)}, u32[]{:S(2)}) copy-start(bf16[32,768]{1,0:T(8,128)(2,1)} %cot_ref.3) | copy-start | bytes 147460
  37.3 18.3 %all-to-all-start.1 = ((bf16[8,32,1536]{2,1,0:T(8,128)(2,1)}), bf16[8,32,1536]{2,1,0:T(8,128)(2,1)S(1)}, u32[]{:S(2)}, u32[]{:S(2)}) async-start(bf16[8,32,1536]{2,1,0:T(8,128)(2,1)} %shard_map.68), calls=%async_computation.1 | async-start | bytes 1572864 | tf_op jit(solution)/shard_map/all_to_all | solution.py:144
  42.2 10.0 %collective-permute-start.2 = (bf16[32,768]{1,0:T(8,128)(2,1)S(1)}, bf16[32,768]{1,0:T(8,128)(2,1)S(1)}, u32[]{:S(2)}, u32[]{:S(2)}) collective-permute-start(bf16[32,768]{1,0:T(8,128)(2,1)S(1)} %copy-done.4), channel_id=1, source_target_pairs={{0,256},{32,288},{64,320},{96,352},{128,384},{160,416},{192,448},{... | collective-permute-start | bytes 147464 | tf_op jit(solution)/shard_map/ppermute | solution.py:147
  45.8 8.2 %collective-permute-start.3 = (bf16[32,1536]{1,0:T(8,128)(2,1)S(1)}, bf16[32,1536]{1,0:T(8,128)(2,1)S(1)}, u32[]{:S(2)}, u32[]{:S(2)}) collective-permute-start(bf16[32,1536]{1,0:T(8,128)(2,1)S(1)} %get-tuple-element.12), channel_id=1, source_target_pairs={{0,256},{32,288},{64,320},{96,352},{128,384},{160,416},{192,448},{... | collective-permute-start | bytes 294920 | tf_op jit(solution)/shard_map/ppermute | solution.py:147
  55.6 19.1 %all-to-all-start.4 = ((bf16[8,32,1536]{2,1,0:T(8,128)(2,1)}), bf16[8,32,1536]{2,1,0:T(8,128)(2,1)S(1)}, u32[]{:S(2)}, u32[]{:S(2)}) async-start(bf16[8,32,1536]{2,1,0:T(8,128)(2,1)} %shard_map.73), calls=%async_computation.4 | async-start | bytes 1572864 | tf_op jit(solution)/shard_map/all_to_all | solution.py:144
  63.4 9.4 %collective-permute-start.1 = (bf16[32,1536]{1,0:T(8,128)(2,1)S(1)}, bf16[32,1536]{1,0:T(8,128)(2,1)S(1)}, u32[]{:S(2)}, u32[]{:S(2)}) collective-permute-start(bf16[32,1536]{1,0:T(8,128)(2,1)S(1)} %get-tuple-element.10), channel_id=1, source_target_pairs={{0,256},{32,288},{64,320},{96,352},{128,384},{160,416},{192,448},{... | collective-permute-start | bytes 294920 | tf_op jit(solution)/shard_map/ppermute | solution.py:147
  74.7 14.1 %all-to-all-start.2 = ((bf16[8,32,1536]{2,1,0:T(8,128)(2,1)}), bf16[8,32,1536]{2,1,0:T(8,128)(2,1)S(1)}, u32[]{:S(2)}, u32[]{:S(2)}) async-start(bf16[8,32,1536]{2,1,0:T(8,128)(2,1)} %shard_map.70), calls=%async_computation.2 | async-start | bytes 1572864 | tf_op jit(solution)/shard_map/all_to_all | solution.py:144
  81.4 7.4 %collective-permute-start.4 = (f32[256,384]{1,0:T(8,128)}, f32[256,384]{1,0:T(8,128)S(1)}, u32[]{:S(2)}, u32[]{:S(2)}) collective-permute-start(f32[256,384]{1,0:T(8,128)} %shard_map.74), channel_id=1, source_target_pairs={{0,1},{1,0},{2,3},{3,2},{4,5},{5,4},{6,7},{7,6},{8,9},{9,8},{10,11... | collective-permute-start | bytes 1179656 | tf_op jit(solution)/shard_map/ppermute | solution.py:147
  90.0 27.2 %all-to-all-start.5 = ((bf16[16,16,384]{2,1,0:T(8,128)(2,1)}), bf16[16,16,384]{2,1,0:T(8,128)(2,1)S(1)}, u32[]{:S(2)}, u32[]{:S(2)}) async-start(bf16[16,16,384]{2,1,0:T(8,128)(2,1)} %shard_map.75), calls=%async_computation.5 | async-start | bytes 393216 | tf_op jit(solution)/shard_map/all_to_all | solution.py:144

commit v4 on v3

--- a/solution.py
+++ b/solution.py
@@ -12,6 +12,7 @@
 
 VMEM = pl.BlockSpec(memory_space=pltpu.VMEM)
 SMEM = pl.BlockSpec(memory_space=pltpu.SMEM)
+ANY = pl.BlockSpec(memory_space=pl.ANY)
 BF16, F32 = jnp.bfloat16, jnp.float32
 
 
@@ -26,7 +27,12 @@
         out_ref[row] = tokens_ref[at, row * depth : (row + 1) * depth]
 
 
-def forward_kernel(tokens_ref, gate_ref, up_ref, out_ref):
+def stage_kernel(gate_ref, up_ref, gate_out_ref, up_out_ref):
+    gate_out_ref[...] = gate_ref[...]
+    up_out_ref[...] = up_ref[...]
+
+
+def forward_kernel(tokens_ref, gate_ref, up_ref, _, out_ref):
     rows, part, depth = tokens_ref.shape
     hidden = gate_ref.shape[1]
     tokens = tokens_ref[...].reshape(rows * part, depth)
@@ -111,11 +117,11 @@
         ref[...] = total.astype(BF16)
 
 
-def call(kernel, outs, n_where, n_in, flops=0, nbytes=0):
+def call(kernel, outs, n_where, n_in, flops=0, nbytes=0, n_any=0):
     return pl.pallas_call(
         kernel,
         out_shape=outs,
-        in_specs=[SMEM] * n_where + [VMEM] * n_in,
+        in_specs=[SMEM] * n_where + [VMEM] * n_in + [ANY] * n_any,
         out_specs=jax.tree.map(lambda _: VMEM, outs),
         compiler_params=pltpu.CompilerParams(vmem_limit_bytes=VMEM_BYTES),
         cost_estimate=pl.CostEstimate(flops=flops, bytes_accessed=nbytes, transcendentals=0),
@@ -150,11 +156,15 @@
     tokens = {"far": exchange(sent, "row")}
     tokens["near"] = swap(tokens["far"], "col", cols, 1)
 
+    grad = shape((depth, hidden))
+    gate, up = call(stage_kernel, [grad, grad], 0, 2, nbytes=8 * depth * hidden)(
+        gate_weight, up_weight
+    )
     far_cot = swap(cotangent, "row", rows, GROUP)
     d = {}
     for half in ("far", "near"):
-        partial = call(forward_kernel, shape((GROUP, 2 * part, wide)), 0, 3, flops)(
-            tokens[half], gate_weight, up_weight
+        partial = call(forward_kernel, shape((GROUP, 2 * part, wide)), 0, 3, flops, n_any=1)(
+            tokens[half], gate, up, far_cot if half == "near" else side
         )
         parts = exchange(partial, "row", pairs)
         keep, send = call(
@@ -167,16 +177,15 @@
         d[half] = exchange(copies, "row", pairs)
 
     far_term = call(far_term_kernel, shape((rows * part, depth), F32), 0, 3, flops)(
-        d["far"], gate_weight, up_weight
+        d["far"], gate, up
     )
     came = swap(far_term, "col", cols, 1)
     term = call(near_term_kernel, shape((rows, part, depth)), 0, 4, flops)(
-        d["near"], gate_weight, up_weight, came
+        d["near"], gate, up, came
     )
     over_col = exchange(term, "col", core_groups)
     input_grad = jnp.sum(over_col.astype(F32), axis=0).astype(BF16)
 
-    grad = shape((depth, hidden))
     gate_grad, up_grad = call(weight_grad_kernel, [grad, grad], 0, 4, 2 * flops)(
         tokens["far"], tokens["near"], d["far"], d["near"]
     )

time: 119 us -> 117 us (0.983)
  blocking collectives: 18.3 us -> 0 us
  starting transfers between devices: 49.2 us -> 59.8 us
  waiting for transfers between devices: 36.2 us -> 41.7 us
    all_to_all x1 -> x0, blocking collectives: 18.3 us -> none  [exchange(): return lax.all_to_all(array, axis, 0, 0, axis_index_groups=groups)]
    all_to_all x5 -> x6, starting transfers between devices: 35.9 us -> 48.5 us  [exchange(): return lax.all_to_all(array, axis, 0, 0, axis_index_groups=groups)]
    ppermute x5, waiting for transfers between devices: 12.9 us -> 16.6 us  [swap(): return lax.ppermute(array, axis, [(i, i ^ bit) for i in range(count)])]
    ppermute x5, starting transfers between devices: 13.2 us -> 11.3 us  [swap(): return lax.ppermute(array, axis, [(i, i ^ bit) for i in range(count)])]
    all_to_all x5 -> x6, waiting for transfers between devices: 23.3 us -> 25.1 us  [exchange(): return lax.all_to_all(array, axis, 0, 0, axis_index_groups=groups)]
    pallas_call x2 -> x3, Pallas kernels: 2.95 us -> 3.03 us  [the longest x2 2.95 us: shards(): call(forward_kernel, shape((GROUP, 2 * part, wide)), 0, 3, flops, n_any=1)]
  transfers between devices with their start and end apart: 10 -> 11, of which waited for: 8 -> 8; matrix products, arithmetic and copies ran while one was open for 0% -> 0% of each run, Pallas kernels for 7% -> 7%
where the time goes in v4:
time: 117 us; the launch traced here: 116 us
  starting transfers between devices  59.8 us (51%)
  waiting for transfers between devices  41.7 us (36%)
  Pallas kernels  11.3 us (10%)
  local copies, waits for them, and re-layouts  2.11 us (2%)
    all_to_all x6, starting transfers between devices, exchange(): return lax.all_to_all(array, axis, 0, 0, axis_index_groups=groups)  48.5 us
    all_to_all x6, waiting for transfers between devices, exchange(): return lax.all_to_all(array, axis, 0, 0, axis_index_groups=groups)  25.1 us
    ppermute x5, waiting for transfers between devices, swap(): return lax.ppermute(array, axis, [(i, i ^ bit) for i in range(count)])  16.6 us
    ppermute x5, starting transfers between devices, swap(): return lax.ppermute(array, axis, [(i, i ^ bit) for i in range(count)])  11.3 us
    pallas_call x2, Pallas kernels, shards(): call(act_kernel, shape((GROUP, 2 * part, wide)), 1, 4)  3.12 us
    pallas_call x2, Pallas kernels, shards(): call(forward_kernel, shape((GROUP, 2 * part, wide)), 0, 3, flops, n_any=1)  2.95 us
  transfers between devices with their start and end apart: 11, of which 8 were waited for; matrix products, arithmetic and copies ran while one was open for 0% of the time, Pallas kernels for 7%

profile of v4, /device:TPU:2, one launch (start us, length us, event | category | flops | bytes accessed | tf_op | source)
XLA Modules:
  0.0 116.4 jit_solution(2399590391920858058)
XLA Ops:
  0.6 0.0 copy-start
  0.7 0.0 copy-start.2
  0.7 1.0 copy-done.2
  1.7 0.7 shard_map.67
  2.4 10.3 %all-to-all-start = ((bf16[16,16,384]{2,1,0:T(8,128)(2,1)}), bf16[16,16,384]{2,1,0:T(8,128)(2,1)S(1)}, u32[]{:S(2)}, u32[]{:S(2)}) async-start(bf16[16,16,384]{2,1,0:T(8,128)(2,1)} %shard_map.67), calls=%async_computation | async-start | bytes 393216 | tf_op jit(solution)/shard_map/all_to_all | solution.py:150
  12.7 0.0 copy-done
  12.7 0.0 copy-start.1
  12.7 1.1 copy-done.1
  13.7 0.1 shard_map.68
  13.8 7.1 %all-to-all-done.tokens_ref.far_ref = bf16[16,16,384]{2,1,0:T(8,128)(2,1)S(1)} async-done(((bf16[16,16,384]{2,1,0:T(8,128)(2,1)}), bf16[16,16,384]{2,1,0:T(8,128)(2,1)S(1)}, u32[]{:S(2)}, u32[]{:S(2)}) %all-to-all-start) | async-done | bytes 196640 | tf_op jit(solution)/shard_map/all_to_all | solution.py:150
  20.9 1.5 %shard_map.72 = bf16[8,32,1536]{2,1,0:T(8,128)(2,1)} custom-call(bf16[16,16,384]{2,1,0:T(8,128)(2,1)S(1)} %all-to-all-done.tokens_ref.far_ref, bf16[384,768]{1,0:T(8,128)(2,1)S(1)} %get-tuple-element.11.gate_ref, bf16[384,768]{1,0:T(8,128)(2,1)S(1)} %get-tuple-element.12.up_ref, s32[1]{0:T(128)} %bitcast._), custom_call_target="tpu_custom_call" | custom-call | flops 301989888 | tf_op jit(solution)/shard_map/pallas_call | solution.py:166
  22.4 0.0 copy-start.3
  22.4 5.0 %all-to-all-start.3 = ((bf16[8,32,1536]{2,1,0:T(8,128)(2,1)}), bf16[8,32,1536]{2,1,0:T(8,128)(2,1)S(1)}, u32[]{:S(2)}, u32[]{:S(2)}) async-start(bf16[8,32,1536]{2,1,0:T(8,128)(2,1)} %shard_map.72), calls=%async_computation.3 | async-start | bytes 1572864 | tf_op jit(solution)/shard_map/all_to_all | solution.py:150
  27.5 1.9 %collective-permute-start = (bf16[16,16,384]{2,1,0:T(8,128)(2,1)S(1)}, bf16[16,16,384]{2,1,0:T(8,128)(2,1)S(1)}, u32[]{:S(2)}, u32[]{:S(2)}) collective-permute-start(bf16[16,16,384]{2,1,0:T(8,128)(2,1)S(1)} %all-to-all-done.tokens_ref.far_ref), channel_id=1, source_target_pairs={{0,1},{1,0},{2,3},{3,2},{4,5},{5,4},{6,7},{7,6},{8,9},{9,8},{10,11... | collective-permute-start | bytes 589832 | tf_op jit(solution)/shard_map/ppermute | solution.py:153
  29.4 0.0 copy-done.3
  29.4 2.6 %collective-permute-start.1 = (bf16[32,768]{1,0:T(8,128)(2,1)S(1)}, bf16[32,768]{1,0:T(8,128)(2,1)S(1)}, u32[]{:S(2)}, u32[]{:S(2)}) collective-permute-start(bf16[32,768]{1,0:T(8,128)(2,1)S(1)} %copy-done.3), channel_id=1, source_target_pairs={{0,256},{32,288},{64,320},{96,352},{128,384},{160,416},{192,448},{... | collective-permute-start | bytes 147464 | tf_op jit(solution)/shard_map/ppermute | solution.py:153
  32.0 4.4 %collective-permute-done.1._.far_cot_ref = bf16[32,768]{1,0:T(8,128)(2,1)S(1)} collective-permute-done((bf16[32,768]{1,0:T(8,128)(2,1)S(1)}, bf16[32,768]{1,0:T(8,128)(2,1)S(1)}, u32[]{:S(2)}, u32[]{:S(2)}) %collective-permute-start.1) | collective-permute-done | bytes 49184 | tf_op jit(solution)/shard_map/ppermute | solution.py:153
  36.4 0.0 collective-permute-done.tokens_ref.near_ref
  36.4 1.5 %shard_map.69 = bf16[8,32,1536]{2,1,0:T(8,128)(2,1)} custom-call(bf16[16,16,384]{2,1,0:T(8,128)(2,1)S(1)} %collective-permute-done.tokens_ref.near_ref, bf16[384,768]{1,0:T(8,128)(2,1)S(1)} %get-tuple-element.11.gate_ref, bf16[384,768]{1,0:T(8,128)(2,1)S(1)} %get-tuple-element.12.up_ref, bf16[32,768]{1,0:T(8,128)(2,1)S(1)} %collective-permute-done.1._.far_cot_ref), custom_call_target="tpu_custom_call" | custom-call | flops 301989888 | tf_op jit(solution)/shard_map/pallas_call | solution.py:166
  37.9 0.0 all-to-all-done.3.parts_ref
  37.9 7.1 %all-to-all-start.1 = ((bf16[8,32,1536]{2,1,0:T(8,128)(2,1)}), bf16[8,32,1536]{2,1,0:T(8,128)(2,1)S(1)}, u32[]{:S(2)}, u32[]{:S(2)}) async-start(bf16[8,32,1536]{2,1,0:T(8,128)(2,1)} %shard_map.69), calls=%async_computation.1 | async-start | bytes 1572864 | tf_op jit(solution)/shard_map/all_to_all | solution.py:150
  45.1 0.1 shard_map.73
  45.2 2.2 %collective-permute-start.3 = (bf16[32,1536]{1,0:T(8,128)(2,1)S(1)}, bf16[32,1536]{1,0:T(8,128)(2,1)S(1)}, u32[]{:S(2)}, u32[]{:S(2)}) collective-permute-start(bf16[32,1536]{1,0:T(8,128)(2,1)S(1)} %get-tuple-element.16), channel_id=1, source_target_pairs={{0,256},{32,288},{64,320},{96,352},{128,384},{160,416},{192,448},{... | collective-permute-start | bytes 294920 | tf_op jit(solution)/shard_map/ppermute | solution.py:153
  47.3 0.1 pad_add_fusion.1.where_ref
  47.4 6.6 %collective-permute-done.3.came_ref = bf16[32,1536]{1,0:T(8,128)(2,1)S(1)} collective-permute-done((bf16[32,1536]{1,0:T(8,128)(2,1)S(1)}, bf16[32,1536]{1,0:T(8,128)(2,1)S(1)}, u32[]{:S(2)}, u32[]{:S(2)}) %collective-permute-start.3) | collective-permute-done | bytes 98336 | tf_op jit(solution)/shard_map/ppermute | solution.py:153
  54.0 1.6 %shard_map.74 = bf16[8,32,1536]{2,1,0:T(8,128)(2,1)} custom-call(s32[2]{0:T(128)S(1)} %pad_add_fusion.1.where_ref, f32[32,1536]{1,0:T(8,128)S(1)} %get-tuple-element.15.keep_ref, bf16[32,1536]{1,0:T(8,128)(2,1)S(1)} %collective-permute-done.3.came_ref, bf16[32,768]{1,0:T(8,128)(2,1)S(1)} %copy-done.3, bf16[32,768]{1,0:T(8,128)(2,1)S(1)} %collective-permute-done.1._.far_cot_ref), custom_call_target="tpu_custom_call" | custom-call | tf_op jit(solution)/shard_map/pallas_call | solution.py:174
  55.6 0.4 all-to-all-done.1.parts_ref
  56.0 7.0 %all-to-all-start.4 = ((bf16[8,32,1536]{2,1,0:T(8,128)(2,1)}), bf16[8,32,1536]{2,1,0:T(8,128)(2,1)S(1)}, u32[]{:S(2)}, u32[]{:S(2)}) async-start(bf16[8,32,1536]{2,1,0:T(8,128)(2,1)} %shard_map.74), calls=%async_computation.4 | async-start | bytes 1572864 | tf_op jit(solution)/shard_map/all_to_all | solution.py:150
  63.0 0.1 shard_map.70
  63.1 2.7 %collective-permute-start.2 = (bf16[32,1536]{1,0:T(8,128)(2,1)S(1)}, bf16[32,1536]{1,0:T(8,128)(2,1)S(1)}, u32[]{:S(2)}, u32[]{:S(2)}) collective-permute-start(bf16[32,1536]{1,0:T(8,128)(2,1)S(1)} %get-tuple-element.14), channel_id=1, source_target_pairs={{0,256},{32,288},{64,320},{96,352},{128,384},{160,416},{192,448},{... | collective-permute-start | bytes 294920 | tf_op jit(solution)/shard_map/ppermute | solution.py:153
  65.8 0.1 pad_add_fusion.where_ref
  65.9 5.6 %collective-permute-done.2.came_ref = bf16[32,1536]{1,0:T(8,128)(2,1)S(1)} collective-permute-done((bf16[32,1536]{1,0:T(8,128)(2,1)S(1)}, bf16[32,1536]{1,0:T(8,128)(2,1)S(1)}, u32[]{:S(2)}, u32[]{:S(2)}) %collective-permute-start.2) | collective-permute-done | bytes 98336 | tf_op jit(solution)/shard_map/ppermute | solution.py:153
  71.5 1.5 %shard_map.71 = bf16[8,32,1536]{2,1,0:T(8,128)(2,1)} custom-call(s32[2]{0:T(128)S(1)} %pad_add_fusion.where_ref, f32[32,1536]{1,0:T(8,128)S(1)} %get-tuple-element.13.keep_ref, bf16[32,1536]{1,0:T(8,128)(2,1)S(1)} %collective-permute-done.2.came_ref, bf16[32,768]{1,0:T(8,128)(2,1)S(1)} %copy-done.3, bf16[32,768]{1,0:T(8,128)(2,1)S(1)} %collective-permute-done.1._.far_cot_ref), custom_call_target="tpu_custom_call" | custom-call | tf_op jit(solution)/shard_map/pallas_call | solution.py:174
  73.0 0.4 all-to-all-done.4.d_ref.d_far_ref
  73.4 6.0 %all-to-all-start.2 = ((bf16[8,32,1536]{2,1,0:T(8,128)(2,1)}), bf16[8,32,1536]{2,1,0:T(8,128)(2,1)S(1)}, u32[]{:S(2)}, u32[]{:S(2)}) async-start(bf16[8,32,1536]{2,1,0:T(8,128)(2,1)} %shard_map.71), calls=%async_computation.2 | async-start | bytes 1572864 | tf_op jit(solution)/shard_map/all_to_all | solution.py:150
  79.4 1.3 %shard_map.75 = f32[256,384]{1,0:T(8,128)} custom-call(bf16[8,32,1536]{2,1,0:T(8,128)(2,1)S(1)} %all-to-all-done.4.d_ref.d_far_ref, bf16[384,768]{1,0:T(8,128)(2,1)S(1)} %get-tuple-element.11.gate_ref, bf16[384,768]{1,0:T(8,128)(2,1)S(1)} %get-tuple-element.12.up_ref), custom_call_target="tpu_custom_call" | custom-call | flops 301989888 | tf_op jit(solution)/shard_map/pallas_call | solution.py:179
  80.7 1.9 %collective-permute-start.4 = (f32[256,384]{1,0:T(8,128)}, f32[256,384]{1,0:T(8,128)S(1)}, u32[]{:S(2)}, u32[]{:S(2)}) collective-permute-start(f32[256,384]{1,0:T(8,128)} %shard_map.75), channel_id=1, source_target_pairs={{0,1},{1,0},{2,3},{3,2},{4,5},{5,4},{6,7},{7,6},{8,9},{9,8},{10,11... | collective-permute-start | bytes 1179656 | tf_op jit(solution)/shard_map/ppermute | solution.py:153
  82.6 4.8 %all-to-all-done.2.d_ref.d_near_ref = bf16[8,32,1536]{2,1,0:T(8,128)(2,1)S(1)} async-done(((bf16[8,32,1536]{2,1,0:T(8,128)(2,1)}), bf16[8,32,1536]{2,1,0:T(8,128)(2,1)S(1)}, u32[]{:S(2)}, u32[]{:S(2)}) %all-to-all-start.2) | async-done | bytes 786464 | tf_op jit(solution)/shard_map/all_to_all | solution.py:150
  87.4 0.0 collective-permute-done.4.came_ref
  87.4 1.3 %shard_map.76 = bf16[16,16,384]{2,1,0:T(8,128)(2,1)} custom-call(bf16[8,32,1536]{2,1,0:T(8,128)(2,1)S(1)} %all-to-all-done.2.d_ref.d_near_ref, bf16[384,768]{1,0:T(8,128)(2,1)S(1)} %get-tuple-element.11.gate_ref, bf16[384,768]{1,0:T(8,128)(2,1)S(1)} %get-tuple-element.12.up_ref, f32[256,384]{1,0:T(8,128)S(1)} %collective-permute-done.4.came_ref), custom_call_target="tpu_custom_call" | custom-call | flops 301989888 | tf_op jit(solution)/shard_map/pallas_call | solution.py:183
  88.7 13.0 %all-to-all-start.5 = ((bf16[16,16,384]{2,1,0:T(8,128)(2,1)}), bf16[16,16,384]{2,1,0:T(8,128)(2,1)S(1)}, u32[]{:S(2)}, u32[]{:S(2)}) async-start(bf16[16,16,384]{2,1,0:T(8,128)(2,1)} %shard_map.76), calls=%async_computation.5 | async-start | bytes 393216 | tf_op jit(solution)/shard_map/all_to_all | solution.py:150
  101.7 1.6 %shard_map.77 = (bf16[384,768]{1,0:T(8,128)(2,1)}, bf16[384,768]{1,0:T(8,128)(2,1)}) custom-call(bf16[16,16,384]{2,1,0:T(8,128)(2,1)S(1)} %all-to-all-done.tokens_ref.far_ref, bf16[16,16,384]{2,1,0:T(8,128)(2,1)S(1)} %collective-permute-done.tokens_ref.near_ref, bf16[8,32,1536]{2,1,0:T(8,128)(2,1)S(1)} %all-to-all-done.4.d_ref.d_far_ref, ...), custom_call_target="tpu_custom_call" | custom-call | flops 603979776 | tf_op jit(solution)/shard_map/pallas_call | solution.py:189
  103.3 12.5 %all-to-all-done.5 = bf16[16,16,384]{2,1,0:T(8,128)(2,1)S(1)} async-done(((bf16[16,16,384]{2,1,0:T(8,128)(2,1)}), bf16[16,16,384]{2,1,0:T(8,128)(2,1)S(1)}, u32[]{:S(2)}, u32[]{:S(2)}) %all-to-all-start.5) | async-done | bytes 196640 | tf_op jit(solution)/shard_map/all_to_all | solution.py:150
  115.8 0.6 reduce_sum.12
Async XLA Ops:
  0.6 12.0 %copy-start = (bf16[384,768]{1,0:T(8,128)(2,1)S(1)}, bf16[384,768]{1,0:T(8,128)(2,1)}, u32[]{:S(2)}) copy-start(bf16[384,768]{1,0:T(8,128)(2,1)} %gate_ref.1) | copy-start | bytes 1769476
  0.7 1.1 copy-start.2
  2.4 18.5 %all-to-all-start = ((bf16[16,16,384]{2,1,0:T(8,128)(2,1)}), bf16[16,16,384]{2,1,0:T(8,128)(2,1)S(1)}, u32[]{:S(2)}, u32[]{:S(2)}) async-start(bf16[16,16,384]{2,1,0:T(8,128)(2,1)} %shard_map.67), calls=%async_computation | async-start | bytes 393216 | tf_op jit(solution)/shard_map/all_to_all | solution.py:150
  12.7 1.1 copy-start.1
  22.4 7.0 %copy-start.3 = (bf16[32,768]{1,0:T(8,128)(2,1)S(1)}, bf16[32,768]{1,0:T(8,128)(2,1)}, u32[]{:S(2)}) copy-start(bf16[32,768]{1,0:T(8,128)(2,1)} %cot_ref.3) | copy-start | bytes 147460
  22.4 15.5 %all-to-all-start.3 = ((bf16[8,32,1536]{2,1,0:T(8,128)(2,1)}), bf16[8,32,1536]{2,1,0:T(8,128)(2,1)S(1)}, u32[]{:S(2)}, u32[]{:S(2)}) async-start(bf16[8,32,1536]{2,1,0:T(8,128)(2,1)} %shard_map.72), calls=%async_computation.3 | async-start | bytes 1572864 | tf_op jit(solution)/shard_map/all_to_all | solution.py:150
  27.5 9.0 %collective-permute-start = (bf16[16,16,384]{2,1,0:T(8,128)(2,1)S(1)}, bf16[16,16,384]{2,1,0:T(8,128)(2,1)S(1)}, u32[]{:S(2)}, u32[]{:S(2)}) collective-permute-start(bf16[16,16,384]{2,1,0:T(8,128)(2,1)S(1)} %all-to-all-done.tokens_ref.far_ref), channel_id=1, source_target_pairs={{0,1},{1,0},{2,3},{3,2},{4,5},{5,4},{6,7},{7,6},{8,9},{9,8},{10,11... | collective-permute-start | bytes 589832 | tf_op jit(solution)/shard_map/ppermute | solution.py:153
  29.4 7.0 %collective-permute-start.1 = (bf16[32,768]{1,0:T(8,128)(2,1)S(1)}, bf16[32,768]{1,0:T(8,128)(2,1)S(1)}, u32[]{:S(2)}, u32[]{:S(2)}) collective-permute-start(bf16[32,768]{1,0:T(8,128)(2,1)S(1)} %copy-done.3), channel_id=1, source_target_pairs={{0,256},{32,288},{64,320},{96,352},{128,384},{160,416},{192,448},{... | collective-permute-start | bytes 147464 | tf_op jit(solution)/shard_map/ppermute | solution.py:153
  37.9 18.1 %all-to-all-start.1 = ((bf16[8,32,1536]{2,1,0:T(8,128)(2,1)}), bf16[8,32,1536]{2,1,0:T(8,128)(2,1)S(1)}, u32[]{:S(2)}, u32[]{:S(2)}) async-start(bf16[8,32,1536]{2,1,0:T(8,128)(2,1)} %shard_map.69), calls=%async_computation.1 | async-start | bytes 1572864 | tf_op jit(solution)/shard_map/all_to_all | solution.py:150
  45.2 8.9 %collective-permute-start.3 = (bf16[32,1536]{1,0:T(8,128)(2,1)S(1)}, bf16[32,1536]{1,0:T(8,128)(2,1)S(1)}, u32[]{:S(2)}, u32[]{:S(2)}) collective-permute-start(bf16[32,1536]{1,0:T(8,128)(2,1)S(1)} %get-tuple-element.16), channel_id=1, source_target_pairs={{0,256},{32,288},{64,320},{96,352},{128,384},{160,416},{192,448},{... | collective-permute-start | bytes 294920 | tf_op jit(solution)/shard_map/ppermute | solution.py:153
  56.0 17.4 %all-to-all-start.4 = ((bf16[8,32,1536]{2,1,0:T(8,128)(2,1)}), bf16[8,32,1536]{2,1,0:T(8,128)(2,1)S(1)}, u32[]{:S(2)}, u32[]{:S(2)}) async-start(bf16[8,32,1536]{2,1,0:T(8,128)(2,1)} %shard_map.74), calls=%async_computation.4 | async-start | bytes 1572864 | tf_op jit(solution)/shard_map/all_to_all | solution.py:150
  63.1 8.4 %collective-permute-start.2 = (bf16[32,1536]{1,0:T(8,128)(2,1)S(1)}, bf16[32,1536]{1,0:T(8,128)(2,1)S(1)}, u32[]{:S(2)}, u32[]{:S(2)}) collective-permute-start(bf16[32,1536]{1,0:T(8,128)(2,1)S(1)} %get-tuple-element.14), channel_id=1, source_target_pairs={{0,256},{32,288},{64,320},{96,352},{128,384},{160,416},{192,448},{... | collective-permute-start | bytes 294920 | tf_op jit(solution)/shard_map/ppermute | solution.py:153
  73.4 14.0 %all-to-all-start.2 = ((bf16[8,32,1536]{2,1,0:T(8,128)(2,1)}), bf16[8,32,1536]{2,1,0:T(8,128)(2,1)S(1)}, u32[]{:S(2)}, u32[]{:S(2)}) async-start(bf16[8,32,1536]{2,1,0:T(8,128)(2,1)} %shard_map.71), calls=%async_computation.2 | async-start | bytes 1572864 | tf_op jit(solution)/shard_map/all_to_all | solution.py:150
  80.7 6.7 %collective-permute-start.4 = (f32[256,384]{1,0:T(8,128)}, f32[256,384]{1,0:T(8,128)S(1)}, u32[]{:S(2)}, u32[]{:S(2)}) collective-permute-start(f32[256,384]{1,0:T(8,128)} %shard_map.75), channel_id=1, source_target_pairs={{0,1},{1,0},{2,3},{3,2},{4,5},{5,4},{6,7},{7,6},{8,9},{9,8},{10,11... | collective-permute-start | bytes 1179656 | tf_op jit(solution)/shard_map/ppermute | solution.py:153
  88.7 27.1 %all-to-all-start.5 = ((bf16[16,16,384]{2,1,0:T(8,128)(2,1)}), bf16[16,16,384]{2,1,0:T(8,128)(2,1)S(1)}, u32[]{:S(2)}, u32[]{:S(2)}) async-start(bf16[16,16,384]{2,1,0:T(8,128)(2,1)} %shard_map.76), calls=%async_computation.5 | async-start | bytes 393216 | tf_op jit(solution)/shard_map/all_to_all | solution.py:150

commit v5 on v4

--- a/solution.py
+++ b/solution.py
@@ -18,13 +18,6 @@
 
 def rows_at(start, size):
     return pl.ds(pl.multiple_of(start * size, size), size)
-
-
-def lay_kernel(half_ref, tokens_ref, out_ref):
-    rows, part, depth = out_ref.shape
-    at = rows_at(half_ref[0], part)
-    for row in range(rows):
-        out_ref[row] = tokens_ref[at, row * depth : (row + 1) * depth]
 
 
 def stage_kernel(gate_ref, up_ref, gate_out_ref, up_out_ref):
@@ -97,11 +90,11 @@
 
 
 def far_term_kernel(d_ref, gate_ref, up_ref, out_ref):
-    out_ref[...] = term_of(d_ref, gate_ref, up_ref)
+    out_ref[...] = term_of(d_ref, gate_ref, up_ref).astype(BF16)
 
 
 def near_term_kernel(d_ref, gate_ref, up_ref, came_ref, out_ref):
-    total = term_of(d_ref, gate_ref, up_ref) + came_ref[...]
+    total = term_of(d_ref, gate_ref, up_ref) + came_ref[...].astype(F32)
     out_ref[...] = total.astype(BF16).reshape(out_ref.shape)
 
 
@@ -152,14 +145,13 @@
     def swap(array, axis, count, bit):
         return lax.ppermute(array, axis, [(i, i ^ bit) for i in range(count)])
 
-    sent = call(lay_kernel, shape((rows, part, depth)), 1, 1)(halves["far"], inputs)
+    sent = lax.dynamic_slice_in_dim(inputs, halves["far"][0] * part, part, axis=0)
+    sent = sent.reshape(part, rows, depth).transpose(1, 0, 2)
     tokens = {"far": exchange(sent, "row")}
     tokens["near"] = swap(tokens["far"], "col", cols, 1)
 
     grad = shape((depth, hidden))
-    gate, up = call(stage_kernel, [grad, grad], 0, 2, nbytes=8 * depth * hidden)(
-        gate_weight, up_weight
-    )
+    gate, up = gate_weight, up_weight
     far_cot = swap(cotangent, "row", rows, GROUP)
     d = {}
     for half in ("far", "near"):
@@ -176,7 +168,7 @@
         )
         d[half] = exchange(copies, "row", pairs)
 
-    far_term = call(far_term_kernel, shape((rows * part, depth), F32), 0, 3, flops)(
+    far_term = call(far_term_kernel, shape((rows * part, depth)), 0, 3, flops)(
         d["far"], gate, up
     )
     came = swap(far_term, "col", cols, 1)

time: 117 us -> 117 us (level)
  Pallas kernels: 11.3 us -> 8.63 us
  local copies, waits for them, and re-layouts: 2.11 us -> 3.6 us
  waiting for transfers between devices: 41.7 us -> 42.9 us
    all_to_all x6, waiting for transfers between devices: 25.1 us -> 26.3 us  [exchange(): return lax.all_to_all(array, axis, 0, 0, axis_index_groups=groups)]
    unnamed x8 -> x16, local copies, waits for them, and re-layouts: 2.11 us -> 2.89 us
  transfers between devices with their start and end apart: 11 -> 11, of which waited for: 8 -> 8; matrix products, arithmetic and copies ran while one was open for 0% -> 0% of each run, Pallas kernels for 7% -> 5%
where the time goes in v5:
time: 117 us
  starting transfers between devices  59.9 us (51%)
  waiting for transfers between devices  42.9 us (37%)
  Pallas kernels  8.63 us (7%)
  local copies, waits for them, and re-layouts  3.6 us (3%)
    all_to_all x6, starting transfers between devices, exchange(): return lax.all_to_all(array, axis, 0, 0, axis_index_groups=groups)  48.6 us
    all_to_all x6, waiting for transfers between devices, exchange(): return lax.all_to_all(array, axis, 0, 0, axis_index_groups=groups)  26.3 us
    ppermute x5, waiting for transfers between devices, swap(): return lax.ppermute(array, axis, [(i, i ^ bit) for i in range(count)])  16.6 us
    ppermute x5, starting transfers between devices, swap(): return lax.ppermute(array, axis, [(i, i ^ bit) for i in range(count)])  11.3 us
    unnamed x16, local copies, waits for them, and re-layouts  2.89 us
  transfers between devices with their start and end apart: 11, of which 8 were waited for; matrix products, arithmetic and copies ran while one was open for 0% of the time, Pallas kernels for 5%

profile of v5, /device:TPU:2, one launch (start us, length us, event | category | flops | bytes accessed | tf_op | source)
XLA Modules:
  0.0 116.6 jit_solution(3006030373751547156)
XLA Ops:
  0.6 0.0 copy-start
  0.7 1.0 copy-done
  1.6 0.0 copy-start.1
  1.6 0.0 copy-start.2
  1.7 0.7 copy.10
  2.4 10.3 %all-to-all-start = ((bf16[16,16,384]{2,1,0:T(8,128)(2,1)}), bf16[16,16,384]{2,1,0:T(8,128)(2,1)S(1)}, u32[]{:S(2)}, u32[]{:S(2)}) async-start(bf16[16,16,384]{2,1,0:T(8,128)(2,1)} %bitcast.9), calls=%async_computation | async-start | bytes 393216 | tf_op jit(solution)/shard_map/all_to_all | solution.py:143
  12.6 8.3 %all-to-all-done.tokens_ref.far_ref = bf16[16,16,384]{2,1,0:T(8,128)(2,1)S(1)} async-done(((bf16[16,16,384]{2,1,0:T(8,128)(2,1)}), bf16[16,16,384]{2,1,0:T(8,128)(2,1)S(1)}, u32[]{:S(2)}, u32[]{:S(2)}) %all-to-all-start) | async-done | bytes 196640 | tf_op jit(solution)/shard_map/all_to_all | solution.py:143
  20.9 0.0 copy-done.1
  20.9 0.0 copy-done.2
  20.9 1.5 %shard_map.70 = bf16[8,32,1536]{2,1,0:T(8,128)(2,1)} custom-call(bf16[16,16,384]{2,1,0:T(8,128)(2,1)S(1)} %all-to-all-done.tokens_ref.far_ref, bf16[384,768]{1,0:T(8,128)(2,1)S(1)} %copy-done.1, bf16[384,768]{1,0:T(8,128)(2,1)S(1)} %copy-done.2, s32[1]{0:T(128)} %bitcast._), custom_call_target="tpu_custom_call" | custom-call | flops 301989888 | tf_op jit(solution)/shard_map/pallas_call | solution.py:158
  22.4 0.0 copy-start.5
  22.4 5.0 %all-to-all-start.3 = ((bf16[8,32,1536]{2,1,0:T(8,128)(2,1)}), bf16[8,32,1536]{2,1,0:T(8,128)(2,1)S(1)}, u32[]{:S(2)}, u32[]{:S(2)}) async-start(bf16[8,32,1536]{2,1,0:T(8,128)(2,1)} %shard_map.70), calls=%async_computation.3 | async-start | bytes 1572864 | tf_op jit(solution)/shard_map/all_to_all | solution.py:143
  27.4 1.9 %collective-permute-start = (bf16[16,16,384]{2,1,0:T(8,128)(2,1)S(1)}, bf16[16,16,384]{2,1,0:T(8,128)(2,1)S(1)}, u32[]{:S(2)}, u32[]{:S(2)}) collective-permute-start(bf16[16,16,384]{2,1,0:T(8,128)(2,1)S(1)} %all-to-all-done.tokens_ref.far_ref), channel_id=1, source_target_pairs={{0,1},{1,0},{2,3},{3,2},{4,5},{5,4},{6,7},{7,6},{8,9},{9,8},{10,11... | collective-permute-start | bytes 589832 | tf_op jit(solution)/shard_map/ppermute | solution.py:146
  29.4 0.0 copy-done.5
  29.4 2.6 %collective-permute-start.1 = (bf16[32,768]{1,0:T(8,128)(2,1)S(1)}, bf16[32,768]{1,0:T(8,128)(2,1)S(1)}, u32[]{:S(2)}, u32[]{:S(2)}) collective-permute-start(bf16[32,768]{1,0:T(8,128)(2,1)S(1)} %copy-done.5), channel_id=1, source_target_pairs={{0,256},{32,288},{64,320},{96,352},{128,384},{160,416},{192,448},{... | collective-permute-start | bytes 147464 | tf_op jit(solution)/shard_map/ppermute | solution.py:146
  32.0 4.4 %collective-permute-done.1._.far_cot_ref = bf16[32,768]{1,0:T(8,128)(2,1)S(1)} collective-permute-done((bf16[32,768]{1,0:T(8,128)(2,1)S(1)}, bf16[32,768]{1,0:T(8,128)(2,1)S(1)}, u32[]{:S(2)}, u32[]{:S(2)}) %collective-permute-start.1) | collective-permute-done | bytes 49184 | tf_op jit(solution)/shard_map/ppermute | solution.py:146
  36.4 0.0 collective-permute-done.tokens_ref.near_ref
  36.4 0.6 shard_map.67
  37.0 0.1 copy-done.6
  37.1 0.9 copy-done.4
  38.0 0.0 all-to-all-done.3.parts_ref
  38.0 7.1 %all-to-all-start.1 = ((bf16[8,32,1536]{2,1,0:T(8,128)(2,1)}), bf16[8,32,1536]{2,1,0:T(8,128)(2,1)S(1)}, u32[]{:S(2)}, u32[]{:S(2)}) async-start(bf16[8,32,1536]{2,1,0:T(8,128)(2,1)} %copy-done.4), calls=%async_computation.1 | async-start | bytes 1572864 | tf_op jit(solution)/shard_map/all_to_all | solution.py:143
  45.1 0.1 shard_map.71
  45.2 2.2 %collective-permute-start.3 = (bf16[32,1536]{1,0:T(8,128)(2,1)S(1)}, bf16[32,1536]{1,0:T(8,128)(2,1)S(1)}, u32[]{:S(2)}, u32[]{:S(2)}) collective-permute-start(bf16[32,1536]{1,0:T(8,128)(2,1)S(1)} %get-tuple-element.12), channel_id=1, source_target_pairs={{0,256},{32,288},{64,320},{96,352},{128,384},{160,416},{192,448},{... | collective-permute-start | bytes 294920 | tf_op jit(solution)/shard_map/ppermute | solution.py:146
  47.4 0.1 pad_add_fusion.1.where_ref
  47.5 6.6 %collective-permute-done.3.came_ref = bf16[32,1536]{1,0:T(8,128)(2,1)S(1)} collective-permute-done((bf16[32,1536]{1,0:T(8,128)(2,1)S(1)}, bf16[32,1536]{1,0:T(8,128)(2,1)S(1)}, u32[]{:S(2)}, u32[]{:S(2)}) %collective-permute-start.3) | collective-permute-done | bytes 98336 | tf_op jit(solution)/shard_map/ppermute | solution.py:146
  54.1 0.7 shard_map.72
  54.8 0.0 copy-start.3
  54.8 0.9 copy-done.3
  55.7 0.3 all-to-all-done.1.parts_ref
  56.0 7.0 %all-to-all-start.4 = ((bf16[8,32,1536]{2,1,0:T(8,128)(2,1)}), bf16[8,32,1536]{2,1,0:T(8,128)(2,1)S(1)}, u32[]{:S(2)}, u32[]{:S(2)}) async-start(bf16[8,32,1536]{2,1,0:T(8,128)(2,1)} %copy-done.3), calls=%async_computation.4 | async-start | bytes 1572864 | tf_op jit(solution)/shard_map/all_to_all | solution.py:143
  63.1 0.1 shard_map.68
  63.2 2.7 %collective-permute-start.2 = (bf16[32,1536]{1,0:T(8,128)(2,1)S(1)}, bf16[32,1536]{1,0:T(8,128)(2,1)S(1)}, u32[]{:S(2)}, u32[]{:S(2)}) collective-permute-start(bf16[32,1536]{1,0:T(8,128)(2,1)S(1)} %get-tuple-element.10), channel_id=1, source_target_pairs={{0,256},{32,288},{64,320},{96,352},{128,384},{160,416},{192,448},{... | collective-permute-start | bytes 294920 | tf_op jit(solution)/shard_map/ppermute | solution.py:146
  65.9 0.1 pad_add_fusion.where_ref
  66.0 5.5 %collective-permute-done.2.came_ref = bf16[32,1536]{1,0:T(8,128)(2,1)S(1)} collective-permute-done((bf16[32,1536]{1,0:T(8,128)(2,1)S(1)}, bf16[32,1536]{1,0:T(8,128)(2,1)S(1)}, u32[]{:S(2)}, u32[]{:S(2)}) %collective-permute-start.2) | collective-permute-done | bytes 98336 | tf_op jit(solution)/shard_map/ppermute | solution.py:146
  71.5 1.5 %shard_map.69 = bf16[8,32,1536]{2,1,0:T(8,128)(2,1)} custom-call(s32[2]{0:T(128)S(1)} %pad_add_fusion.where_ref, f32[32,1536]{1,0:T(8,128)S(1)} %get-tuple-element.9.keep_ref, bf16[32,1536]{1,0:T(8,128)(2,1)S(1)} %collective-permute-done.2.came_ref, bf16[32,768]{1,0:T(8,128)(2,1)S(1)} %copy-done.5, bf16[32,768]{1,0:T(8,128)(2,1)S(1)} %collective-permute-done.1._.far_cot_ref), custom_call_target="tpu_custom_call" | custom-call | tf_op jit(solution)/shard_map/pallas_call | solution.py:166
  73.1 0.4 all-to-all-done.4.d_ref.d_far_ref
  73.5 6.0 %all-to-all-start.2 = ((bf16[8,32,1536]{2,1,0:T(8,128)(2,1)}), bf16[8,32,1536]{2,1,0:T(8,128)(2,1)S(1)}, u32[]{:S(2)}, u32[]{:S(2)}) async-start(bf16[8,32,1536]{2,1,0:T(8,128)(2,1)} %shard_map.69), calls=%async_computation.2 | async-start | bytes 1572864 | tf_op jit(solution)/shard_map/all_to_all | solution.py:143
  79.5 1.3 %shard_map.73 = bf16[256,384]{1,0:T(8,128)(2,1)} custom-call(bf16[8,32,1536]{2,1,0:T(8,128)(2,1)S(1)} %all-to-all-done.4.d_ref.d_far_ref, bf16[384,768]{1,0:T(8,128)(2,1)S(1)} %copy-done.1, bf16[384,768]{1,0:T(8,128)(2,1)S(1)} %copy-done.2), custom_call_target="tpu_custom_call" | custom-call | flops 301989888 | tf_op jit(solution)/shard_map/pallas_call | solution.py:171
  80.7 1.9 %collective-permute-start.4 = (bf16[256,384]{1,0:T(8,128)(2,1)}, bf16[256,384]{1,0:T(8,128)(2,1)S(1)}, u32[]{:S(2)}, u32[]{:S(2)}) collective-permute-start(bf16[256,384]{1,0:T(8,128)(2,1)} %shard_map.73), channel_id=1, source_target_pairs={{0,1},{1,0},{2,3},{3,2},{4,5},{5,4},{6,7},{7,6},{8,9},{9,8},{10,11... | collective-permute-start | bytes 589832 | tf_op jit(solution)/shard_map/ppermute | solution.py:146
  82.7 4.8 %all-to-all-done.2.d_ref.d_near_ref = bf16[8,32,1536]{2,1,0:T(8,128)(2,1)S(1)} async-done(((bf16[8,32,1536]{2,1,0:T(8,128)(2,1)}), bf16[8,32,1536]{2,1,0:T(8,128)(2,1)S(1)}, u32[]{:S(2)}, u32[]{:S(2)}) %all-to-all-start.2) | async-done | bytes 786464 | tf_op jit(solution)/shard_map/all_to_all | solution.py:143
  87.5 0.0 collective-permute-done.4.came_ref
  87.5 1.3 %shard_map.74 = bf16[16,16,384]{2,1,0:T(8,128)(2,1)} custom-call(bf16[8,32,1536]{2,1,0:T(8,128)(2,1)S(1)} %all-to-all-done.2.d_ref.d_near_ref, bf16[384,768]{1,0:T(8,128)(2,1)S(1)} %copy-done.1, bf16[384,768]{1,0:T(8,128)(2,1)S(1)} %copy-done.2, bf16[256,384]{1,0:T(8,128)(2,1)S(1)} %collective-permute-done.4.came_ref), custom_call_target="tpu_custom_call" | custom-call | flops 301989888 | tf_op jit(solution)/shard_map/pallas_call | solution.py:175
  88.8 13.1 %all-to-all-start.5 = ((bf16[16,16,384]{2,1,0:T(8,128)(2,1)}), bf16[16,16,384]{2,1,0:T(8,128)(2,1)S(1)}, u32[]{:S(2)}, u32[]{:S(2)}) async-start(bf16[16,16,384]{2,1,0:T(8,128)(2,1)} %shard_map.74), calls=%async_computation.5 | async-start | bytes 393216 | tf_op jit(solution)/shard_map/all_to_all | solution.py:143
  101.9 0.0 copy-done.7
  101.9 1.6 %shard_map.75 = (bf16[384,768]{1,0:T(8,128)(2,1)}, bf16[384,768]{1,0:T(8,128)(2,1)}) custom-call(bf16[16,16,384]{2,1,0:T(8,128)(2,1)S(1)} %all-to-all-done.tokens_ref.far_ref, bf16[16,16,384]{2,1,0:T(8,128)(2,1)S(1)} %copy-done.7, bf16[8,32,1536]{2,1,0:T(8,128)(2,1)S(1)} %all-to-all-done.4.d_ref.d_far_ref, ...), custom_call_target="tpu_custom_call" | custom-call | flops 603979776 | tf_op jit(solution)/shard_map/pallas_call | solution.py:181
  103.5 12.5 %all-to-all-done.5 = bf16[16,16,384]{2,1,0:T(8,128)(2,1)S(1)} async-done(((bf16[16,16,384]{2,1,0:T(8,128)(2,1)}), bf16[16,16,384]{2,1,0:T(8,128)(2,1)S(1)}, u32[]{:S(2)}, u32[]{:S(2)}) %all-to-all-start.5) | async-done | bytes 196640 | tf_op jit(solution)/shard_map/all_to_all | solution.py:143
  116.0 0.6 reduce_sum.12
  (4 shorter events, 0.0 us)
Async XLA Ops:
  0.6 1.0 copy-start
  1.6 19.3 %copy-start.1 = (bf16[384,768]{1,0:T(8,128)(2,1)S(1)}, bf16[384,768]{1,0:T(8,128)(2,1)}, u32[]{:S(2)}) copy-start(bf16[384,768]{1,0:T(8,128)(2,1)} %gate_ref.7) | copy-start | bytes 1769476
  1.6 19.3 %copy-start.2 = (bf16[384,768]{1,0:T(8,128)(2,1)S(1)}, bf16[384,768]{1,0:T(8,128)(2,1)}, u32[]{:S(2)}) copy-start(bf16[384,768]{1,0:T(8,128)(2,1)} %up_ref.7) | copy-start | bytes 1769476
  2.4 18.5 %all-to-all-start = ((bf16[16,16,384]{2,1,0:T(8,128)(2,1)}), bf16[16,16,384]{2,1,0:T(8,128)(2,1)S(1)}, u32[]{:S(2)}, u32[]{:S(2)}) async-start(bf16[16,16,384]{2,1,0:T(8,128)(2,1)} %bitcast.9), calls=%async_computation | async-start | bytes 393216 | tf_op jit(solution)/shard_map/all_to_all | solution.py:143
  22.4 7.0 %copy-start.5 = (bf16[32,768]{1,0:T(8,128)(2,1)S(1)}, bf16[32,768]{1,0:T(8,128)(2,1)}, u32[]{:S(2)}) copy-start(bf16[32,768]{1,0:T(8,128)(2,1)} %cot_ref.3) | copy-start | bytes 147460
  22.4 15.6 %all-to-all-start.3 = ((bf16[8,32,1536]{2,1,0:T(8,128)(2,1)}), bf16[8,32,1536]{2,1,0:T(8,128)(2,1)S(1)}, u32[]{:S(2)}, u32[]{:S(2)}) async-start(bf16[8,32,1536]{2,1,0:T(8,128)(2,1)} %shard_map.70), calls=%async_computation.3 | async-start | bytes 1572864 | tf_op jit(solution)/shard_map/all_to_all | solution.py:143
  27.4 9.0 %collective-permute-start = (bf16[16,16,384]{2,1,0:T(8,128)(2,1)S(1)}, bf16[16,16,384]{2,1,0:T(8,128)(2,1)S(1)}, u32[]{:S(2)}, u32[]{:S(2)}) collective-permute-start(bf16[16,16,384]{2,1,0:T(8,128)(2,1)S(1)} %all-to-all-done.tokens_ref.far_ref), channel_id=1, source_target_pairs={{0,1},{1,0},{2,3},{3,2},{4,5},{5,4},{6,7},{7,6},{8,9},{9,8},{10,11... | collective-permute-start | bytes 589832 | tf_op jit(solution)/shard_map/ppermute | solution.py:146
  29.4 7.0 %collective-permute-start.1 = (bf16[32,768]{1,0:T(8,128)(2,1)S(1)}, bf16[32,768]{1,0:T(8,128)(2,1)S(1)}, u32[]{:S(2)}, u32[]{:S(2)}) collective-permute-start(bf16[32,768]{1,0:T(8,128)(2,1)S(1)} %copy-done.5), channel_id=1, source_target_pairs={{0,256},{32,288},{64,320},{96,352},{128,384},{160,416},{192,448},{... | collective-permute-start | bytes 147464 | tf_op jit(solution)/shard_map/ppermute | solution.py:146
  36.4 0.7 copy-start.6
  37.1 0.9 copy-start.4
  38.0 18.1 %all-to-all-start.1 = ((bf16[8,32,1536]{2,1,0:T(8,128)(2,1)}), bf16[8,32,1536]{2,1,0:T(8,128)(2,1)S(1)}, u32[]{:S(2)}, u32[]{:S(2)}) async-start(bf16[8,32,1536]{2,1,0:T(8,128)(2,1)} %copy-done.4), calls=%async_computation.1 | async-start | bytes 1572864 | tf_op jit(solution)/shard_map/all_to_all | solution.py:143
  45.2 8.9 %collective-permute-start.3 = (bf16[32,1536]{1,0:T(8,128)(2,1)S(1)}, bf16[32,1536]{1,0:T(8,128)(2,1)S(1)}, u32[]{:S(2)}, u32[]{:S(2)}) collective-permute-start(bf16[32,1536]{1,0:T(8,128)(2,1)S(1)} %get-tuple-element.12), channel_id=1, source_target_pairs={{0,256},{32,288},{64,320},{96,352},{128,384},{160,416},{192,448},{... | collective-permute-start | bytes 294920 | tf_op jit(solution)/shard_map/ppermute | solution.py:146
  54.8 0.9 copy-start.3
  56.0 17.4 %all-to-all-start.4 = ((bf16[8,32,1536]{2,1,0:T(8,128)(2,1)}), bf16[8,32,1536]{2,1,0:T(8,128)(2,1)S(1)}, u32[]{:S(2)}, u32[]{:S(2)}) async-start(bf16[8,32,1536]{2,1,0:T(8,128)(2,1)} %copy-done.3), calls=%async_computation.4 | async-start | bytes 1572864 | tf_op jit(solution)/shard_map/all_to_all | solution.py:143
  63.2 8.4 %collective-permute-start.2 = (bf16[32,1536]{1,0:T(8,128)(2,1)S(1)}, bf16[32,1536]{1,0:T(8,128)(2,1)S(1)}, u32[]{:S(2)}, u32[]{:S(2)}) collective-permute-start(bf16[32,1536]{1,0:T(8,128)(2,1)S(1)} %get-tuple-element.10), channel_id=1, source_target_pairs={{0,256},{32,288},{64,320},{96,352},{128,384},{160,416},{192,448},{... | collective-permute-start | bytes 294920 | tf_op jit(solution)/shard_map/ppermute | solution.py:146
  73.5 14.0 %all-to-all-start.2 = ((bf16[8,32,1536]{2,1,0:T(8,128)(2,1)}), bf16[8,32,1536]{2,1,0:T(8,128)(2,1)S(1)}, u32[]{:S(2)}, u32[]{:S(2)}) async-start(bf16[8,32,1536]{2,1,0:T(8,128)(2,1)} %shard_map.69), calls=%async_computation.2 | async-start | bytes 1572864 | tf_op jit(solution)/shard_map/all_to_all | solution.py:143
  80.7 6.8 %collective-permute-start.4 = (bf16[256,384]{1,0:T(8,128)(2,1)}, bf16[256,384]{1,0:T(8,128)(2,1)S(1)}, u32[]{:S(2)}, u32[]{:S(2)}) collective-permute-start(bf16[256,384]{1,0:T(8,128)(2,1)} %shard_map.73), channel_id=1, source_target_pairs={{0,1},{1,0},{2,3},{3,2},{4,5},{5,4},{6,7},{7,6},{8,9},{9,8},{10,11... | collective-permute-start | bytes 589832 | tf_op jit(solution)/shard_map/ppermute | solution.py:146
  88.8 13.1 %copy-start.7 = (bf16[16,16,384]{2,1,0:T(8,128)(2,1)S(1)}, bf16[16,16,384]{2,1,0:T(8,128)(2,1)}, u32[]{:S(2)}) copy-start(bf16[16,16,384]{2,1,0:T(8,128)(2,1)} %copy-done.6) | copy-start | bytes 589828
  88.8 27.2 %all-to-all-start.5 = ((bf16[16,16,384]{2,1,0:T(8,128)(2,1)}), bf16[16,16,384]{2,1,0:T(8,128)(2,1)S(1)}, u32[]{:S(2)}, u32[]{:S(2)}) async-start(bf16[16,16,384]{2,1,0:T(8,128)(2,1)} %shard_map.74), calls=%async_computation.5 | async-start | bytes 393216 | tf_op jit(solution)/shard_map/all_to_all | solution.py:143

commit v6 on v4

--- a/solution.py
+++ b/solution.py
@@ -100,9 +100,15 @@
     out_ref[...] = term_of(d_ref, gate_ref, up_ref)
 
 
+def by_z_hi(rows):
+    return [2 * y + z_hi for z_hi in range(2) for y in range(rows // 2)]
+
+
 def near_term_kernel(d_ref, gate_ref, up_ref, came_ref, out_ref):
-    total = term_of(d_ref, gate_ref, up_ref) + came_ref[...]
-    out_ref[...] = total.astype(BF16).reshape(out_ref.shape)
+    rows, part, _ = out_ref.shape
+    total = (term_of(d_ref, gate_ref, up_ref) + came_ref[...]).astype(BF16)
+    for i, row in enumerate(by_z_hi(rows)):
+        out_ref[i] = total[row * part : (row + 1) * part]
 
 
 def weight_grad_kernel(far_ref, near_ref, d_far_ref, d_near_ref, gate_ref, up_ref):
@@ -134,7 +140,7 @@
     wide = 2 * hidden
     flops = 2 * rows * part * depth * wide
     pairs = [list(range(0, GROUP)), list(range(GROUP, 2 * GROUP))]
-    core_groups = [[2 * i + core for i in range(cols // 2)] for core in range(2)]
+    core_groups = [[2 * r + core for r in by_z_hi(rows)] for core in range(2)]
     row, col = lax.axis_index("row"), lax.axis_index("col")
 
     def scalar(value):

time: 117 us -> 117 us (level)
  the two profiles are of different devices: /device:TPU:2 before, /device:TPU:8 now
where the time goes in v6:
time: 117 us; the launch traced here: 116 us
  starting transfers between devices  53.1 us (45%)
  waiting for transfers between devices  48 us (41%)
  Pallas kernels  11.3 us (10%)
  local copies, waits for them, and re-layouts  2.11 us (2%)
    all_to_all x6, starting transfers between devices, exchange(): return lax.all_to_all(array, axis, 0, 0, axis_index_groups=groups)  41.8 us
    all_to_all x6, waiting for transfers between devices, exchange(): return lax.all_to_all(array, axis, 0, 0, axis_index_groups=groups)  30.7 us
    ppermute x5, waiting for transfers between devices, swap(): return lax.ppermute(array, axis, [(i, i ^ bit) for i in range(count)])  17.2 us
    ppermute x5, starting transfers between devices, swap(): return lax.ppermute(array, axis, [(i, i ^ bit) for i in range(count)])  11.4 us
    pallas_call x2, Pallas kernels, shards(): call(act_kernel, shape((GROUP, 2 * part, wide)), 1, 4)  3.12 us
    pallas_call x2, Pallas kernels, shards(): call(forward_kernel, shape((GROUP, 2 * part, wide)), 0, 3, flops, n_any=1)  2.95 us
  transfers between devices with their start and end apart: 11, of which 9 were waited for; matrix products, arithmetic and copies ran while one was open for 0% of the time, Pallas kernels for 7%

profile of v6, /device:TPU:8, one launch (start us, length us, event | category | flops | bytes accessed | tf_op | source)
XLA Modules:
  0.0 116.0 jit_solution(5711376110926353069)
XLA Ops:
  0.6 0.0 copy-start
  0.7 0.0 copy-start.2
  0.7 1.0 copy-done.2
  1.7 0.7 shard_map.67
  2.4 9.8 %all-to-all-start = ((bf16[16,16,384]{2,1,0:T(8,128)(2,1)}), bf16[16,16,384]{2,1,0:T(8,128)(2,1)S(1)}, u32[]{:S(2)}, u32[]{:S(2)}) async-start(bf16[16,16,384]{2,1,0:T(8,128)(2,1)} %shard_map.67), calls=%async_computation | async-start | bytes 393216 | tf_op jit(solution)/shard_map/all_to_all | solution.py:156
  12.3 0.0 copy-done
  12.3 0.0 copy-start.1
  12.3 1.1 copy-done.1
  13.3 0.1 shard_map.68
  13.4 8.5 %all-to-all-done.tokens_ref.far_ref = bf16[16,16,384]{2,1,0:T(8,128)(2,1)S(1)} async-done(((bf16[16,16,384]{2,1,0:T(8,128)(2,1)}), bf16[16,16,384]{2,1,0:T(8,128)(2,1)S(1)}, u32[]{:S(2)}, u32[]{:S(2)}) %all-to-all-start) | async-done | bytes 196640 | tf_op jit(solution)/shard_map/all_to_all | solution.py:156
  21.9 1.5 %shard_map.72 = bf16[8,32,1536]{2,1,0:T(8,128)(2,1)} custom-call(bf16[16,16,384]{2,1,0:T(8,128)(2,1)S(1)} %all-to-all-done.tokens_ref.far_ref, bf16[384,768]{1,0:T(8,128)(2,1)S(1)} %get-tuple-element.11.gate_ref, bf16[384,768]{1,0:T(8,128)(2,1)S(1)} %get-tuple-element.12.up_ref, s32[1]{0:T(128)} %bitcast._), custom_call_target="tpu_custom_call" | custom-call | flops 301989888 | tf_op jit(solution)/shard_map/pallas_call | solution.py:172
  23.3 0.0 copy-start.3
  23.3 3.7 %all-to-all-start.3 = ((bf16[8,32,1536]{2,1,0:T(8,128)(2,1)}), bf16[8,32,1536]{2,1,0:T(8,128)(2,1)S(1)}, u32[]{:S(2)}, u32[]{:S(2)}) async-start(bf16[8,32,1536]{2,1,0:T(8,128)(2,1)} %shard_map.72), calls=%async_computation.3 | async-start | bytes 1572864 | tf_op jit(solution)/shard_map/all_to_all | solution.py:156
  27.0 1.9 %collective-permute-start = (bf16[16,16,384]{2,1,0:T(8,128)(2,1)S(1)}, bf16[16,16,384]{2,1,0:T(8,128)(2,1)S(1)}, u32[]{:S(2)}, u32[]{:S(2)}) collective-permute-start(bf16[16,16,384]{2,1,0:T(8,128)(2,1)S(1)} %all-to-all-done.tokens_ref.far_ref), channel_id=1, source_target_pairs={{0,1},{1,0},{2,3},{3,2},{4,5},{5,4},{6,7},{7,6},{8,9},{9,8},{10,11... | collective-permute-start | bytes 589832 | tf_op jit(solution)/shard_map/ppermute | solution.py:159
  29.0 0.0 copy-done.3
  29.0 2.6 %collective-permute-start.1 = (bf16[32,768]{1,0:T(8,128)(2,1)S(1)}, bf16[32,768]{1,0:T(8,128)(2,1)S(1)}, u32[]{:S(2)}, u32[]{:S(2)}) collective-permute-start(bf16[32,768]{1,0:T(8,128)(2,1)S(1)} %copy-done.3), channel_id=1, source_target_pairs={{0,256},{32,288},{64,320},{96,352},{128,384},{160,416},{192,448},{... | collective-permute-start | bytes 147464 | tf_op jit(solution)/shard_map/ppermute | solution.py:159
  31.6 4.4 %collective-permute-done.1._.far_cot_ref = bf16[32,768]{1,0:T(8,128)(2,1)S(1)} collective-permute-done((bf16[32,768]{1,0:T(8,128)(2,1)S(1)}, bf16[32,768]{1,0:T(8,128)(2,1)S(1)}, u32[]{:S(2)}, u32[]{:S(2)}) %collective-permute-start.1) | collective-permute-done | bytes 49184 | tf_op jit(solution)/shard_map/ppermute | solution.py:159
  36.0 0.0 collective-permute-done.tokens_ref.near_ref
  36.0 1.5 %shard_map.69 = bf16[8,32,1536]{2,1,0:T(8,128)(2,1)} custom-call(bf16[16,16,384]{2,1,0:T(8,128)(2,1)S(1)} %collective-permute-done.tokens_ref.near_ref, bf16[384,768]{1,0:T(8,128)(2,1)S(1)} %get-tuple-element.11.gate_ref, bf16[384,768]{1,0:T(8,128)(2,1)S(1)} %get-tuple-element.12.up_ref, bf16[32,768]{1,0:T(8,128)(2,1)S(1)} %collective-permute-done.1._.far_cot_ref), custom_call_target="tpu_custom_call" | custom-call | flops 301989888 | tf_op jit(solution)/shard_map/pallas_call | solution.py:172
  37.5 1.2 %all-to-all-done.3.parts_ref = bf16[8,32,1536]{2,1,0:T(8,128)(2,1)S(1)} async-done(((bf16[8,32,1536]{2,1,0:T(8,128)(2,1)}), bf16[8,32,1536]{2,1,0:T(8,128)(2,1)S(1)}, u32[]{:S(2)}, u32[]{:S(2)}) %all-to-all-start.3) | async-done | bytes 786464 | tf_op jit(solution)/shard_map/all_to_all | solution.py:156
  38.7 5.8 %all-to-all-start.1 = ((bf16[8,32,1536]{2,1,0:T(8,128)(2,1)}), bf16[8,32,1536]{2,1,0:T(8,128)(2,1)S(1)}, u32[]{:S(2)}, u32[]{:S(2)}) async-start(bf16[8,32,1536]{2,1,0:T(8,128)(2,1)} %shard_map.69), calls=%async_computation.1 | async-start | bytes 1572864 | tf_op jit(solution)/shard_map/all_to_all | solution.py:156
  44.5 0.1 shard_map.73
  44.6 2.2 %collective-permute-start.3 = (bf16[32,1536]{1,0:T(8,128)(2,1)S(1)}, bf16[32,1536]{1,0:T(8,128)(2,1)S(1)}, u32[]{:S(2)}, u32[]{:S(2)}) collective-permute-start(bf16[32,1536]{1,0:T(8,128)(2,1)S(1)} %get-tuple-element.16), channel_id=1, source_target_pairs={{0,256},{32,288},{64,320},{96,352},{128,384},{160,416},{192,448},{... | collective-permute-start | bytes 294920 | tf_op jit(solution)/shard_map/ppermute | solution.py:159
  46.8 0.1 pad_add_fusion.1.where_ref
  46.9 6.9 %collective-permute-done.3.came_ref = bf16[32,1536]{1,0:T(8,128)(2,1)S(1)} collective-permute-done((bf16[32,1536]{1,0:T(8,128)(2,1)S(1)}, bf16[32,1536]{1,0:T(8,128)(2,1)S(1)}, u32[]{:S(2)}, u32[]{:S(2)}) %collective-permute-start.3) | collective-permute-done | bytes 98336 | tf_op jit(solution)/shard_map/ppermute | solution.py:159
  53.8 1.6 %shard_map.74 = bf16[8,32,1536]{2,1,0:T(8,128)(2,1)} custom-call(s32[2]{0:T(128)S(1)} %pad_add_fusion.1.where_ref, f32[32,1536]{1,0:T(8,128)S(1)} %get-tuple-element.15.keep_ref, bf16[32,1536]{1,0:T(8,128)(2,1)S(1)} %collective-permute-done.3.came_ref, bf16[32,768]{1,0:T(8,128)(2,1)S(1)} %copy-done.3, bf16[32,768]{1,0:T(8,128)(2,1)S(1)} %collective-permute-done.1._.far_cot_ref), custom_call_target="tpu_custom_call" | custom-call | tf_op jit(solution)/shard_map/pallas_call | solution.py:180
  55.4 2.0 %all-to-all-done.1.parts_ref = bf16[8,32,1536]{2,1,0:T(8,128)(2,1)S(1)} async-done(((bf16[8,32,1536]{2,1,0:T(8,128)(2,1)}), bf16[8,32,1536]{2,1,0:T(8,128)(2,1)S(1)}, u32[]{:S(2)}, u32[]{:S(2)}) %all-to-all-start.1) | async-done | bytes 786464 | tf_op jit(solution)/shard_map/all_to_all | solution.py:156
  57.4 5.1 %all-to-all-start.4 = ((bf16[8,32,1536]{2,1,0:T(8,128)(2,1)}), bf16[8,32,1536]{2,1,0:T(8,128)(2,1)S(1)}, u32[]{:S(2)}, u32[]{:S(2)}) async-start(bf16[8,32,1536]{2,1,0:T(8,128)(2,1)} %shard_map.74), calls=%async_computation.4 | async-start | bytes 1572864 | tf_op jit(solution)/shard_map/all_to_all | solution.py:156
  62.5 0.1 shard_map.70
  62.6 2.7 %collective-permute-start.2 = (bf16[32,1536]{1,0:T(8,128)(2,1)S(1)}, bf16[32,1536]{1,0:T(8,128)(2,1)S(1)}, u32[]{:S(2)}, u32[]{:S(2)}) collective-permute-start(bf16[32,1536]{1,0:T(8,128)(2,1)S(1)} %get-tuple-element.14), channel_id=1, source_target_pairs={{0,256},{32,288},{64,320},{96,352},{128,384},{160,416},{192,448},{... | collective-permute-start | bytes 294920 | tf_op jit(solution)/shard_map/ppermute | solution.py:159
  65.3 0.1 pad_add_fusion.where_ref
  65.4 5.9 %collective-permute-done.2.came_ref = bf16[32,1536]{1,0:T(8,128)(2,1)S(1)} collective-permute-done((bf16[32,1536]{1,0:T(8,128)(2,1)S(1)}, bf16[32,1536]{1,0:T(8,128)(2,1)S(1)}, u32[]{:S(2)}, u32[]{:S(2)}) %collective-permute-start.2) | collective-permute-done | bytes 98336 | tf_op jit(solution)/shard_map/ppermute | solution.py:159
  71.3 1.5 %shard_map.71 = bf16[8,32,1536]{2,1,0:T(8,128)(2,1)} custom-call(s32[2]{0:T(128)S(1)} %pad_add_fusion.where_ref, f32[32,1536]{1,0:T(8,128)S(1)} %get-tuple-element.13.keep_ref, bf16[32,1536]{1,0:T(8,128)(2,1)S(1)} %collective-permute-done.2.came_ref, bf16[32,768]{1,0:T(8,128)(2,1)S(1)} %copy-done.3, bf16[32,768]{1,0:T(8,128)(2,1)S(1)} %collective-permute-done.1._.far_cot_ref), custom_call_target="tpu_custom_call" | custom-call | tf_op jit(solution)/shard_map/pallas_call | solution.py:180
  72.8 2.0 %all-to-all-done.4.d_ref.d_far_ref = bf16[8,32,1536]{2,1,0:T(8,128)(2,1)S(1)} async-done(((bf16[8,32,1536]{2,1,0:T(8,128)(2,1)}), bf16[8,32,1536]{2,1,0:T(8,128)(2,1)S(1)}, u32[]{:S(2)}, u32[]{:S(2)}) %all-to-all-start.4) | async-done | bytes 786464 | tf_op jit(solution)/shard_map/all_to_all | solution.py:156
  74.8 4.1 %all-to-all-start.2 = ((bf16[8,32,1536]{2,1,0:T(8,128)(2,1)}), bf16[8,32,1536]{2,1,0:T(8,128)(2,1)S(1)}, u32[]{:S(2)}, u32[]{:S(2)}) async-start(bf16[8,32,1536]{2,1,0:T(8,128)(2,1)} %shard_map.71), calls=%async_computation.2 | async-start | bytes 1572864 | tf_op jit(solution)/shard_map/all_to_all | solution.py:156
  78.9 1.3 %shard_map.75 = f32[256,384]{1,0:T(8,128)} custom-call(bf16[8,32,1536]{2,1,0:T(8,128)(2,1)S(1)} %all-to-all-done.4.d_ref.d_far_ref, bf16[384,768]{1,0:T(8,128)(2,1)S(1)} %get-tuple-element.11.gate_ref, bf16[384,768]{1,0:T(8,128)(2,1)S(1)} %get-tuple-element.12.up_ref), custom_call_target="tpu_custom_call" | custom-call | flops 301989888 | tf_op jit(solution)/shard_map/pallas_call | solution.py:185
  80.2 1.9 %collective-permute-start.4 = (f32[256,384]{1,0:T(8,128)}, f32[256,384]{1,0:T(8,128)S(1)}, u32[]{:S(2)}, u32[]{:S(2)}) collective-permute-start(f32[256,384]{1,0:T(8,128)} %shard_map.75), channel_id=1, source_target_pairs={{0,1},{1,0},{2,3},{3,2},{4,5},{5,4},{6,7},{7,6},{8,9},{9,8},{10,11... | collective-permute-start | bytes 1179656 | tf_op jit(solution)/shard_map/ppermute | solution.py:159
  82.1 6.2 %all-to-all-done.2.d_ref.d_near_ref = bf16[8,32,1536]{2,1,0:T(8,128)(2,1)S(1)} async-done(((bf16[8,32,1536]{2,1,0:T(8,128)(2,1)}), bf16[8,32,1536]{2,1,0:T(8,128)(2,1)S(1)}, u32[]{:S(2)}, u32[]{:S(2)}) %all-to-all-start.2) | async-done | bytes 786464 | tf_op jit(solution)/shard_map/all_to_all | solution.py:156
  88.3 0.0 collective-permute-done.4.came_ref
  88.3 1.3 %shard_map.76 = bf16[16,16,384]{2,1,0:T(8,128)(2,1)} custom-call(bf16[8,32,1536]{2,1,0:T(8,128)(2,1)S(1)} %all-to-all-done.2.d_ref.d_near_ref, bf16[384,768]{1,0:T(8,128)(2,1)S(1)} %get-tuple-element.11.gate_ref, bf16[384,768]{1,0:T(8,128)(2,1)S(1)} %get-tuple-element.12.up_ref, f32[256,384]{1,0:T(8,128)S(1)} %collective-permute-done.4.came_ref), custom_call_target="tpu_custom_call" | custom-call | flops 301989888 | tf_op jit(solution)/shard_map/pallas_call | solution.py:189
  89.6 13.3 %all-to-all-start.5 = ((bf16[16,16,384]{2,1,0:T(8,128)(2,1)}), bf16[16,16,384]{2,1,0:T(8,128)(2,1)S(1)}, u32[]{:S(2)}, u32[]{:S(2)}) async-start(bf16[16,16,384]{2,1,0:T(8,128)(2,1)} %shard_map.76), calls=%async_computation.5 | async-start | bytes 393216 | tf_op jit(solution)/shard_map/all_to_all | solution.py:156
  102.9 1.6 %shard_map.77 = (bf16[384,768]{1,0:T(8,128)(2,1)}, bf16[384,768]{1,0:T(8,128)(2,1)}) custom-call(bf16[16,16,384]{2,1,0:T(8,128)(2,1)S(1)} %all-to-all-done.tokens_ref.far_ref, bf16[16,16,384]{2,1,0:T(8,128)(2,1)S(1)} %collective-permute-done.tokens_ref.near_ref, bf16[8,32,1536]{2,1,0:T(8,128)(2,1)S(1)} %all-to-all-done.4.d_ref.d_far_ref, ...), custom_call_target="tpu_custom_call" | custom-call | flops 603979776 | tf_op jit(solution)/shard_map/pallas_call | solution.py:195
  104.6 10.8 %all-to-all-done.5 = bf16[16,16,384]{2,1,0:T(8,128)(2,1)S(1)} async-done(((bf16[16,16,384]{2,1,0:T(8,128)(2,1)}), bf16[16,16,384]{2,1,0:T(8,128)(2,1)S(1)}, u32[]{:S(2)}, u32[]{:S(2)}) %all-to-all-start.5) | async-done | bytes 196640 | tf_op jit(solution)/shard_map/all_to_all | solution.py:156
  115.4 0.6 reduce_sum.12
Async XLA Ops:
  0.6 11.6 %copy-start = (bf16[384,768]{1,0:T(8,128)(2,1)S(1)}, bf16[384,768]{1,0:T(8,128)(2,1)}, u32[]{:S(2)}) copy-start(bf16[384,768]{1,0:T(8,128)(2,1)} %gate_ref.1) | copy-start | bytes 1769476
  0.7 1.1 copy-start.2
  2.4 19.5 %all-to-all-start = ((bf16[16,16,384]{2,1,0:T(8,128)(2,1)}), bf16[16,16,384]{2,1,0:T(8,128)(2,1)S(1)}, u32[]{:S(2)}, u32[]{:S(2)}) async-start(bf16[16,16,384]{2,1,0:T(8,128)(2,1)} %shard_map.67), calls=%async_computation | async-start | bytes 393216 | tf_op jit(solution)/shard_map/all_to_all | solution.py:156
  12.3 1.1 copy-start.1
  23.3 5.6 %copy-start.3 = (bf16[32,768]{1,0:T(8,128)(2,1)S(1)}, bf16[32,768]{1,0:T(8,128)(2,1)}, u32[]{:S(2)}) copy-start(bf16[32,768]{1,0:T(8,128)(2,1)} %cot_ref.3) | copy-start | bytes 147460
  23.3 15.4 %all-to-all-start.3 = ((bf16[8,32,1536]{2,1,0:T(8,128)(2,1)}), bf16[8,32,1536]{2,1,0:T(8,128)(2,1)S(1)}, u32[]{:S(2)}, u32[]{:S(2)}) async-start(bf16[8,32,1536]{2,1,0:T(8,128)(2,1)} %shard_map.72), calls=%async_computation.3 | async-start | bytes 1572864 | tf_op jit(solution)/shard_map/all_to_all | solution.py:156
  27.0 9.0 %collective-permute-start = (bf16[16,16,384]{2,1,0:T(8,128)(2,1)S(1)}, bf16[16,16,384]{2,1,0:T(8,128)(2,1)S(1)}, u32[]{:S(2)}, u32[]{:S(2)}) collective-permute-start(bf16[16,16,384]{2,1,0:T(8,128)(2,1)S(1)} %all-to-all-done.tokens_ref.far_ref), channel_id=1, source_target_pairs={{0,1},{1,0},{2,3},{3,2},{4,5},{5,4},{6,7},{7,6},{8,9},{9,8},{10,11... | collective-permute-start | bytes 589832 | tf_op jit(solution)/shard_map/ppermute | solution.py:159
  29.0 7.0 %collective-permute-start.1 = (bf16[32,768]{1,0:T(8,128)(2,1)S(1)}, bf16[32,768]{1,0:T(8,128)(2,1)S(1)}, u32[]{:S(2)}, u32[]{:S(2)}) collective-permute-start(bf16[32,768]{1,0:T(8,128)(2,1)S(1)} %copy-done.3), channel_id=1, source_target_pairs={{0,256},{32,288},{64,320},{96,352},{128,384},{160,416},{192,448},{... | collective-permute-start | bytes 147464 | tf_op jit(solution)/shard_map/ppermute | solution.py:159
  38.7 18.7 %all-to-all-start.1 = ((bf16[8,32,1536]{2,1,0:T(8,128)(2,1)}), bf16[8,32,1536]{2,1,0:T(8,128)(2,1)S(1)}, u32[]{:S(2)}, u32[]{:S(2)}) async-start(bf16[8,32,1536]{2,1,0:T(8,128)(2,1)} %shard_map.69), calls=%async_computation.1 | async-start | bytes 1572864 | tf_op jit(solution)/shard_map/all_to_all | solution.py:156
  44.6 9.2 %collective-permute-start.3 = (bf16[32,1536]{1,0:T(8,128)(2,1)S(1)}, bf16[32,1536]{1,0:T(8,128)(2,1)S(1)}, u32[]{:S(2)}, u32[]{:S(2)}) collective-permute-start(bf16[32,1536]{1,0:T(8,128)(2,1)S(1)} %get-tuple-element.16), channel_id=1, source_target_pairs={{0,256},{32,288},{64,320},{96,352},{128,384},{160,416},{192,448},{... | collective-permute-start | bytes 294920 | tf_op jit(solution)/shard_map/ppermute | solution.py:159
  57.4 17.4 %all-to-all-start.4 = ((bf16[8,32,1536]{2,1,0:T(8,128)(2,1)}), bf16[8,32,1536]{2,1,0:T(8,128)(2,1)S(1)}, u32[]{:S(2)}, u32[]{:S(2)}) async-start(bf16[8,32,1536]{2,1,0:T(8,128)(2,1)} %shard_map.74), calls=%async_computation.4 | async-start | bytes 1572864 | tf_op jit(solution)/shard_map/all_to_all | solution.py:156
  62.6 8.7 %collective-permute-start.2 = (bf16[32,1536]{1,0:T(8,128)(2,1)S(1)}, bf16[32,1536]{1,0:T(8,128)(2,1)S(1)}, u32[]{:S(2)}, u32[]{:S(2)}) collective-permute-start(bf16[32,1536]{1,0:T(8,128)(2,1)S(1)} %get-tuple-element.14), channel_id=1, source_target_pairs={{0,256},{32,288},{64,320},{96,352},{128,384},{160,416},{192,448},{... | collective-permute-start | bytes 294920 | tf_op jit(solution)/shard_map/ppermute | solution.py:159
  74.8 13.5 %all-to-all-start.2 = ((bf16[8,32,1536]{2,1,0:T(8,128)(2,1)}), bf16[8,32,1536]{2,1,0:T(8,128)(2,1)S(1)}, u32[]{:S(2)}, u32[]{:S(2)}) async-start(bf16[8,32,1536]{2,1,0:T(8,128)(2,1)} %shard_map.71), calls=%async_computation.2 | async-start | bytes 1572864 | tf_op jit(solution)/shard_map/all_to_all | solution.py:156
  80.2 8.2 %collective-permute-start.4 = (f32[256,384]{1,0:T(8,128)}, f32[256,384]{1,0:T(8,128)S(1)}, u32[]{:S(2)}, u32[]{:S(2)}) collective-permute-start(f32[256,384]{1,0:T(8,128)} %shard_map.75), channel_id=1, source_target_pairs={{0,1},{1,0},{2,3},{3,2},{4,5},{5,4},{6,7},{7,6},{8,9},{9,8},{10,11... | collective-permute-start | bytes 1179656 | tf_op jit(solution)/shard_map/ppermute | solution.py:159
  89.6 25.8 %all-to-all-start.5 = ((bf16[16,16,384]{2,1,0:T(8,128)(2,1)}), bf16[16,16,384]{2,1,0:T(8,128)(2,1)S(1)}, u32[]{:S(2)}, u32[]{:S(2)}) async-start(bf16[16,16,384]{2,1,0:T(8,128)(2,1)} %shard_map.76), calls=%async_computation.5 | async-start | bytes 393216 | tf_op jit(solution)/shard_map/all_to_all | solution.py:156

commit v7 on v6

--- a/solution.py
+++ b/solution.py
@@ -8,6 +8,7 @@
 from jax.sharding import PartitionSpec as P
 
 GROUP = 8
+ORDER = (0, 4, 1, 5, 2, 6, 3, 7)
 VMEM_BYTES = 40 * 1024 * 1024
 
 VMEM = pl.BlockSpec(memory_space=pltpu.VMEM)
@@ -40,7 +41,7 @@
         total = jnp.dot(tokens, weight_ref[...], preferred_element_type=F32).astype(BF16)
         for row in range(rows):
             side, m = divmod(row, GROUP)
-            out_ref[m, side * part : (side + 1) * part, i * hidden : (i + 1) * hidden] = total[
+            out_ref[ORDER.index(m), side * part : (side + 1) * part, i * hidden : (i + 1) * hidden] = total[
                 row * part : (row + 1) * part
             ]
 
@@ -74,7 +75,7 @@
     part = d_ref.shape[1] // 2
     return jnp.concatenate(
         [
-            d_ref[m, side * part : (side + 1) * part, :]
+            d_ref[ORDER.index(m), side * part : (side + 1) * part, :]
             for side in range(2)
             for m in range(GROUP)
         ],
@@ -139,7 +140,7 @@
     part = inputs.shape[0] // 2
     wide = 2 * hidden
     flops = 2 * rows * part * depth * wide
-    pairs = [list(range(0, GROUP)), list(range(GROUP, 2 * GROUP))]
+    pairs = [[start + m for m in ORDER] for start in (0, GROUP)]
     core_groups = [[2 * r + core for r in by_z_hi(rows)] for core in range(2)]
     row, col = lax.axis_index("row"), lax.axis_index("col")
 

time: 117 us -> 118 us (level)
  waiting for transfers between devices: 48 us -> 51 us
  starting transfers between devices: 53.1 us -> 50.8 us
    all_to_all x6, waiting for transfers between devices: 30.7 us -> 33.9 us  [exchange(): return lax.all_to_all(array, axis, 0, 0, axis_index_groups=groups)]
    all_to_all x6, starting transfers between devices: 41.8 us -> 39.4 us  [exchange(): return lax.all_to_all(array, axis, 0, 0, axis_index_groups=groups)]
where the time goes in v7:
time: 118 us; the launch traced here: 117 us
  waiting for transfers between devices  51 us (43%)
  starting transfers between devices  50.8 us (43%)
  Pallas kernels  11.3 us (10%)
  local copies, waits for them, and re-layouts  2.11 us (2%)
    all_to_all x6, starting transfers between devices, exchange(): return lax.all_to_all(array, axis, 0, 0, axis_index_groups=groups)  39.4 us
    all_to_all x6, waiting for transfers between devices, exchange(): return lax.all_to_all(array, axis, 0, 0, axis_index_groups=groups)  33.9 us
    ppermute x5, waiting for transfers between devices, swap(): return lax.ppermute(array, axis, [(i, i ^ bit) for i in range(count)])  17.1 us
    ppermute x5, starting transfers between devices, swap(): return lax.ppermute(array, axis, [(i, i ^ bit) for i in range(count)])  11.4 us
    pallas_call x2, Pallas kernels, shards(): call(act_kernel, shape((GROUP, 2 * part, wide)), 1, 4)  3.12 us
    pallas_call x2, Pallas kernels, shards(): call(forward_kernel, shape((GROUP, 2 * part, wide)), 0, 3, flops, n_any=1)  2.95 us
  transfers between devices with their start and end apart: 11, of which 9 were waited for; matrix products, arithmetic and copies ran while one was open for 0% of the time, Pallas kernels for 7%

profile of v7, /device:TPU:8, one launch (start us, length us, event | category | flops | bytes accessed | tf_op | source)
XLA Modules:
  0.0 116.8 jit_solution(2332943243299753803)
XLA Ops:
  0.6 0.0 copy-start
  0.7 0.0 copy-start.2
  0.7 1.0 copy-done.2
  1.7 0.7 shard_map.67
  2.4 9.8 %all-to-all-start = ((bf16[16,16,384]{2,1,0:T(8,128)(2,1)}), bf16[16,16,384]{2,1,0:T(8,128)(2,1)S(1)}, u32[]{:S(2)}, u32[]{:S(2)}) async-start(bf16[16,16,384]{2,1,0:T(8,128)(2,1)} %shard_map.67), calls=%async_computation | async-start | bytes 393216 | tf_op jit(solution)/shard_map/all_to_all | solution.py:157
  12.3 0.0 copy-done
  12.3 0.0 copy-start.1
  12.3 1.1 copy-done.1
  13.3 0.1 shard_map.68
  13.4 8.5 %all-to-all-done.tokens_ref.far_ref = bf16[16,16,384]{2,1,0:T(8,128)(2,1)S(1)} async-done(((bf16[16,16,384]{2,1,0:T(8,128)(2,1)}), bf16[16,16,384]{2,1,0:T(8,128)(2,1)S(1)}, u32[]{:S(2)}, u32[]{:S(2)}) %all-to-all-start) | async-done | bytes 196640 | tf_op jit(solution)/shard_map/all_to_all | solution.py:157
  21.9 1.5 %shard_map.72 = bf16[8,32,1536]{2,1,0:T(8,128)(2,1)} custom-call(bf16[16,16,384]{2,1,0:T(8,128)(2,1)S(1)} %all-to-all-done.tokens_ref.far_ref, bf16[384,768]{1,0:T(8,128)(2,1)S(1)} %get-tuple-element.11.gate_ref, bf16[384,768]{1,0:T(8,128)(2,1)S(1)} %get-tuple-element.12.up_ref, s32[1]{0:T(128)} %bitcast._), custom_call_target="tpu_custom_call" | custom-call | flops 301989888 | tf_op jit(solution)/shard_map/pallas_call | solution.py:173
  23.3 0.0 copy-start.3
  23.3 3.7 %all-to-all-start.3 = ((bf16[8,32,1536]{2,1,0:T(8,128)(2,1)}), bf16[8,32,1536]{2,1,0:T(8,128)(2,1)S(1)}, u32[]{:S(2)}, u32[]{:S(2)}) async-start(bf16[8,32,1536]{2,1,0:T(8,128)(2,1)} %shard_map.72), calls=%async_computation.3 | async-start | bytes 1572864 | tf_op jit(solution)/shard_map/all_to_all | solution.py:157
  27.0 1.9 %collective-permute-start = (bf16[16,16,384]{2,1,0:T(8,128)(2,1)S(1)}, bf16[16,16,384]{2,1,0:T(8,128)(2,1)S(1)}, u32[]{:S(2)}, u32[]{:S(2)}) collective-permute-start(bf16[16,16,384]{2,1,0:T(8,128)(2,1)S(1)} %all-to-all-done.tokens_ref.far_ref), channel_id=1, source_target_pairs={{0,1},{1,0},{2,3},{3,2},{4,5},{5,4},{6,7},{7,6},{8,9},{9,8},{10,11... | collective-permute-start | bytes 589832 | tf_op jit(solution)/shard_map/ppermute | solution.py:160
  29.0 0.0 copy-done.3
  29.0 2.6 %collective-permute-start.1 = (bf16[32,768]{1,0:T(8,128)(2,1)S(1)}, bf16[32,768]{1,0:T(8,128)(2,1)S(1)}, u32[]{:S(2)}, u32[]{:S(2)}) collective-permute-start(bf16[32,768]{1,0:T(8,128)(2,1)S(1)} %copy-done.3), channel_id=1, source_target_pairs={{0,256},{32,288},{64,320},{96,352},{128,384},{160,416},{192,448},{... | collective-permute-start | bytes 147464 | tf_op jit(solution)/shard_map/ppermute | solution.py:160
  31.6 4.4 %collective-permute-done.1._.far_cot_ref = bf16[32,768]{1,0:T(8,128)(2,1)S(1)} collective-permute-done((bf16[32,768]{1,0:T(8,128)(2,1)S(1)}, bf16[32,768]{1,0:T(8,128)(2,1)S(1)}, u32[]{:S(2)}, u32[]{:S(2)}) %collective-permute-start.1) | collective-permute-done | bytes 49184 | tf_op jit(solution)/shard_map/ppermute | solution.py:160
  36.0 0.0 collective-permute-done.tokens_ref.near_ref
  36.0 1.5 %shard_map.69 = bf16[8,32,1536]{2,1,0:T(8,128)(2,1)} custom-call(bf16[16,16,384]{2,1,0:T(8,128)(2,1)S(1)} %collective-permute-done.tokens_ref.near_ref, bf16[384,768]{1,0:T(8,128)(2,1)S(1)} %get-tuple-element.11.gate_ref, bf16[384,768]{1,0:T(8,128)(2,1)S(1)} %get-tuple-element.12.up_ref, bf16[32,768]{1,0:T(8,128)(2,1)S(1)} %collective-permute-done.1._.far_cot_ref), custom_call_target="tpu_custom_call" | custom-call | flops 301989888 | tf_op jit(solution)/shard_map/pallas_call | solution.py:173
  37.5 2.3 %all-to-all-done.3.parts_ref = bf16[8,32,1536]{2,1,0:T(8,128)(2,1)S(1)} async-done(((bf16[8,32,1536]{2,1,0:T(8,128)(2,1)}), bf16[8,32,1536]{2,1,0:T(8,128)(2,1)S(1)}, u32[]{:S(2)}, u32[]{:S(2)}) %all-to-all-start.3) | async-done | bytes 786464 | tf_op jit(solution)/shard_map/all_to_all | solution.py:157
  39.8 4.7 %all-to-all-start.1 = ((bf16[8,32,1536]{2,1,0:T(8,128)(2,1)}), bf16[8,32,1536]{2,1,0:T(8,128)(2,1)S(1)}, u32[]{:S(2)}, u32[]{:S(2)}) async-start(bf16[8,32,1536]{2,1,0:T(8,128)(2,1)} %shard_map.69), calls=%async_computation.1 | async-start | bytes 1572864 | tf_op jit(solution)/shard_map/all_to_all | solution.py:157
  44.5 0.1 shard_map.73
  44.6 2.2 %collective-permute-start.3 = (bf16[32,1536]{1,0:T(8,128)(2,1)S(1)}, bf16[32,1536]{1,0:T(8,128)(2,1)S(1)}, u32[]{:S(2)}, u32[]{:S(2)}) collective-permute-start(bf16[32,1536]{1,0:T(8,128)(2,1)S(1)} %get-tuple-element.16), channel_id=1, source_target_pairs={{0,256},{32,288},{64,320},{96,352},{128,384},{160,416},{192,448},{... | collective-permute-start | bytes 294920 | tf_op jit(solution)/shard_map/ppermute | solution.py:160
  46.8 0.1 pad_add_fusion.1.where_ref
  46.9 6.9 %collective-permute-done.3.came_ref = bf16[32,1536]{1,0:T(8,128)(2,1)S(1)} collective-permute-done((bf16[32,1536]{1,0:T(8,128)(2,1)S(1)}, bf16[32,1536]{1,0:T(8,128)(2,1)S(1)}, u32[]{:S(2)}, u32[]{:S(2)}) %collective-permute-start.3) | collective-permute-done | bytes 98336 | tf_op jit(solution)/shard_map/ppermute | solution.py:160
  53.8 1.6 %shard_map.74 = bf16[8,32,1536]{2,1,0:T(8,128)(2,1)} custom-call(s32[2]{0:T(128)S(1)} %pad_add_fusion.1.where_ref, f32[32,1536]{1,0:T(8,128)S(1)} %get-tuple-element.15.keep_ref, bf16[32,1536]{1,0:T(8,128)(2,1)S(1)} %collective-permute-done.3.came_ref, bf16[32,768]{1,0:T(8,128)(2,1)S(1)} %copy-done.3, bf16[32,768]{1,0:T(8,128)(2,1)S(1)} %collective-permute-done.1._.far_cot_ref), custom_call_target="tpu_custom_call" | custom-call | tf_op jit(solution)/shard_map/pallas_call | solution.py:181
  55.4 2.7 %all-to-all-done.1.parts_ref = bf16[8,32,1536]{2,1,0:T(8,128)(2,1)S(1)} async-done(((bf16[8,32,1536]{2,1,0:T(8,128)(2,1)}), bf16[8,32,1536]{2,1,0:T(8,128)(2,1)S(1)}, u32[]{:S(2)}, u32[]{:S(2)}) %all-to-all-start.1) | async-done | bytes 786464 | tf_op jit(solution)/shard_map/all_to_all | solution.py:157
  58.1 4.4 %all-to-all-start.4 = ((bf16[8,32,1536]{2,1,0:T(8,128)(2,1)}), bf16[8,32,1536]{2,1,0:T(8,128)(2,1)S(1)}, u32[]{:S(2)}, u32[]{:S(2)}) async-start(bf16[8,32,1536]{2,1,0:T(8,128)(2,1)} %shard_map.74), calls=%async_computation.4 | async-start | bytes 1572864 | tf_op jit(solution)/shard_map/all_to_all | solution.py:157
  62.5 0.1 shard_map.70
  62.6 2.7 %collective-permute-start.2 = (bf16[32,1536]{1,0:T(8,128)(2,1)S(1)}, bf16[32,1536]{1,0:T(8,128)(2,1)S(1)}, u32[]{:S(2)}, u32[]{:S(2)}) collective-permute-start(bf16[32,1536]{1,0:T(8,128)(2,1)S(1)} %get-tuple-element.14), channel_id=1, source_target_pairs={{0,256},{32,288},{64,320},{96,352},{128,384},{160,416},{192,448},{... | collective-permute-start | bytes 294920 | tf_op jit(solution)/shard_map/ppermute | solution.py:160
  65.3 0.1 pad_add_fusion.where_ref
  65.4 5.8 %collective-permute-done.2.came_ref = bf16[32,1536]{1,0:T(8,128)(2,1)S(1)} collective-permute-done((bf16[32,1536]{1,0:T(8,128)(2,1)S(1)}, bf16[32,1536]{1,0:T(8,128)(2,1)S(1)}, u32[]{:S(2)}, u32[]{:S(2)}) %collective-permute-start.2) | collective-permute-done | bytes 98336 | tf_op jit(solution)/shard_map/ppermute | solution.py:160
  71.2 1.5 %shard_map.71 = bf16[8,32,1536]{2,1,0:T(8,128)(2,1)} custom-call(s32[2]{0:T(128)S(1)} %pad_add_fusion.where_ref, f32[32,1536]{1,0:T(8,128)S(1)} %get-tuple-element.13.keep_ref, bf16[32,1536]{1,0:T(8,128)(2,1)S(1)} %collective-permute-done.2.came_ref, bf16[32,768]{1,0:T(8,128)(2,1)S(1)} %copy-done.3, bf16[32,768]{1,0:T(8,128)(2,1)S(1)} %collective-permute-done.1._.far_cot_ref), custom_call_target="tpu_custom_call" | custom-call | tf_op jit(solution)/shard_map/pallas_call | solution.py:181
  72.7 2.7 %all-to-all-done.4.d_ref.d_far_ref = bf16[8,32,1536]{2,1,0:T(8,128)(2,1)S(1)} async-done(((bf16[8,32,1536]{2,1,0:T(8,128)(2,1)}), bf16[8,32,1536]{2,1,0:T(8,128)(2,1)S(1)}, u32[]{:S(2)}, u32[]{:S(2)}) %all-to-all-start.4) | async-done | bytes 786464 | tf_op jit(solution)/shard_map/all_to_all | solution.py:157
  75.5 3.5 %all-to-all-start.2 = ((bf16[8,32,1536]{2,1,0:T(8,128)(2,1)}), bf16[8,32,1536]{2,1,0:T(8,128)(2,1)S(1)}, u32[]{:S(2)}, u32[]{:S(2)}) async-start(bf16[8,32,1536]{2,1,0:T(8,128)(2,1)} %shard_map.71), calls=%async_computation.2 | async-start | bytes 1572864 | tf_op jit(solution)/shard_map/all_to_all | solution.py:157
  79.0 1.3 %shard_map.75 = f32[256,384]{1,0:T(8,128)} custom-call(bf16[8,32,1536]{2,1,0:T(8,128)(2,1)S(1)} %all-to-all-done.4.d_ref.d_far_ref, bf16[384,768]{1,0:T(8,128)(2,1)S(1)} %get-tuple-element.11.gate_ref, bf16[384,768]{1,0:T(8,128)(2,1)S(1)} %get-tuple-element.12.up_ref), custom_call_target="tpu_custom_call" | custom-call | flops 301989888 | tf_op jit(solution)/shard_map/pallas_call | solution.py:186
  80.4 1.9 %collective-permute-start.4 = (f32[256,384]{1,0:T(8,128)}, f32[256,384]{1,0:T(8,128)S(1)}, u32[]{:S(2)}, u32[]{:S(2)}) collective-permute-start(f32[256,384]{1,0:T(8,128)} %shard_map.75), channel_id=1, source_target_pairs={{0,1},{1,0},{2,3},{3,2},{4,5},{5,4},{6,7},{7,6},{8,9},{9,8},{10,11... | collective-permute-start | bytes 1179656 | tf_op jit(solution)/shard_map/ppermute | solution.py:160
  82.3 6.8 %all-to-all-done.2.d_ref.d_near_ref = bf16[8,32,1536]{2,1,0:T(8,128)(2,1)S(1)} async-done(((bf16[8,32,1536]{2,1,0:T(8,128)(2,1)}), bf16[8,32,1536]{2,1,0:T(8,128)(2,1)S(1)}, u32[]{:S(2)}, u32[]{:S(2)}) %all-to-all-start.2) | async-done | bytes 786464 | tf_op jit(solution)/shard_map/all_to_all | solution.py:157
  89.1 0.0 collective-permute-done.4.came_ref
  89.1 1.3 %shard_map.76 = bf16[16,16,384]{2,1,0:T(8,128)(2,1)} custom-call(bf16[8,32,1536]{2,1,0:T(8,128)(2,1)S(1)} %all-to-all-done.2.d_ref.d_near_ref, bf16[384,768]{1,0:T(8,128)(2,1)S(1)} %get-tuple-element.11.gate_ref, bf16[384,768]{1,0:T(8,128)(2,1)S(1)} %get-tuple-element.12.up_ref, f32[256,384]{1,0:T(8,128)S(1)} %collective-permute-done.4.came_ref), custom_call_target="tpu_custom_call" | custom-call | flops 301989888 | tf_op jit(solution)/shard_map/pallas_call | solution.py:190
  90.4 13.3 %all-to-all-start.5 = ((bf16[16,16,384]{2,1,0:T(8,128)(2,1)}), bf16[16,16,384]{2,1,0:T(8,128)(2,1)S(1)}, u32[]{:S(2)}, u32[]{:S(2)}) async-start(bf16[16,16,384]{2,1,0:T(8,128)(2,1)} %shard_map.76), calls=%async_computation.5 | async-start | bytes 393216 | tf_op jit(solution)/shard_map/all_to_all | solution.py:157
  103.7 1.6 %shard_map.77 = (bf16[384,768]{1,0:T(8,128)(2,1)}, bf16[384,768]{1,0:T(8,128)(2,1)}) custom-call(bf16[16,16,384]{2,1,0:T(8,128)(2,1)S(1)} %all-to-all-done.tokens_ref.far_ref, bf16[16,16,384]{2,1,0:T(8,128)(2,1)S(1)} %collective-permute-done.tokens_ref.near_ref, bf16[8,32,1536]{2,1,0:T(8,128)(2,1)S(1)} %all-to-all-done.4.d_ref.d_far_ref, ...), custom_call_target="tpu_custom_call" | custom-call | flops 603979776 | tf_op jit(solution)/shard_map/pallas_call | solution.py:196
  105.3 10.8 %all-to-all-done.5 = bf16[16,16,384]{2,1,0:T(8,128)(2,1)S(1)} async-done(((bf16[16,16,384]{2,1,0:T(8,128)(2,1)}), bf16[16,16,384]{2,1,0:T(8,128)(2,1)S(1)}, u32[]{:S(2)}, u32[]{:S(2)}) %all-to-all-start.5) | async-done | bytes 196640 | tf_op jit(solution)/shard_map/all_to_all | solution.py:157
  116.1 0.6 reduce_sum.12
Async XLA Ops:
  0.6 11.6 %copy-start = (bf16[384,768]{1,0:T(8,128)(2,1)S(1)}, bf16[384,768]{1,0:T(8,128)(2,1)}, u32[]{:S(2)}) copy-start(bf16[384,768]{1,0:T(8,128)(2,1)} %gate_ref.1) | copy-start | bytes 1769476
  0.7 1.1 copy-start.2
  2.4 19.5 %all-to-all-start = ((bf16[16,16,384]{2,1,0:T(8,128)(2,1)}), bf16[16,16,384]{2,1,0:T(8,128)(2,1)S(1)}, u32[]{:S(2)}, u32[]{:S(2)}) async-start(bf16[16,16,384]{2,1,0:T(8,128)(2,1)} %shard_map.67), calls=%async_computation | async-start | bytes 393216 | tf_op jit(solution)/shard_map/all_to_all | solution.py:157
  12.3 1.1 copy-start.1
  23.3 5.6 %copy-start.3 = (bf16[32,768]{1,0:T(8,128)(2,1)S(1)}, bf16[32,768]{1,0:T(8,128)(2,1)}, u32[]{:S(2)}) copy-start(bf16[32,768]{1,0:T(8,128)(2,1)} %cot_ref.3) | copy-start | bytes 147460
  23.3 16.5 %all-to-all-start.3 = ((bf16[8,32,1536]{2,1,0:T(8,128)(2,1)}), bf16[8,32,1536]{2,1,0:T(8,128)(2,1)S(1)}, u32[]{:S(2)}, u32[]{:S(2)}) async-start(bf16[8,32,1536]{2,1,0:T(8,128)(2,1)} %shard_map.72), calls=%async_computation.3 | async-start | bytes 1572864 | tf_op jit(solution)/shard_map/all_to_all | solution.py:157
  27.0 9.0 %collective-permute-start = (bf16[16,16,384]{2,1,0:T(8,128)(2,1)S(1)}, bf16[16,16,384]{2,1,0:T(8,128)(2,1)S(1)}, u32[]{:S(2)}, u32[]{:S(2)}) collective-permute-start(bf16[16,16,384]{2,1,0:T(8,128)(2,1)S(1)} %all-to-all-done.tokens_ref.far_ref), channel_id=1, source_target_pairs={{0,1},{1,0},{2,3},{3,2},{4,5},{5,4},{6,7},{7,6},{8,9},{9,8},{10,11... | collective-permute-start | bytes 589832 | tf_op jit(solution)/shard_map/ppermute | solution.py:160
  29.0 7.0 %collective-permute-start.1 = (bf16[32,768]{1,0:T(8,128)(2,1)S(1)}, bf16[32,768]{1,0:T(8,128)(2,1)S(1)}, u32[]{:S(2)}, u32[]{:S(2)}) collective-permute-start(bf16[32,768]{1,0:T(8,128)(2,1)S(1)} %copy-done.3), channel_id=1, source_target_pairs={{0,256},{32,288},{64,320},{96,352},{128,384},{160,416},{192,448},{... | collective-permute-start | bytes 147464 | tf_op jit(solution)/shard_map/ppermute | solution.py:160
  39.8 18.3 %all-to-all-start.1 = ((bf16[8,32,1536]{2,1,0:T(8,128)(2,1)}), bf16[8,32,1536]{2,1,0:T(8,128)(2,1)S(1)}, u32[]{:S(2)}, u32[]{:S(2)}) async-start(bf16[8,32,1536]{2,1,0:T(8,128)(2,1)} %shard_map.69), calls=%async_computation.1 | async-start | bytes 1572864 | tf_op jit(solution)/shard_map/all_to_all | solution.py:157
  44.6 9.2 %collective-permute-start.3 = (bf16[32,1536]{1,0:T(8,128)(2,1)S(1)}, bf16[32,1536]{1,0:T(8,128)(2,1)S(1)}, u32[]{:S(2)}, u32[]{:S(2)}) collective-permute-start(bf16[32,1536]{1,0:T(8,128)(2,1)S(1)} %get-tuple-element.16), channel_id=1, source_target_pairs={{0,256},{32,288},{64,320},{96,352},{128,384},{160,416},{192,448},{... | collective-permute-start | bytes 294920 | tf_op jit(solution)/shard_map/ppermute | solution.py:160
  58.1 17.4 %all-to-all-start.4 = ((bf16[8,32,1536]{2,1,0:T(8,128)(2,1)}), bf16[8,32,1536]{2,1,0:T(8,128)(2,1)S(1)}, u32[]{:S(2)}, u32[]{:S(2)}) async-start(bf16[8,32,1536]{2,1,0:T(8,128)(2,1)} %shard_map.74), calls=%async_computation.4 | async-start | bytes 1572864 | tf_op jit(solution)/shard_map/all_to_all | solution.py:157
  62.6 8.6 %collective-permute-start.2 = (bf16[32,1536]{1,0:T(8,128)(2,1)S(1)}, bf16[32,1536]{1,0:T(8,128)(2,1)S(1)}, u32[]{:S(2)}, u32[]{:S(2)}) collective-permute-start(bf16[32,1536]{1,0:T(8,128)(2,1)S(1)} %get-tuple-element.14), channel_id=1, source_target_pairs={{0,256},{32,288},{64,320},{96,352},{128,384},{160,416},{192,448},{... | collective-permute-start | bytes 294920 | tf_op jit(solution)/shard_map/ppermute | solution.py:160
  75.5 13.6 %all-to-all-start.2 = ((bf16[8,32,1536]{2,1,0:T(8,128)(2,1)}), bf16[8,32,1536]{2,1,0:T(8,128)(2,1)S(1)}, u32[]{:S(2)}, u32[]{:S(2)}) async-start(bf16[8,32,1536]{2,1,0:T(8,128)(2,1)} %shard_map.71), calls=%async_computation.2 | async-start | bytes 1572864 | tf_op jit(solution)/shard_map/all_to_all | solution.py:157
  80.4 8.7 %collective-permute-start.4 = (f32[256,384]{1,0:T(8,128)}, f32[256,384]{1,0:T(8,128)S(1)}, u32[]{:S(2)}, u32[]{:S(2)}) collective-permute-start(f32[256,384]{1,0:T(8,128)} %shard_map.75), channel_id=1, source_target_pairs={{0,1},{1,0},{2,3},{3,2},{4,5},{5,4},{6,7},{7,6},{8,9},{9,8},{10,11... | collective-permute-start | bytes 1179656 | tf_op jit(solution)/shard_map/ppermute | solution.py:160
  90.4 25.7 %all-to-all-start.5 = ((bf16[16,16,384]{2,1,0:T(8,128)(2,1)}), bf16[16,16,384]{2,1,0:T(8,128)(2,1)S(1)}, u32[]{:S(2)}, u32[]{:S(2)}) async-start(bf16[16,16,384]{2,1,0:T(8,128)(2,1)} %shard_map.76), calls=%async_computation.5 | async-start | bytes 393216 | tf_op jit(solution)/shard_map/all_to_all | solution.py:157

commit v8 on v6

--- a/solution.py
+++ b/solution.py
@@ -97,7 +97,7 @@
 
 
 def far_term_kernel(d_ref, gate_ref, up_ref, out_ref):
-    out_ref[...] = term_of(d_ref, gate_ref, up_ref)
+    out_ref[...] = term_of(d_ref, gate_ref, up_ref).astype(BF16)
 
 
 def by_z_hi(rows):
@@ -106,7 +106,7 @@
 
 def near_term_kernel(d_ref, gate_ref, up_ref, came_ref, out_ref):
     rows, part, _ = out_ref.shape
-    total = (term_of(d_ref, gate_ref, up_ref) + came_ref[...]).astype(BF16)
+    total = (term_of(d_ref, gate_ref, up_ref) + came_ref[...].astype(F32)).astype(BF16)
     for i, row in enumerate(by_z_hi(rows)):
         out_ref[i] = total[row * part : (row + 1) * part]
 
@@ -182,7 +182,7 @@
         )
         d[half] = exchange(copies, "row", pairs)
 
-    far_term = call(far_term_kernel, shape((rows * part, depth), F32), 0, 3, flops)(
+    far_term = call(far_term_kernel, shape((rows * part, depth)), 0, 3, flops)(
         d["far"], gate, up
     )
     came = swap(far_term, "col", cols, 1)

time: 117 us -> 117 us (level)
  no operation moved by 1% of the time
where the time goes in v8:
time: 117 us; the launch traced here: 116 us
  starting transfers between devices  53.1 us (45%)
  waiting for transfers between devices  48 us (41%)
  Pallas kernels  11.2 us (10%)
  local copies, waits for them, and re-layouts  2.11 us (2%)
    all_to_all x6, starting transfers between devices, exchange(): return lax.all_to_all(array, axis, 0, 0, axis_index_groups=groups)  41.8 us
    all_to_all x6, waiting for transfers between devices, exchange(): return lax.all_to_all(array, axis, 0, 0, axis_index_groups=groups)  30.8 us
    ppermute x5, waiting for transfers between devices, swap(): return lax.ppermute(array, axis, [(i, i ^ bit) for i in range(count)])  17.2 us
    ppermute x5, starting transfers between devices, swap(): return lax.ppermute(array, axis, [(i, i ^ bit) for i in range(count)])  11.4 us
    pallas_call x2, Pallas kernels, shards(): call(act_kernel, shape((GROUP, 2 * part, wide)), 1, 4)  3.12 us
    pallas_call x2, Pallas kernels, shards(): call(forward_kernel, shape((GROUP, 2 * part, wide)), 0, 3, flops, n_any=1)  2.95 us
  transfers between devices with their start and end apart: 11, of which 9 were waited for; matrix products, arithmetic and copies ran while one was open for 0% of the time, Pallas kernels for 7%

profile of v8, /device:TPU:8, one launch (start us, length us, event | category | flops | bytes accessed | tf_op | source)
XLA Modules:
  0.0 116.0 jit_solution(12905126346311162108)
XLA Ops:
  0.6 0.0 copy-start
  0.7 0.0 copy-start.2
  0.7 1.0 copy-done.2
  1.7 0.7 shard_map.67
  2.4 9.8 %all-to-all-start = ((bf16[16,16,384]{2,1,0:T(8,128)(2,1)}), bf16[16,16,384]{2,1,0:T(8,128)(2,1)S(1)}, u32[]{:S(2)}, u32[]{:S(2)}) async-start(bf16[16,16,384]{2,1,0:T(8,128)(2,1)} %shard_map.67), calls=%async_computation | async-start | bytes 393216 | tf_op jit(solution)/shard_map/all_to_all | solution.py:156
  12.3 0.0 copy-done
  12.3 0.0 copy-start.1
  12.3 1.1 copy-done.1
  13.3 0.1 shard_map.68
  13.4 8.5 %all-to-all-done.tokens_ref.far_ref = bf16[16,16,384]{2,1,0:T(8,128)(2,1)S(1)} async-done(((bf16[16,16,384]{2,1,0:T(8,128)(2,1)}), bf16[16,16,384]{2,1,0:T(8,128)(2,1)S(1)}, u32[]{:S(2)}, u32[]{:S(2)}) %all-to-all-start) | async-done | bytes 196640 | tf_op jit(solution)/shard_map/all_to_all | solution.py:156
  21.9 1.5 %shard_map.72 = bf16[8,32,1536]{2,1,0:T(8,128)(2,1)} custom-call(bf16[16,16,384]{2,1,0:T(8,128)(2,1)S(1)} %all-to-all-done.tokens_ref.far_ref, bf16[384,768]{1,0:T(8,128)(2,1)S(1)} %get-tuple-element.11.gate_ref, bf16[384,768]{1,0:T(8,128)(2,1)S(1)} %get-tuple-element.12.up_ref, s32[1]{0:T(128)} %bitcast._), custom_call_target="tpu_custom_call" | custom-call | flops 301989888 | tf_op jit(solution)/shard_map/pallas_call | solution.py:172
  23.3 0.0 copy-start.3
  23.3 3.7 %all-to-all-start.3 = ((bf16[8,32,1536]{2,1,0:T(8,128)(2,1)}), bf16[8,32,1536]{2,1,0:T(8,128)(2,1)S(1)}, u32[]{:S(2)}, u32[]{:S(2)}) async-start(bf16[8,32,1536]{2,1,0:T(8,128)(2,1)} %shard_map.72), calls=%async_computation.3 | async-start | bytes 1572864 | tf_op jit(solution)/shard_map/all_to_all | solution.py:156
  27.0 1.9 %collective-permute-start = (bf16[16,16,384]{2,1,0:T(8,128)(2,1)S(1)}, bf16[16,16,384]{2,1,0:T(8,128)(2,1)S(1)}, u32[]{:S(2)}, u32[]{:S(2)}) collective-permute-start(bf16[16,16,384]{2,1,0:T(8,128)(2,1)S(1)} %all-to-all-done.tokens_ref.far_ref), channel_id=1, source_target_pairs={{0,1},{1,0},{2,3},{3,2},{4,5},{5,4},{6,7},{7,6},{8,9},{9,8},{10,11... | collective-permute-start | bytes 589832 | tf_op jit(solution)/shard_map/ppermute | solution.py:159
  29.0 0.0 copy-done.3
  29.0 2.6 %collective-permute-start.1 = (bf16[32,768]{1,0:T(8,128)(2,1)S(1)}, bf16[32,768]{1,0:T(8,128)(2,1)S(1)}, u32[]{:S(2)}, u32[]{:S(2)}) collective-permute-start(bf16[32,768]{1,0:T(8,128)(2,1)S(1)} %copy-done.3), channel_id=1, source_target_pairs={{0,256},{32,288},{64,320},{96,352},{128,384},{160,416},{192,448},{... | collective-permute-start | bytes 147464 | tf_op jit(solution)/shard_map/ppermute | solution.py:159
  31.6 4.4 %collective-permute-done.1._.far_cot_ref = bf16[32,768]{1,0:T(8,128)(2,1)S(1)} collective-permute-done((bf16[32,768]{1,0:T(8,128)(2,1)S(1)}, bf16[32,768]{1,0:T(8,128)(2,1)S(1)}, u32[]{:S(2)}, u32[]{:S(2)}) %collective-permute-start.1) | collective-permute-done | bytes 49184 | tf_op jit(solution)/shard_map/ppermute | solution.py:159
  36.0 0.0 collective-permute-done.tokens_ref.near_ref
  36.0 1.5 %shard_map.69 = bf16[8,32,1536]{2,1,0:T(8,128)(2,1)} custom-call(bf16[16,16,384]{2,1,0:T(8,128)(2,1)S(1)} %collective-permute-done.tokens_ref.near_ref, bf16[384,768]{1,0:T(8,128)(2,1)S(1)} %get-tuple-element.11.gate_ref, bf16[384,768]{1,0:T(8,128)(2,1)S(1)} %get-tuple-element.12.up_ref, bf16[32,768]{1,0:T(8,128)(2,1)S(1)} %collective-permute-done.1._.far_cot_ref), custom_call_target="tpu_custom_call" | custom-call | flops 301989888 | tf_op jit(solution)/shard_map/pallas_call | solution.py:172
  37.5 1.2 %all-to-all-done.3.parts_ref = bf16[8,32,1536]{2,1,0:T(8,128)(2,1)S(1)} async-done(((bf16[8,32,1536]{2,1,0:T(8,128)(2,1)}), bf16[8,32,1536]{2,1,0:T(8,128)(2,1)S(1)}, u32[]{:S(2)}, u32[]{:S(2)}) %all-to-all-start.3) | async-done | bytes 786464 | tf_op jit(solution)/shard_map/all_to_all | solution.py:156
  38.7 5.8 %all-to-all-start.1 = ((bf16[8,32,1536]{2,1,0:T(8,128)(2,1)}), bf16[8,32,1536]{2,1,0:T(8,128)(2,1)S(1)}, u32[]{:S(2)}, u32[]{:S(2)}) async-start(bf16[8,32,1536]{2,1,0:T(8,128)(2,1)} %shard_map.69), calls=%async_computation.1 | async-start | bytes 1572864 | tf_op jit(solution)/shard_map/all_to_all | solution.py:156
  44.5 0.1 shard_map.73
  44.6 2.2 %collective-permute-start.3 = (bf16[32,1536]{1,0:T(8,128)(2,1)S(1)}, bf16[32,1536]{1,0:T(8,128)(2,1)S(1)}, u32[]{:S(2)}, u32[]{:S(2)}) collective-permute-start(bf16[32,1536]{1,0:T(8,128)(2,1)S(1)} %get-tuple-element.16), channel_id=1, source_target_pairs={{0,256},{32,288},{64,320},{96,352},{128,384},{160,416},{192,448},{... | collective-permute-start | bytes 294920 | tf_op jit(solution)/shard_map/ppermute | solution.py:159
  46.8 0.1 pad_add_fusion.1.where_ref
  46.9 6.9 %collective-permute-done.3.came_ref = bf16[32,1536]{1,0:T(8,128)(2,1)S(1)} collective-permute-done((bf16[32,1536]{1,0:T(8,128)(2,1)S(1)}, bf16[32,1536]{1,0:T(8,128)(2,1)S(1)}, u32[]{:S(2)}, u32[]{:S(2)}) %collective-permute-start.3) | collective-permute-done | bytes 98336 | tf_op jit(solution)/shard_map/ppermute | solution.py:159
  53.8 1.6 %shard_map.74 = bf16[8,32,1536]{2,1,0:T(8,128)(2,1)} custom-call(s32[2]{0:T(128)S(1)} %pad_add_fusion.1.where_ref, f32[32,1536]{1,0:T(8,128)S(1)} %get-tuple-element.15.keep_ref, bf16[32,1536]{1,0:T(8,128)(2,1)S(1)} %collective-permute-done.3.came_ref, bf16[32,768]{1,0:T(8,128)(2,1)S(1)} %copy-done.3, bf16[32,768]{1,0:T(8,128)(2,1)S(1)} %collective-permute-done.1._.far_cot_ref), custom_call_target="tpu_custom_call" | custom-call | tf_op jit(solution)/shard_map/pallas_call | solution.py:180
  55.4 2.0 %all-to-all-done.1.parts_ref = bf16[8,32,1536]{2,1,0:T(8,128)(2,1)S(1)} async-done(((bf16[8,32,1536]{2,1,0:T(8,128)(2,1)}), bf16[8,32,1536]{2,1,0:T(8,128)(2,1)S(1)}, u32[]{:S(2)}, u32[]{:S(2)}) %all-to-all-start.1) | async-done | bytes 786464 | tf_op jit(solution)/shard_map/all_to_all | solution.py:156
  57.4 5.1 %all-to-all-start.4 = ((bf16[8,32,1536]{2,1,0:T(8,128)(2,1)}), bf16[8,32,1536]{2,1,0:T(8,128)(2,1)S(1)}, u32[]{:S(2)}, u32[]{:S(2)}) async-start(bf16[8,32,1536]{2,1,0:T(8,128)(2,1)} %shard_map.74), calls=%async_computation.4 | async-start | bytes 1572864 | tf_op jit(solution)/shard_map/all_to_all | solution.py:156
  62.5 0.1 shard_map.70
  62.6 2.7 %collective-permute-start.2 = (bf16[32,1536]{1,0:T(8,128)(2,1)S(1)}, bf16[32,1536]{1,0:T(8,128)(2,1)S(1)}, u32[]{:S(2)}, u32[]{:S(2)}) collective-permute-start(bf16[32,1536]{1,0:T(8,128)(2,1)S(1)} %get-tuple-element.14), channel_id=1, source_target_pairs={{0,256},{32,288},{64,320},{96,352},{128,384},{160,416},{192,448},{... | collective-permute-start | bytes 294920 | tf_op jit(solution)/shard_map/ppermute | solution.py:159
  65.3 0.1 pad_add_fusion.where_ref
  65.4 5.9 %collective-permute-done.2.came_ref = bf16[32,1536]{1,0:T(8,128)(2,1)S(1)} collective-permute-done((bf16[32,1536]{1,0:T(8,128)(2,1)S(1)}, bf16[32,1536]{1,0:T(8,128)(2,1)S(1)}, u32[]{:S(2)}, u32[]{:S(2)}) %collective-permute-start.2) | collective-permute-done | bytes 98336 | tf_op jit(solution)/shard_map/ppermute | solution.py:159
  71.3 1.5 %shard_map.71 = bf16[8,32,1536]{2,1,0:T(8,128)(2,1)} custom-call(s32[2]{0:T(128)S(1)} %pad_add_fusion.where_ref, f32[32,1536]{1,0:T(8,128)S(1)} %get-tuple-element.13.keep_ref, bf16[32,1536]{1,0:T(8,128)(2,1)S(1)} %collective-permute-done.2.came_ref, bf16[32,768]{1,0:T(8,128)(2,1)S(1)} %copy-done.3, bf16[32,768]{1,0:T(8,128)(2,1)S(1)} %collective-permute-done.1._.far_cot_ref), custom_call_target="tpu_custom_call" | custom-call | tf_op jit(solution)/shard_map/pallas_call | solution.py:180
  72.8 2.0 %all-to-all-done.4.d_ref.d_far_ref = bf16[8,32,1536]{2,1,0:T(8,128)(2,1)S(1)} async-done(((bf16[8,32,1536]{2,1,0:T(8,128)(2,1)}), bf16[8,32,1536]{2,1,0:T(8,128)(2,1)S(1)}, u32[]{:S(2)}, u32[]{:S(2)}) %all-to-all-start.4) | async-done | bytes 786464 | tf_op jit(solution)/shard_map/all_to_all | solution.py:156
  74.8 4.1 %all-to-all-start.2 = ((bf16[8,32,1536]{2,1,0:T(8,128)(2,1)}), bf16[8,32,1536]{2,1,0:T(8,128)(2,1)S(1)}, u32[]{:S(2)}, u32[]{:S(2)}) async-start(bf16[8,32,1536]{2,1,0:T(8,128)(2,1)} %shard_map.71), calls=%async_computation.2 | async-start | bytes 1572864 | tf_op jit(solution)/shard_map/all_to_all | solution.py:156
  78.9 1.3 %shard_map.75 = bf16[256,384]{1,0:T(8,128)(2,1)} custom-call(bf16[8,32,1536]{2,1,0:T(8,128)(2,1)S(1)} %all-to-all-done.4.d_ref.d_far_ref, bf16[384,768]{1,0:T(8,128)(2,1)S(1)} %get-tuple-element.11.gate_ref, bf16[384,768]{1,0:T(8,128)(2,1)S(1)} %get-tuple-element.12.up_ref), custom_call_target="tpu_custom_call" | custom-call | flops 301989888 | tf_op jit(solution)/shard_map/pallas_call | solution.py:185
  80.1 1.9 %collective-permute-start.4 = (bf16[256,384]{1,0:T(8,128)(2,1)}, bf16[256,384]{1,0:T(8,128)(2,1)S(1)}, u32[]{:S(2)}, u32[]{:S(2)}) collective-permute-start(bf16[256,384]{1,0:T(8,128)(2,1)} %shard_map.75), channel_id=1, source_target_pairs={{0,1},{1,0},{2,3},{3,2},{4,5},{5,4},{6,7},{7,6},{8,9},{9,8},{10,11... | collective-permute-start | bytes 589832 | tf_op jit(solution)/shard_map/ppermute | solution.py:159
  82.0 6.3 %all-to-all-done.2.d_ref.d_near_ref = bf16[8,32,1536]{2,1,0:T(8,128)(2,1)S(1)} async-done(((bf16[8,32,1536]{2,1,0:T(8,128)(2,1)}), bf16[8,32,1536]{2,1,0:T(8,128)(2,1)S(1)}, u32[]{:S(2)}, u32[]{:S(2)}) %all-to-all-start.2) | async-done | bytes 786464 | tf_op jit(solution)/shard_map/all_to_all | solution.py:156
  88.3 0.0 collective-permute-done.4.came_ref
  88.3 1.3 %shard_map.76 = bf16[16,16,384]{2,1,0:T(8,128)(2,1)} custom-call(bf16[8,32,1536]{2,1,0:T(8,128)(2,1)S(1)} %all-to-all-done.2.d_ref.d_near_ref, bf16[384,768]{1,0:T(8,128)(2,1)S(1)} %get-tuple-element.11.gate_ref, bf16[384,768]{1,0:T(8,128)(2,1)S(1)} %get-tuple-element.12.up_ref, bf16[256,384]{1,0:T(8,128)(2,1)S(1)} %collective-permute-done.4.came_ref), custom_call_target="tpu_custom_call" | custom-call | flops 301989888 | tf_op jit(solution)/shard_map/pallas_call | solution.py:189
  89.6 13.3 %all-to-all-start.5 = ((bf16[16,16,384]{2,1,0:T(8,128)(2,1)}), bf16[16,16,384]{2,1,0:T(8,128)(2,1)S(1)}, u32[]{:S(2)}, u32[]{:S(2)}) async-start(bf16[16,16,384]{2,1,0:T(8,128)(2,1)} %shard_map.76), calls=%async_computation.5 | async-start | bytes 393216 | tf_op jit(solution)/shard_map/all_to_all | solution.py:156
  102.9 1.6 %shard_map.77 = (bf16[384,768]{1,0:T(8,128)(2,1)}, bf16[384,768]{1,0:T(8,128)(2,1)}) custom-call(bf16[16,16,384]{2,1,0:T(8,128)(2,1)S(1)} %all-to-all-done.tokens_ref.far_ref, bf16[16,16,384]{2,1,0:T(8,128)(2,1)S(1)} %collective-permute-done.tokens_ref.near_ref, bf16[8,32,1536]{2,1,0:T(8,128)(2,1)S(1)} %all-to-all-done.4.d_ref.d_far_ref, ...), custom_call_target="tpu_custom_call" | custom-call | flops 603979776 | tf_op jit(solution)/shard_map/pallas_call | solution.py:195
  104.6 10.8 %all-to-all-done.5 = bf16[16,16,384]{2,1,0:T(8,128)(2,1)S(1)} async-done(((bf16[16,16,384]{2,1,0:T(8,128)(2,1)}), bf16[16,16,384]{2,1,0:T(8,128)(2,1)S(1)}, u32[]{:S(2)}, u32[]{:S(2)}) %all-to-all-start.5) | async-done | bytes 196640 | tf_op jit(solution)/shard_map/all_to_all | solution.py:156
  115.4 0.6 reduce_sum.12
Async XLA Ops:
  0.6 11.6 %copy-start = (bf16[384,768]{1,0:T(8,128)(2,1)S(1)}, bf16[384,768]{1,0:T(8,128)(2,1)}, u32[]{:S(2)}) copy-start(bf16[384,768]{1,0:T(8,128)(2,1)} %gate_ref.1) | copy-start | bytes 1769476
  0.7 1.1 copy-start.2
  2.4 19.5 %all-to-all-start = ((bf16[16,16,384]{2,1,0:T(8,128)(2,1)}), bf16[16,16,384]{2,1,0:T(8,128)(2,1)S(1)}, u32[]{:S(2)}, u32[]{:S(2)}) async-start(bf16[16,16,384]{2,1,0:T(8,128)(2,1)} %shard_map.67), calls=%async_computation | async-start | bytes 393216 | tf_op jit(solution)/shard_map/all_to_all | solution.py:156
  12.3 1.1 copy-start.1
  23.3 5.6 %copy-start.3 = (bf16[32,768]{1,0:T(8,128)(2,1)S(1)}, bf16[32,768]{1,0:T(8,128)(2,1)}, u32[]{:S(2)}) copy-start(bf16[32,768]{1,0:T(8,128)(2,1)} %cot_ref.3) | copy-start | bytes 147460
  23.3 15.4 %all-to-all-start.3 = ((bf16[8,32,1536]{2,1,0:T(8,128)(2,1)}), bf16[8,32,1536]{2,1,0:T(8,128)(2,1)S(1)}, u32[]{:S(2)}, u32[]{:S(2)}) async-start(bf16[8,32,1536]{2,1,0:T(8,128)(2,1)} %shard_map.72), calls=%async_computation.3 | async-start | bytes 1572864 | tf_op jit(solution)/shard_map/all_to_all | solution.py:156
  27.0 9.0 %collective-permute-start = (bf16[16,16,384]{2,1,0:T(8,128)(2,1)S(1)}, bf16[16,16,384]{2,1,0:T(8,128)(2,1)S(1)}, u32[]{:S(2)}, u32[]{:S(2)}) collective-permute-start(bf16[16,16,384]{2,1,0:T(8,128)(2,1)S(1)} %all-to-all-done.tokens_ref.far_ref), channel_id=1, source_target_pairs={{0,1},{1,0},{2,3},{3,2},{4,5},{5,4},{6,7},{7,6},{8,9},{9,8},{10,11... | collective-permute-start | bytes 589832 | tf_op jit(solution)/shard_map/ppermute | solution.py:159
  29.0 7.0 %collective-permute-start.1 = (bf16[32,768]{1,0:T(8,128)(2,1)S(1)}, bf16[32,768]{1,0:T(8,128)(2,1)S(1)}, u32[]{:S(2)}, u32[]{:S(2)}) collective-permute-start(bf16[32,768]{1,0:T(8,128)(2,1)S(1)} %copy-done.3), channel_id=1, source_target_pairs={{0,256},{32,288},{64,320},{96,352},{128,384},{160,416},{192,448},{... | collective-permute-start | bytes 147464 | tf_op jit(solution)/shard_map/ppermute | solution.py:159
  38.7 18.7 %all-to-all-start.1 = ((bf16[8,32,1536]{2,1,0:T(8,128)(2,1)}), bf16[8,32,1536]{2,1,0:T(8,128)(2,1)S(1)}, u32[]{:S(2)}, u32[]{:S(2)}) async-start(bf16[8,32,1536]{2,1,0:T(8,128)(2,1)} %shard_map.69), calls=%async_computation.1 | async-start | bytes 1572864 | tf_op jit(solution)/shard_map/all_to_all | solution.py:156
  44.6 9.2 %collective-permute-start.3 = (bf16[32,1536]{1,0:T(8,128)(2,1)S(1)}, bf16[32,1536]{1,0:T(8,128)(2,1)S(1)}, u32[]{:S(2)}, u32[]{:S(2)}) collective-permute-start(bf16[32,1536]{1,0:T(8,128)(2,1)S(1)} %get-tuple-element.16), channel_id=1, source_target_pairs={{0,256},{32,288},{64,320},{96,352},{128,384},{160,416},{192,448},{... | collective-permute-start | bytes 294920 | tf_op jit(solution)/shard_map/ppermute | solution.py:159
  57.4 17.4 %all-to-all-start.4 = ((bf16[8,32,1536]{2,1,0:T(8,128)(2,1)}), bf16[8,32,1536]{2,1,0:T(8,128)(2,1)S(1)}, u32[]{:S(2)}, u32[]{:S(2)}) async-start(bf16[8,32,1536]{2,1,0:T(8,128)(2,1)} %shard_map.74), calls=%async_computation.4 | async-start | bytes 1572864 | tf_op jit(solution)/shard_map/all_to_all | solution.py:156
  62.6 8.7 %collective-permute-start.2 = (bf16[32,1536]{1,0:T(8,128)(2,1)S(1)}, bf16[32,1536]{1,0:T(8,128)(2,1)S(1)}, u32[]{:S(2)}, u32[]{:S(2)}) collective-permute-start(bf16[32,1536]{1,0:T(8,128)(2,1)S(1)} %get-tuple-element.14), channel_id=1, source_target_pairs={{0,256},{32,288},{64,320},{96,352},{128,384},{160,416},{192,448},{... | collective-permute-start | bytes 294920 | tf_op jit(solution)/shard_map/ppermute | solution.py:159
  74.8 13.5 %all-to-all-start.2 = ((bf16[8,32,1536]{2,1,0:T(8,128)(2,1)}), bf16[8,32,1536]{2,1,0:T(8,128)(2,1)S(1)}, u32[]{:S(2)}, u32[]{:S(2)}) async-start(bf16[8,32,1536]{2,1,0:T(8,128)(2,1)} %shard_map.71), calls=%async_computation.2 | async-start | bytes 1572864 | tf_op jit(solution)/shard_map/all_to_all | solution.py:156
  80.1 8.2 %collective-permute-start.4 = (bf16[256,384]{1,0:T(8,128)(2,1)}, bf16[256,384]{1,0:T(8,128)(2,1)S(1)}, u32[]{:S(2)}, u32[]{:S(2)}) collective-permute-start(bf16[256,384]{1,0:T(8,128)(2,1)} %shard_map.75), channel_id=1, source_target_pairs={{0,1},{1,0},{2,3},{3,2},{4,5},{5,4},{6,7},{7,6},{8,9},{9,8},{10,11... | collective-permute-start | bytes 589832 | tf_op jit(solution)/shard_map/ppermute | solution.py:159
  89.6 25.8 %all-to-all-start.5 = ((bf16[16,16,384]{2,1,0:T(8,128)(2,1)}), bf16[16,16,384]{2,1,0:T(8,128)(2,1)S(1)}, u32[]{:S(2)}, u32[]{:S(2)}) async-start(bf16[16,16,384]{2,1,0:T(8,128)(2,1)} %shard_map.76), calls=%async_computation.5 | async-start | bytes 393216 | tf_op jit(solution)/shard_map/all_to_all | solution.py:156
